TPU v7x, 32 devices: a whole 2x2x4 slice. The times are simulated.
32 devices in a mesh: dp: 2 (over y), seq: 16 (over z, x, core).
Axes of the slice: x: 2, y: 2, z: 4, core: 2. Of those that a mesh axis runs over, the one named last changes fastest.
Arguments:
- tokens: bfloat16 [2, 4096, 768], P('dp', 'seq'), may hold values from -6 to 6
- qkv_weight: bfloat16 [1769472], P(('dp', 'seq')), may hold values from -0.21875 to 0.21875
- out_weight: bfloat16 [589824], P(('dp', 'seq')), may hold values from -0.875 to 0.875
- expand_weight: bfloat16 [2359296], P(('dp', 'seq')), may hold values from -0.21875 to 0.21875
- contract_weight: bfloat16 [2359296], P(('dp', 'seq')), may hold values from -0.109375 to 0.109375
- bias_vectors: bfloat16 [4608], P(('dp', 'seq')), may hold values from -3 to 3
- gain_vectors: bfloat16 [1536], P(('dp', 'seq')), may hold values from 0.5 to 1.5
- ffn_bias: bfloat16 [3072], P(('dp', 'seq')), may hold values from -3 to 3
- random_blocks: int32 [2, 12, 64, 3], P('dp', None, 'seq'), may hold values from 0 to 63, as said below
- cotangent: bfloat16 [2, 4096, 768], P('dp', 'seq'), may hold values from -6 to 6
Outputs:
- output: float32 [2, 4096, 768], P('dp', 'seq')
- grad_tokens: float32 [2, 4096, 768], P('dp', 'seq')
- grad_qkv: float32 [1769472], P(('dp', 'seq'))
- grad_out: float32 [589824], P(('dp', 'seq'))
- grad_expand: float32 [2359296], P(('dp', 'seq'))
- grad_contract: float32 [2359296], P(('dp', 'seq'))
- grad_biases: float32 [4608], P(('dp', 'seq'))
- grad_gains: float32 [1536], P(('dp', 'seq'))
- grad_ffn_bias: float32 [3072], P(('dp', 'seq'))
Inputs may be any that keep to these rules, and one draw needn't show every extreme that they name: `random_blocks`: over the 1 sequence of one index of dp, all 12 heads and the three picks, the (head, query block, pick) entries of the query blocks held by one seq device, counted with repeats, name blocks held by any single seq device at most 9 times (each device holds 4 consecutive blocks of every sequence), and exactly 9 for some device.
All inputs are finite; a program needn't handle non-finite values.
Results may differ from a plain program's by a relative error of at most 0.014.
Values may be sent and summed in bfloat16 or wider, within the bound.
A program may use at most 192 MiB of HBM per device.

v0:
```python
import jax
import jax.numpy as jnp
from jax import lax
from jax.sharding import PartitionSpec as P

D = 768
FF = 3072
H = 12
HD = 64
BLOCK = 64
TOK_SEQ = 256
SEQ_GRP = 1
BPD = 4


norm_eps = 1e-12
masked_score = -1e30


def with_halo(cells, sides, width):
    for axis, dim in sides:
        count = lax.axis_size(axis)
        ends = count - 1
        head = lax.slice_in_dim(cells, 0, width, axis=dim)
        tail = lax.slice_in_dim(cells, cells.shape[dim] - width, cells.shape[dim], axis=dim)
        cells = jnp.concatenate(
            [
                lax.ppermute(tail, axis, [(i, (i + 1) % count) for i in range(ends)]),
                cells,
                lax.ppermute(head, axis, [((i + 1) % count, i) for i in range(ends)]),
            ],
            axis=dim,
        )
    return cells


def spread(block, axis, source):
    block = jnp.where(lax.axis_index(axis) == source, block, jnp.zeros_like(block))
    return lax.psum(block, axis)


def matmul(left, right):
    return jnp.dot(left, right, preferred_element_type=jnp.float32)


def inner_rows(left, right):
    return lax.dot_general(
        left, right, (((0,), (0,)), ((), ())), preferred_element_type=jnp.float32
    )


def outer_cols(left, right):
    return lax.dot_general(
        left, right, (((1,), (1,)), ((), ())), preferred_element_type=jnp.float32
    )


def gelu_tanh(value):
    return jax.nn.gelu(value, approximate=True)


def normalize(value, gain, shift):
    mean = jnp.mean(value, axis=-1, keepdims=True)
    centred = value - mean
    inverse = lax.rsqrt(jnp.mean(centred * centred, axis=-1, keepdims=True) + norm_eps)
    normed = centred * inverse
    return (normed * gain + shift, normed, inverse)


def normalize_back(grad, normed, inverse, gain):
    scaled = grad * gain
    centred = scaled - jnp.mean(scaled, axis=-1, keepdims=True)
    return inverse * (centred - normed * jnp.mean(scaled * normed, axis=-1, keepdims=True))


def gather_weights(
    qkv_weight, out_weight, expand_weight, contract_weight, bias_vectors, gain_vectors, ffn_bias
):
    whole = (
        lax.all_gather(qkv_weight, ("dp", "seq"), axis=0, tiled=True),
        lax.all_gather(out_weight, ("dp", "seq"), axis=0, tiled=True),
        lax.all_gather(expand_weight, ("dp", "seq"), axis=0, tiled=True),
        lax.all_gather(contract_weight, ("dp", "seq"), axis=0, tiled=True),
        lax.all_gather(bias_vectors, ("dp", "seq"), axis=0, tiled=True),
        lax.all_gather(gain_vectors, ("dp", "seq"), axis=0, tiled=True),
        lax.all_gather(ffn_bias, ("dp", "seq"), axis=0, tiled=True),
    )
    return (
        whole[0].reshape(3, D, D),
        whole[1].reshape(D, D),
        whole[2].reshape(D, FF),
        whole[3].reshape(FF, D),
        whole[4].astype(jnp.float32).reshape(6, D),
        whole[5].astype(jnp.float32).reshape(2, D),
        whole[6].astype(jnp.float32),
    )


def to_heads(rows):
    return rows.reshape(SEQ_GRP, BPD, BLOCK, H, HD).transpose(0, 1, 3, 2, 4)


def from_heads(heads):
    return heads.transpose(0, 1, 3, 2, 4).reshape(SEQ_GRP * TOK_SEQ, D)


def key_blocks(pair, picks):
    shards = lax.axis_size("seq")
    place = lax.axis_index("seq")
    nblocks = BPD * shards
    rims = with_halo(pair, (("seq", 2),), BLOCK)
    wide = rims.reshape(2, SEQ_GRP, BPD + 2, BLOCK, D)
    window = jnp.stack(
        [wide[:, :, 0:BPD], wide[:, :, 1 : BPD + 1], wide[:, :, 2 : BPD + 2]], axis=3
    )
    window = window.reshape(2, SEQ_GRP, BPD, 3, BLOCK, H, HD).transpose(0, 1, 2, 5, 3, 4, 6)
    first = spread(pair[:, :, :BLOCK], "seq", 0)
    last = spread(pair[:, :, TOK_SEQ - BLOCK :], "seq", shards - 1)
    ends = (
        jnp.stack([first, last], axis=2)
        .reshape(2, SEQ_GRP, 2, BLOCK, H, HD)
        .transpose(0, 1, 4, 2, 3, 5)
    )
    ends = jnp.broadcast_to(ends[:, :, None], (2, SEQ_GRP, BPD, H, 2, BLOCK, HD))
    count = SEQ_GRP * H * BPD * 3
    cap = (count + shards - 1) // shards
    flat = picks.reshape(count)
    holder = flat // BPD
    within = flat % BPD
    order = jnp.arange(count, dtype=jnp.int32)
    seq_of = order // (H * BPD * 3)
    head_of = order // (BPD * 3) % H
    tile_id = (seq_of * BPD + within) * H + head_of
    owners = (holder[:, None] == jnp.arange(shards, dtype=jnp.int32)[None, :]).astype(jnp.int32)
    rank = jnp.sum((jnp.cumsum(owners, axis=0) - owners) * owners, axis=1)
    slot = holder * cap + rank
    asked = jnp.zeros((shards * cap,), jnp.int32).at[slot].set(tile_id).reshape(shards, cap)
    tiles = (
        pair.reshape(2, SEQ_GRP, BPD, BLOCK, H, HD)
        .transpose(1, 2, 4, 0, 3, 5)
        .reshape(SEQ_GRP * BPD * H, 2, BLOCK * HD)
    )
    wanted = lax.all_to_all(asked, "seq", split_axis=0, concat_axis=0, tiled=True)
    picked = tiles[wanted]
    returned = lax.all_to_all(picked, "seq", split_axis=0, concat_axis=0, tiled=True)
    mine = returned.reshape(shards * cap, 2, BLOCK * HD)[slot]
    mine = mine.reshape(SEQ_GRP, H, BPD, 3, 2, BLOCK, HD).transpose(4, 0, 2, 1, 3, 5, 6)
    listing = jnp.concatenate([window, ends, mine], axis=4).reshape(
        2, SEQ_GRP, BPD, H, 8 * BLOCK, HD
    )
    position = place * BPD + jnp.arange(BPD, dtype=jnp.int32)
    always = jnp.ones((BPD,), dtype=bool)
    valid = jnp.stack(
        [position >= 1, always, position + 1 < nblocks, always, always, always, always, always],
        axis=1,
    )
    valid = jnp.broadcast_to(valid[:, :, None], (BPD, 8, BLOCK)).reshape(BPD, 8 * BLOCK)
    return (listing, valid, slot, wanted, cap)


def score(query, keys, valid):
    scores = jnp.einsum(
        "sbhqd,sbhkd->sbhqk", query, keys, preferred_element_type=jnp.float32
    ) * HD ** (-0.5)
    return jnp.where(valid[None, :, None, None, :], scores, masked_score)


def attend(query, listing, valid):
    scores = score(query, listing[0], valid)
    top = jnp.max(scores, axis=-1, keepdims=True)
    weights = jnp.exp(scores - top)
    total = jnp.sum(weights, axis=-1, keepdims=True)
    probs = (weights / total).astype(jnp.bfloat16)
    attended = jnp.einsum(
        "sbhqk,sbhkd->sbhqd", probs, listing[1], preferred_element_type=jnp.float32
    )
    return (attended, top + jnp.log(total))


def attend_back(query, listing, valid, lse, grad_out):
    probs = jnp.exp(score(query, listing[0], valid) - lse)
    d_probs = jnp.einsum(
        "sbhqd,sbhkd->sbhqk", grad_out, listing[1], preferred_element_type=jnp.float32
    )
    d_values = jnp.einsum(
        "sbhqk,sbhqd->sbhkd",
        probs.astype(jnp.bfloat16),
        grad_out,
        preferred_element_type=jnp.float32,
    )
    d_scores = (probs * (d_probs - jnp.sum(probs * d_probs, axis=-1, keepdims=True))).astype(
        jnp.bfloat16
    )
    d_query = jnp.einsum(
        "sbhqk,sbhkd->sbhqd", d_scores, listing[0], preferred_element_type=jnp.float32
    ) * HD ** (-0.5)
    d_keys = jnp.einsum(
        "sbhqk,sbhqd->sbhkd", d_scores, query, preferred_element_type=jnp.float32
    ) * HD ** (-0.5)
    return (d_query, jnp.stack([d_keys, d_values]))


def return_grads(grads, slot, served, cap):
    shards = lax.axis_size("seq")
    place = lax.axis_index("seq")
    count = SEQ_GRP * H * BPD * 3
    parts = grads.reshape(2, SEQ_GRP, BPD, H, 8, BLOCK, HD)
    window = (
        parts[:, :, :, :, 0:3].transpose(0, 1, 2, 4, 5, 3, 6).reshape(2, SEQ_GRP, BPD, 3, BLOCK, D)
    )
    wide = sum(
        (
            jnp.pad(window[:, :, :, w], ((0, 0), (0, 0), (w, 2 - w), (0, 0), (0, 0)))
            for w in range(3)
        )
    )
    edges = jnp.concatenate([wide[:, :, 0], wide[:, :, BPD + 1]], axis=2)
    arrived = with_halo(edges.astype(jnp.bfloat16), (("seq", 2),), BLOCK).astype(edges.dtype)
    local = wide[:, :, 1 : BPD + 1].reshape(2, SEQ_GRP, TOK_SEQ, D)
    local = local.at[:, :, :BLOCK].add(arrived[:, :, :BLOCK])
    local = local.at[:, :, TOK_SEQ - BLOCK :].add(arrived[:, :, 3 * BLOCK :])
    ends = (
        jnp.sum(parts[:, :, :, :, 3:5], axis=2)
        .transpose(0, 1, 3, 4, 2, 5)
        .reshape(2, SEQ_GRP, 2, BLOCK, D)
    )
    ends = lax.psum(ends.astype(jnp.bfloat16), "seq").astype(jnp.float32)
    local = local.at[:, :, :BLOCK].add(jnp.where(place == 0, ends[:, :, 0], 0.0))
    local = local.at[:, :, TOK_SEQ - BLOCK :].add(
        jnp.where(place == shards - 1, ends[:, :, 1], 0.0)
    )
    picked = parts[:, :, :, :, 5:8].transpose(1, 3, 2, 4, 0, 5, 6).reshape(count, 2, BLOCK * HD)
    outbox = jnp.zeros((shards * cap, 2, BLOCK * HD), jnp.float32).at[slot].set(picked)
    inbox = lax.all_to_all(
        outbox.reshape(shards, cap, 2, BLOCK * HD).astype(jnp.bfloat16),
        "seq",
        split_axis=0,
        concat_axis=0,
        tiled=True,
    ).astype(jnp.float32)
    table = jnp.zeros((SEQ_GRP * BPD * H, 2, BLOCK * HD), jnp.float32)
    table = table.at[served.reshape(shards * cap)].add(inbox.reshape(shards * cap, 2, BLOCK * HD))
    table = (
        table.reshape(SEQ_GRP, BPD, H, 2, BLOCK, HD)
        .transpose(3, 0, 1, 4, 2, 5)
        .reshape(2, SEQ_GRP, TOK_SEQ, D)
    )
    return local + table


def layer_forward(tokens, picks, weights):
    qkv, out_w, expand, contract, biases, gains, ffn_bias = weights
    rows = tokens.reshape(SEQ_GRP * TOK_SEQ, D)
    projected = jnp.einsum("rd,edf->erf", rows, qkv, preferred_element_type=jnp.float32)
    query = (projected[0] + biases[0]).astype(jnp.bfloat16)
    pair = (
        jnp.stack([projected[1], projected[2] + biases[1]])
        .astype(jnp.bfloat16)
        .reshape(2, SEQ_GRP, TOK_SEQ, D)
    )
    listing, valid, slot, served, cap = key_blocks(pair, picks)
    query_heads = to_heads(query)
    attended, lse = attend(query_heads, listing, valid)
    mixed = from_heads(attended.astype(jnp.bfloat16))
    hidden1 = rows.astype(jnp.float32) + matmul(mixed, out_w) + biases[2]
    normed_out1, normed1, inverse1 = normalize(hidden1, gains[0], biases[3])
    lowered = normed_out1.astype(jnp.bfloat16)
    up = matmul(lowered, expand) + ffn_bias
    active = gelu_tanh(up).astype(jnp.bfloat16)
    hidden2 = normed_out1 + matmul(active, contract) + biases[4]
    result, normed2, inverse2 = normalize(hidden2, gains[1], biases[5])
    saved = (
        query_heads,
        listing,
        valid,
        lse,
        mixed,
        normed1,
        inverse1,
        lowered,
        up,
        active,
        normed2,
        inverse2,
        slot,
        served,
        cap,
    )
    return (result, saved)


def layer_backward(tokens, cotangent, weights, saved):
    qkv, out_w, expand, contract, biases, gains, ffn_bias = weights
    (
        query_heads,
        listing,
        valid,
        lse,
        mixed,
        normed1,
        inverse1,
        lowered,
        up,
        active,
        normed2,
        inverse2,
        slot,
        served,
        cap,
    ) = saved
    rows = tokens.reshape(SEQ_GRP * TOK_SEQ, D)
    grad = cotangent.reshape(SEQ_GRP * TOK_SEQ, D).astype(jnp.float32)
    d_gain2 = jnp.sum(grad * normed2, axis=0)
    d_shift2 = jnp.sum(grad, axis=0)
    d_sum2 = normalize_back(grad, normed2, inverse2, gains[1])
    d_down = d_sum2.astype(jnp.bfloat16)
    d_bias2 = jnp.sum(d_down.astype(jnp.float32), axis=0)
    d_contract = inner_rows(active, d_down)
    d_active = outer_cols(d_down, contract)
    gelu_value, gelu_pull = jax.vjp(gelu_tanh, up)
    d_up = gelu_pull(d_active)[0].astype(jnp.bfloat16)
    d_ffn_bias = jnp.sum(d_up.astype(jnp.float32), axis=0)
    d_expand = inner_rows(lowered, d_up)
    d_norm1 = d_sum2 + outer_cols(d_up, expand)
    d_gain1 = jnp.sum(d_norm1 * normed1, axis=0)
    d_shift1 = jnp.sum(d_norm1, axis=0)
    d_sum1 = normalize_back(d_norm1, normed1, inverse1, gains[0])
    d_attn = d_sum1.astype(jnp.bfloat16)
    d_bias_out = jnp.sum(d_attn.astype(jnp.float32), axis=0)
    d_out_w = inner_rows(mixed, d_attn)
    d_mixed = outer_cols(d_attn, out_w).astype(jnp.bfloat16)
    d_query_heads, d_list = attend_back(query_heads, listing, valid, lse, to_heads(d_mixed))
    d_pair = (
        return_grads(d_list, slot, served, cap)
        .astype(jnp.bfloat16)
        .reshape(2, SEQ_GRP * TOK_SEQ, D)
    )
    d_query = from_heads(d_query_heads).astype(jnp.bfloat16)
    d_proj = jnp.concatenate([d_query[None], d_pair], axis=0)
    d_qkv = jnp.einsum("rd,erf->edf", rows, d_proj, preferred_element_type=jnp.float32)
    d_tokens = d_sum1 + jnp.einsum("erf,edf->rd", d_proj, qkv, preferred_element_type=jnp.float32)
    d_bias_q = jnp.sum(d_query.astype(jnp.float32), axis=0)
    d_bias_v = jnp.sum(d_pair[1].astype(jnp.float32), axis=0)
    d_biases = jnp.stack([d_bias_q, d_bias_v, d_bias_out, d_shift1, d_bias2, d_shift2]).reshape(
        6 * D
    )
    d_gains = jnp.stack([d_gain1, d_gain2]).reshape(2 * D)
    shares = (
        lax.psum_scatter(d_qkv.reshape(3 * D * D), ("dp", "seq"), scatter_dimension=0, tiled=True),
        lax.psum_scatter(d_out_w.reshape(D * D), ("dp", "seq"), scatter_dimension=0, tiled=True),
        lax.psum_scatter(d_expand.reshape(D * FF), ("dp", "seq"), scatter_dimension=0, tiled=True),
        lax.psum_scatter(
            d_contract.reshape(FF * D), ("dp", "seq"), scatter_dimension=0, tiled=True
        ),
        lax.psum_scatter(d_biases, ("dp", "seq"), scatter_dimension=0, tiled=True),
        lax.psum_scatter(d_gains, ("dp", "seq"), scatter_dimension=0, tiled=True),
        lax.psum_scatter(d_ffn_bias, ("dp", "seq"), scatter_dimension=0, tiled=True),
    )
    return (d_tokens, shares)


def on_device(
    tokens,
    qkv_weight,
    out_weight,
    expand_weight,
    contract_weight,
    bias_vectors,
    gain_vectors,
    ffn_bias,
    random_blocks,
    cotangent,
):
    weights = gather_weights(
        qkv_weight, out_weight, expand_weight, contract_weight, bias_vectors, gain_vectors, ffn_bias
    )
    result, saved = layer_forward(tokens, random_blocks, weights)
    weights = gather_weights(
        qkv_weight, out_weight, expand_weight, contract_weight, bias_vectors, gain_vectors, ffn_bias
    )
    unused, saved = layer_forward(tokens, random_blocks, weights)
    d_tokens, shares = layer_backward(tokens, cotangent, weights, saved)
    return (
        result.reshape(SEQ_GRP, TOK_SEQ, D),
        d_tokens.reshape(SEQ_GRP, TOK_SEQ, D),
        shares[0],
        shares[1],
        shares[2],
        shares[3],
        shares[4],
        shares[5],
        shares[6],
    )


def solution(mesh):
    return jax.shard_map(
        on_device,
        mesh=mesh,
        in_specs=(
            P("dp", "seq", None),
            P(("dp", "seq")),
            P(("dp", "seq")),
            P(("dp", "seq")),
            P(("dp", "seq")),
            P(("dp", "seq")),
            P(("dp", "seq")),
            P(("dp", "seq")),
            P("dp", None, "seq", None),
            P("dp", "seq", None),
        ),
        out_specs=(
            P("dp", "seq", None),
            P("dp", "seq", None),
            P(("dp", "seq")),
            P(("dp", "seq")),
            P(("dp", "seq")),
            P(("dp", "seq")),
            P(("dp", "seq")),
            P(("dp", "seq")),
            P(("dp", "seq")),
        ),
        check_vma=False,
    )
```

profile of v0, /device:TPU:8, one launch (start us, length us, event | category | flops | bytes accessed | tf_op | source)
XLA Modules:
  0.0 1241.5 jit_solution(2309093241407086661)
XLA Ops:
  11.3 41.2 %all-reduce.16 = (bf16[4608]{0:T(1024)(128)(2,1)S(1)}, bf16[1536]{0:T(1024)(128)(2,1)}, bf16[3072]{0:T(1024)(128)(2,1)}) all-reduce(bf16[4608]{0:T(1024)(128)(2,1)S(1)} %dynamic-update-slice.12, bf16[1536]{0:T(1024)(128)(2,1)S(1)} %dynamic-update-slice.13, ...), channel_id=1, replica_groups=mesh['dp'=2,'seq'=16] {'dp','seq'}, use_global_device_ids=true, to_apply=%add.4 | all-reduce | flops 9216 | bytes 36864
  53.1 18.6 %all-gather.5.cloned.1.call-done = bf16[1769472]{0:T(1024)(128)(2,1)} async-done(((bf16[55296]{0:T(1024)(128)(2,1)}), bf16[1769472]{0:T(1024)(128)(2,1)}) %all-gather.5.cloned.1.call-update) | async-done | bytes 3538960 | tf_op jit(solution)/shard_map/all_gather | solution.py:80
  89.2 10.3 all_to_all.24
  106.1 10.8 gather_fusion
  148.2 10.8 collective-permute-done.1
  159.0 10.3 collective-permute-done
  180.6 68.3 %all-reduce.26.cloned.1.call-done = (bf16[2,1,1,64,12,64]{5,4,3,0,2,1:T(8,128)(2,1)}, bf16[2,1,1,64,12,64]{5,4,3,0,2,1:T(8,128)(2,1)}) async-done(((bf16[2,1,1,64,12,64]{5,4,3,0,2,1:T(8,128)(2,1)}, bf16[2,1,1,64,12,64]{5,4,3,0,2,1:T(8,128)(2,1)}), (bf16[2,1,1,64,12,64]{5,4,3,0,2,1:T(8,128)(2,1)}, bf16[2,1,1,64,12,64]{5,4,3,0,2,1:T(8,128)(2,1)})) %all-reduce.26.cloned.1.call-update) | async-done | bytes 393232 | tf_op jit(solution)/shard_map/psum | solution.py:39
  257.1 57.7 %all-gather.9.cloned.1.call-done = bf16[2359296]{0:T(1024)(128)(2,1)} async-done(((bf16[73728]{0:T(1024)(128)(2,1)}), bf16[2359296]{0:T(1024)(128)(2,1)}) %all-gather.9.cloned.1.call-update) | async-done | bytes 4718608 | tf_op jit(solution)/shard_map/all_gather | solution.py:82
  314.8 8.2 reshape.902
  323.0 56.9 %all-gather.11.cloned.1.call-done = bf16[2359296]{0:T(1024)(128)(2,1)} async-done(((bf16[73728]{0:T(1024)(128)(2,1)}), bf16[2359296]{0:T(1024)(128)(2,1)}) %all-gather.11.cloned.1.call-update) | async-done | bytes 4718608 | tf_op jit(solution)/shard_map/all_gather | solution.py:83
  379.9 9.2 reshape.903
  389.2 10.9 gather_fusion.1
  400.1 9.3 reshape.976
  428.4 11.3 copy.108
  447.7 12.1 copy.110
  459.9 9.3 reshape.899
  519.3 9.6 copy.138
  528.9 9.6 copy.139
  538.5 15.6 %fusion.2 = (f32[1,12,4,3,2,64,64]{6,5,3,2,1,4,0:T(8,128)}, f32[2,1,4,3,64,12,64]{6,4,3,2,5,0,1:T(8,128)}) fusion(f32[1,1,4,12,8,64,64]{6,5,4,2,3,0,1:T(8,128)} %bitcast.209, f32[1,1,4,12,8,64,64]{6,5,4,2,3,0,1:T(8,128)} %bitcast.207), kind=kLoop, calls=%fused_computation.13 | loop fusion | flops 2359296 | bytes 22020096 | tf_op jit(solution)/shard_map/transpose | solution.py:232
  554.1 8.3 reshape.954
  562.4 8.1 copy.126
  575.0 22.1 %scatter_fusion = f32[144,2,4096]{2,1,0:T(2,128)} fusion(f32[144,2,4096]{2,1,0:T(2,128)} %broadcast_in_dim.44, s32[144]{0:T(256)S(1)} %bitcast.237, f32[144,2,4096]{2,1,0:T(2,128)} %copy.126), kind=kCustom, calls=%fused_computation.3 | custom fusion | bytes 14156352 | tf_op jit(solution)/shard_map/scatter | solution.py:233
  614.5 16.1 %copy.144 = f32[2,1,4,3,64,12,64]{6,5,4,0,2,3,1:T(8,128)} copy(f32[2,1,4,3,64,12,64]{6,4,3,2,5,0,1:T(8,128)} %get-tuple-element.85) | data formatting | bytes 9437184 | tf_op jit(solution)/shard_map/reshape | solution.py:209
  630.6 10.0 reshape.980
  670.5 11.1 reshape.920
  681.6 9.6 copy.150
  693.8 32.7 %all-reduce.22.cloned.1.call-done = bf16[2,1,2,64,768]{4,3,0,2,1:T(8,128)(2,1)} async-done(((bf16[2,1,2,64,768]{4,3,0,2,1:T(8,128)(2,1)}), bf16[2,1,2,64,768]{4,3,0,2,1:T(8,128)(2,1)}) %all-reduce.22.cloned.1.call-update) | async-done | bytes 393232 | tf_op jit(solution)/shard_map/psum | solution.py:227
  736.6 21.8 %scatter_fusion.1 = f32[48,2,4096]{2,1,0:T(2,128)S(1)} fusion(f32[48,2,4096]{2,1,0:T(2,128)S(1)} %broadcast_in_dim.43, s32[144]{0:T(256)S(1)} %bitcast.238, f32[144,2,4096]{2,1,0:T(2,128)} %bitcast_convert_fusion), kind=kCustom, calls=%fused_computation.4 | custom fusion | flops 1179648 | bytes 14156352 | tf_op jit(solution)/shard_map/scatter-add | solution.py:242
  778.7 8.1 copy.132
  786.9 8.2 reshape.917
  804.7 42.2 %all-reduce.14 = (f32[4608]{0:T(1024)}, f32[1536]{0:T(1024)S(1)}, f32[3072]{0:T(1024)}) all-reduce(f32[4608]{0:T(1024)} %reshape.921, f32[1536]{0:T(1024)S(1)} %reshape.922, f32[3072]{0:T(1024)} %get-tuple-element.122), channel_id=6, replica_groups=mesh['dp'=2,'seq'=16] {'dp','seq'}, use_global_device_ids=true, to_apply=%region_31.32.clone | all-reduce | flops 9216 | bytes 73728
  853.7 373.9 %all-reduce.24.cloned.1.call-done = (f32[1769472]{0:T(1024)}, f32[589824]{0:T(1024)}, f32[2359296]{0:T(1024)}, f32[2359296]{0:T(1024)}) async-done(((f32[1769472]{0:T(1024)}, f32[589824]{0:T(1024)}, f32[2359296]{0:T(1024)}, f32[2359296]{0:T(1024)}), (f32[1769472]{0:T(1024)}, f32[589824]{0:T(1024)}, f32[2359296]{0:T(1024)}, f32[2359296]{0:T(1024)})) %all-reduce.24.cloned.1.call-update) | async-done | bytes 28311568
  (292 shorter events, 263.5 us)
Async XLA Ops:
  7.2 64.5 %all-gather.5.cloned.1.call-start = ((), (), s32[]{:S(2)}) async-start(), calls=%async_computation.3 | async-start | bytes 3649536 | tf_op jit(solution)/shard_map/all_gather | solution.py:80
  7.9 119.2 %all-gather.7.cloned.1.call-start = ((), (), s32[]{:S(2)}) async-start(), calls=%async_computation.4 | async-start | bytes 1216512 | tf_op jit(solution)/shard_map/all_gather | solution.py:81
  8.7 240.3 %all-reduce.26.cloned.1.call-start = ((), (), s32[]{:S(2)}) async-start(), calls=%async_computation.9 | async-start | bytes 2097152 | tf_op jit(solution)/shard_map/psum | solution.py:39
  85.5 229.3 %all-gather.9.cloned.1.call-start = ((), (), s32[]{:S(2)}) async-start(), calls=%async_computation.5 | async-start | bytes 4866048 | tf_op jit(solution)/shard_map/all_gather | solution.py:82
  86.1 293.8 %all-gather.11.cloned.1.call-start = ((), (), s32[]{:S(2)}) async-start(), calls=%async_computation.6 | async-start | bytes 4866048 | tf_op jit(solution)/shard_map/all_gather | solution.py:83
  88.1 12.1 copy-start.39
  116.8 5.5 copy-start.42
  116.8 6.8 copy-start.40
  116.8 7.4 copy-start.37
  116.8 272.3 %all-to-all-start.1 = ((bf16[16,9,2,4096]{3,2,1,0:T(2,128)(2,1)}), bf16[16,9,2,4096]{3,2,1,0:T(2,128)(2,1)S(1)}, u32[]{:S(2)}, u32[]{:S(2)}) async-start(bf16[16,9,2,4096]{3,2,1,0:T(2,128)(2,1)} %bitcast.220), calls=%async_computation.1 | async-start | bytes 4718592 | tf_op jit(solution)/shard_map/all_to_all | solution.py:145
  130.5 38.9 %copy-start.22 = (bf16[1,1,256,768]{3,2,1,0:T(8,128)(2,1)S(1)}, bf16[1,1,256,768]{3,2,1,0:T(8,128)(2,1)}, u32[]{:S(2)}) copy-start(bf16[1,1,256,768]{3,2,1,0:T(8,128)(2,1)} %copy-done.21) | copy-start | bytes 1179652
  135.7 23.3 %collective-permute-start.1 = (bf16[2,1,64,768]{3,2,1,0:T(8,128)(2,1)}, bf16[2,1,64,768]{3,2,1,0:T(8,128)(2,1)S(1)}, u32[]{:S(2)}, u32[]{:S(2)}) collective-permute-start(bf16[2,1,64,768]{3,2,1,0:T(8,128)(2,1)} %get-tuple-element.81), channel_id=1, source_target_pairs={{1,0},{2,1},{3,2},{4,3},{5,4},{6,5},{7,6},{8,7},{9,8},{10,9},{11,1... | collective-permute-start | bytes 589832 | tf_op jit(solution)/shard_map/ppermute | solution.py:30
  143.1 26.2 %collective-permute-start = (bf16[2,1,64,768]{3,2,1,0:T(8,128)(2,1)}, bf16[2,1,64,768]{3,2,1,0:T(8,128)(2,1)S(1)}, u32[]{:S(2)}, u32[]{:S(2)}) collective-permute-start(bf16[2,1,64,768]{3,2,1,0:T(8,128)(2,1)} %get-tuple-element.100), channel_id=1, source_target_pairs={{0,1},{1,2},{2,3},{3,4},{4,5},{5,6},{6,7},{7,8},{8,9},{9,10},{10,1... | collective-permute-start | bytes 589832 | tf_op jit(solution)/shard_map/ppermute | solution.py:28
  400.1 16.9 %slice-start.2 = ((s8[6291456]{0:T(1024)(128)(4,1)}), s8[2097152]{0:T(1024)(128)(4,1)S(1)}, s32[]{:S(2)}) async-start(s8[6291456]{0:T(1024)(128)(4,1)} %bitcast.212), calls=%async_computation.12 | async-start | bytes 4194304
  409.4 7.6 slice-start.3
  447.7 21.5 %copy-start.1 = (bf16[4,12,512,64]{2,3,1,0:T(8,128)(2,1)}, bf16[4,12,512,64]{2,3,1,0:T(8,128)(2,1)S(1)}, u32[]{:S(2)}) copy-start(bf16[4,12,512,64]{2,3,1,0:T(8,128)(2,1)S(1)} %reshape.898) | copy-start | bytes 9437188
  478.8 5.3 copy-start.19
  487.5 5.6 slice-start.5
  495.4 7.1 copy-start.30
  499.4 9.7 slice-start
  502.5 6.6 slice-start.1
  502.5 6.6 copy-start.12
  603.1 126.6 %all-to-all-start.2 = ((bf16[16,9,2,4096]{3,2,1,0:T(2,128)(2,1)}), bf16[16,9,2,4096]{3,2,1,0:T(2,128)(2,1)}, u32[]{:S(2)}, u32[]{:S(2)}) async-start(bf16[16,9,2,4096]{3,2,1,0:T(2,128)(2,1)} %bitcast.218), calls=%async_computation.2 | async-start | bytes 4718592 | tf_op jit(solution)/shard_map/all_to_all | solution.py:234
  607.7 118.8 %all-reduce.22.cloned.1.call-start = ((), (), s32[]{:S(2)}) async-start(), calls=%async_computation.7 | async-start | bytes 786432 | tf_op jit(solution)/shard_map/psum | solution.py:227
  614.5 613.1 %all-reduce.24.cloned.1.call-start = ((), (), s32[]{:S(2)}) async-start(), calls=%async_computation.8 | async-start | bytes 56623104
  643.4 6.2 copy-start.28
  644.2 83.3 %collective-permute-start.3 = (bf16[2,1,64,768]{3,2,0,1:T(8,128)(2,1)}, bf16[2,1,64,768]{3,2,0,1:T(8,128)(2,1)}, u32[]{:S(2)}, u32[]{:S(2)}) collective-permute-start(bf16[2,1,64,768]{3,2,0,1:T(8,128)(2,1)} %bitcast.41), channel_id=1, source_target_pairs={{1,0},{2,1},{3,2},{4,3},{5,4},{6,5},{7,6},{8,7},{9,8},{10,9},{11,1... | collective-permute-start | bytes 589832 | tf_op jit(solution)/shard_map/ppermute | solution.py:30
  647.3 7.6 copy-start.14
  647.4 7.6 copy-start.20
  647.4 80.2 %collective-permute-start.2 = (bf16[2,1,64,768]{3,2,0,1:T(8,128)(2,1)}, bf16[2,1,64,768]{3,2,0,1:T(8,128)(2,1)}, u32[]{:S(2)}, u32[]{:S(2)}) collective-permute-start(bf16[2,1,64,768]{3,2,0,1:T(8,128)(2,1)} %bitcast.37), channel_id=1, source_target_pairs={{0,1},{1,2},{2,3},{3,4},{4,5},{5,6},{6,7},{7,8},{8,9},{9,10},{10,1... | collective-permute-start | bytes 589832 | tf_op jit(solution)/shard_map/ppermute | solution.py:28
  649.6 5.8 copy-start.7
  795.1 55.0 %copy-start.4 = (bf16[3,768,768]{2,1,0:T(8,128)(2,1)S(1)}, bf16[3,768,768]{2,1,0:T(8,128)(2,1)}, u32[]{:S(2)}) copy-start(bf16[3,768,768]{2,1,0:T(8,128)(2,1)} %copy-done.3) | copy-start | bytes 10616836
  (36 other events, 99.8 us)
Sparse Core Ops, SparseCore 0:
  10.9 60.7 all-gather.4
  74.6 52.5 all-gather.6
  130.7 118.2 all-reduce.25
  251.6 63.0 all-gather.8
  317.5 62.3 all-gather.10
  614.6 111.8 all-reduce.21
  795.2 432.3 all-reduce.23
where the time goes:
time: 1250 us; the launch traced here: 1240 us
  waiting for transfers between devices  635 us (51%)
  local copies, waits for them, and re-layouts  325 us (26%)
  blocking collectives  93.7 us (7%)
  other arithmetic  91.4 us (7%)
  matrix products  56.3 us (5%)
  starting transfers between devices  25 us (2%)
  between operations  15.6 us (1%)
    unnamed x8, waiting for transfers between devices  376 us
    unnamed x2, blocking collectives  83.4 us
    psum x1, waiting for transfers between devices, spread(): return lax.psum(block, axis)  68.3 us
    all_gather x1, waiting for transfers between devices, gather_weights(): lax.all_gather(expand_weight, ('dp', 'seq'), axis=0, tiled=True)  57.7 us
    all_gather x1, waiting for transfers between devices, gather_weights(): lax.all_gather(contract_weight, ('dp', 'seq'), axis=0, tiled=True)  56.9 us
    psum x1, waiting for transfers between devices, return_grads(): ends = lax.psum(ends.astype(jnp.bfloat16), 'seq').astype(jnp.float32)  32.7 us
    unnamed x123, local copies, waits for them, and re-layouts  30.2 us
    reshape x2, local copies, waits for them, and re-layouts, return_grads(): parts[:, :, :, :, 0:3].transpose(0, 1, 2, 4, 5, 3, 6)  26.1 us
  transfers between devices with their start and end apart: 13, of which 9 were waited for; matrix products, arithmetic and copies ran while one was open for 15% of the time, Pallas kernels for 0%

commit v1 on v0

--- a/solution.py
+++ b/solution.py
@@ -1,7 +1,13 @@
+import functools
+
 import jax
 import jax.numpy as jnp
 from jax import lax
+from jax.experimental import pallas as pl
+from jax.experimental.pallas import tpu as pltpu
 from jax.sharding import PartitionSpec as P
+
+MESH = pl.DeviceIdType.MESH
 
 D = 768
 FF = 3072
@@ -73,26 +79,489 @@
     return inverse * (centred - normed * jnp.mean(scaled * normed, axis=-1, keepdims=True))
 
 
+def place(nz):
+    y = lax.axis_index("dp")
+    s = lax.axis_index("seq")
+    return {"y": y, "z": s // 4, "x": (s // 2) % 2, "c": s % 2}
+
+def device(p):
+    return (p["y"], p["z"] * 4 + p["x"] * 2 + p["c"])
+
+def chip(p, nz):
+    return (p["y"] * nz + p["z"]) * 2 + p["x"]
+
+def index(p, nz):
+    return chip(p, nz) * 2 + p["c"]
+
+def nearest(m, n, j):
+    if n == 2:
+        return m if j == 0 else 1 - m
+    out = 0
+    for i in range(n):
+        rank = sorted(range(n), key=lambda s: (abs(s - i), s))
+        out = jnp.where(m == i, rank[j], out)
+    return out
+
+ORDERS = (("z", "x", "y"), ("z", "y", "x"), ("x", "y", "z"))
+
+def gather_kernel(nz, *refs):
+    k = len(ORDERS)
+    xs, gs = refs[:k], refs[k:2 * k]
+    own_sem, send_sem, recv_sem, csend, crecv = refs[2 * k:]
+    me = place(nz)
+    size = {"y": 2, "z": nz, "x": 2}
+    sib = dict(me, c=1 - me["c"])
+    bar = pltpu.get_barrier_semaphore()
+    for d in ("x", "y", "c"):
+        pl.semaphore_signal(bar, inc=1, device_id=device(dict(me, **{d: 1 - me[d]})), device_id_type=MESH)
+    @pl.when(me["z"] > 0)
+    def _():
+        pl.semaphore_signal(bar, inc=1, device_id=device(dict(me, z=me["z"] - 1)), device_id_type=MESH)
+    @pl.when(me["z"] < nz - 1)
+    def _():
+        pl.semaphore_signal(bar, inc=1, device_id=device(dict(me, z=me["z"] + 1)), device_id_type=MESH)
+    inside = jnp.where(me["z"] > 0, 1, 0) + jnp.where(me["z"] < nz - 1, 1, 0)
+    pl.semaphore_wait(bar, 3 + inside)
+
+    pending = []
+    def remote(item, src_ref, slot, sem_slot, way, to, cond=None):
+        cp = pltpu.make_async_remote_copy(src_ref=src_ref, dst_ref=gs[item].at[slot], send_sem=send_sem.at[item, sem_slot, way],
+            recv_sem=recv_sem.at[item, sem_slot], device_id=device(to), device_id_type=MESH)
+        if cond is None:
+            cp.start()
+        else:
+            pl.when(cond)(cp.start)
+        pending.append((cp, cond))
+
+    work = []
+    for item in range(k):
+        order = ORDERS[item]
+        n0, n1, n2 = (size[d] for d in order)
+        for i2 in range(n2):
+            for i1 in range(n1):
+                for i0 in range(n0):
+                    work.append((i0 + i1 + i2, item, i0, i1, i2))
+    work.sort(key=lambda w: w[0])
+    local = []
+    for depth, item, i0, i1, i2 in work:
+        order = ORDERS[item]
+        src = dict(me)
+        for d, i in zip(order, (i0, i1, i2)):
+            src[d] = nearest(me[d], size[d], i)
+        c = chip(src, nz)
+        slot = c * 2 + me["c"]
+        own = depth == 0
+        ref = xs[item] if own else gs[item].at[slot]
+        if not own:
+            pltpu.make_async_remote_copy(src_ref=ref, dst_ref=ref, send_sem=send_sem.at[item, c, 0], recv_sem=recv_sem.at[item, c],
+                device_id=device(sib), device_id_type=MESH).wait_recv()
+        stage = 2 if i2 else (1 if i1 else 0)
+        for t in range(stage, 3):
+            d = order[t]
+            onward = t == stage and not own
+            if d == "z":
+                if nz > 1:
+                    up = me["z"] < nz - 1
+                    dn = me["z"] > 0
+                    if onward:
+                        up = jnp.logical_and(up, src["z"] <= me["z"])
+                        dn = jnp.logical_and(dn, src["z"] >= me["z"])
+                    remote(item, ref, slot, c, 0, dict(me, z=jnp.minimum(me["z"] + 1, nz - 1)), up)
+                    remote(item, ref, slot, c, 1, dict(me, z=jnp.maximum(me["z"] - 1, 0)), dn)
+            elif not (onward and (i0, i1, i2)[t]):
+                remote(item, ref, slot, c, 2 if d == "x" else 3, dict(me, **{d: 1 - me[d]}))
+        cp = pltpu.make_async_remote_copy(src_ref=ref, dst_ref=gs[item].at[slot], send_sem=csend.at[item, c],
+            recv_sem=crecv.at[item, c], device_id=device(sib), device_id_type=MESH)
+        cp.start()
+        pending.append((cp, None))
+        if own:
+            lc = pltpu.make_async_copy(xs[item], gs[item].at[slot], own_sem.at[item])
+            lc.start()
+            local.append(lc)
+    for lc in local:
+        lc.wait()
+    for item in range(k):
+        def body(c, _):
+            ref = gs[item].at[c * 2 + 1 - me["c"]]
+            pltpu.make_async_remote_copy(src_ref=ref, dst_ref=ref, send_sem=csend.at[item, c], recv_sem=crecv.at[item, c],
+                device_id=device(sib), device_id_type=MESH).wait_recv()
+            return 0
+        lax.fori_loop(0, 4 * nz, body, 0)
+    for cp, cond in pending:
+        if cond is None:
+            cp.wait_send()
+        else:
+            pl.when(cond)(cp.wait_send)
+
+def gather_all(xs, nz):
+    n = 8 * nz
+    k = len(xs)
+    chips = 4 * nz
+    return pl.pallas_call(
+        functools.partial(gather_kernel, nz),
+        out_shape=[jax.ShapeDtypeStruct((n,) + x.shape, x.dtype) for x in xs],
+        in_specs=[pl.BlockSpec(memory_space=pl.ANY)] * k,
+        out_specs=[pl.BlockSpec(memory_space=pl.ANY)] * k,
+        scratch_shapes=[pltpu.SemaphoreType.DMA((k,)), pltpu.SemaphoreType.DMA((k, chips, 4)), pltpu.SemaphoreType.DMA((k, chips)),
+            pltpu.SemaphoreType.DMA((k, chips)), pltpu.SemaphoreType.DMA((k, chips))],
+        compiler_params=pltpu.CompilerParams(collective_id=0, has_side_effects=True),
+        name="gather_weights",
+    )(*xs)
+
+
+CHAIN_FIRST = (False, False, False, True, False)
+LINKS = (("x", "y"), ("x", "y"), ("y", "x"), ("x", "y"), ("x", "y"))
+
+def combine(dst, srcs):
+    rows, cols = dst.shape
+    step = min(cols, max(128, (24 * 1024 // rows) // 128 * 128))
+    while cols % step:
+        step -= 128
+    def part(sl):
+        total = srcs[0][:, sl].astype(jnp.float32)
+        for s in srcs[1:]:
+            total = total + s[:, sl].astype(jnp.float32)
+        dst[:, sl] = total.astype(dst.dtype)
+    if cols == step:
+        part(slice(None))
+    else:
+        def body(i, _):
+            part(pl.ds(pl.multiple_of(i * step, 128), step))
+            return 0
+        lax.fori_loop(0, cols // step, body, 0)
+
+def scatter_kernel(nz, k, *refs):
+    xs, outs = refs[:k], refs[k:2 * k]
+    scr = refs[2 * k:]
+    acc, rc, ra, rb, below, above = (scr[i * k:(i + 1) * k] for i in range(6))
+    csend, crecv, send_sem, recv_sem = scr[6 * k:]
+    me = place(nz)
+    mz = me["z"]
+    sib = dict(me, c=1 - me["c"])
+    bar = pltpu.get_barrier_semaphore()
+    for d in ("x", "y", "c"):
+        pl.semaphore_signal(bar, inc=1, device_id=device(dict(me, **{d: 1 - me[d]})), device_id_type=MESH)
+    @pl.when(mz > 0)
+    def _():
+        pl.semaphore_signal(bar, inc=1, device_id=device(dict(me, z=mz - 1)), device_id_type=MESH)
+    @pl.when(mz < nz - 1)
+    def _():
+        pl.semaphore_signal(bar, inc=1, device_id=device(dict(me, z=mz + 1)), device_id_type=MESH)
+    pl.semaphore_wait(bar, 3 + jnp.where(mz > 0, 1, 0) + jnp.where(mz < nz - 1, 1, 0))
+
+    pending = []
+    up_to = dict(me, z=jnp.minimum(mz + 1, nz - 1))
+    dn_to = dict(me, z=jnp.maximum(mz - 1, 0))
+
+    def copy(item, src, dst, ss, rs, to):
+        return pltpu.make_async_remote_copy(src_ref=src, dst_ref=dst, send_sem=ss, recv_sem=rs, device_id=device(to), device_id_type=MESH)
+
+    def start(cp, cond=None):
+        if cond is None:
+            cp.start()
+        else:
+            pl.when(cond)(cp.start)
+        pending.append((cp, cond))
+
+    def arrived(item, ref, sem):
+        copy(item, ref, ref, send_sem.at[item, 0], sem, sib).wait_recv()
+
+    def piece(z, x, y):
+        return (y * nz + z) * 2 + x
+
+    def coords(a, b, item):
+        la, lb = LINKS[item]
+        return {la: a, lb: b}
+
+    def wanted(item):
+        la, lb = LINKS[item]
+        out = []
+        zs = [0, nz - 1, 1, nz - 2][:nz] if nz == 4 else list(range(nz))
+        if CHAIN_FIRST[item]:
+            for z in zs:
+                for fa in (1, 0):
+                    for fb in (1, 0):
+                        out.append((z, fa, fb))
+        else:
+            for fb in (1, 0):
+                for fa in (1, 0):
+                    for z in zs:
+                        out.append((z, fa, fb))
+        return out
+
+    def flip(d, f):
+        return 1 - me[d] if f else me[d]
+
+    order_items = (1, 2, 3, 4, 0)
+    lists = {i: wanted(i) for i in range(k)}
+    for n in range(4 * nz):
+        for item in order_items:
+            z, fa, fb = lists[item][n]
+            la, lb = LINKS[item]
+            p = piece(z, **{la: flip(la, fa), lb: flip(lb, fb)})
+            start(copy(item, xs[item].at[p * 2 + 1 - me["c"]], rc[item].at[p], csend.at[item, p], crecv.at[item, p], sib))
+
+    steps = []
+    def tail(item):
+        la, lb = LINKS[item]
+        def own(p):
+            arrived(item, rc[item].at[p], crecv.at[item, p])
+            return [xs[item].at[p * 2 + me["c"]], rc[item].at[p]]
+        zs = [nz - 1, 0, nz - 2, 1] if nz == 4 else list(reversed(range(nz)))
+        if not CHAIN_FIRST[item]:
+            def stage_b(z, fa):
+                def run():
+                    a = flip(la, fa)
+                    p = piece(z, **{la: a, lb: 1 - me[lb]})
+                    combine(acc[item].at[p], own(p))
+                    s = z * 2 + a
+                    start(copy(item, acc[item].at[p], rb[item].at[s], send_sem.at[item, s], recv_sem.at[item, s], dict(me, **{lb: 1 - me[lb]})))
+                return run
+            def stage_a(z):
+                def run():
+                    a = 1 - me[la]
+                    p = piece(z, **{la: a, lb: me[lb]})
+                    s = z * 2 + a
+                    srcs = own(p)
+                    arrived(item, rb[item].at[s], recv_sem.at[item, s])
+                    combine(acc[item].at[p], srcs + [rb[item].at[s]])
+                    s2 = 2 * nz + z
+                    start(copy(item, acc[item].at[p], ra[item].at[z], send_sem.at[item, s2], recv_sem.at[item, s2], dict(me, **{la: 1 - me[la]})))
+                return run
+            def base(z):
+                p = piece(z, **{la: me[la], lb: me[lb]})
+                s = z * 2 + me[la]
+                srcs = own(p)
+                arrived(item, rb[item].at[s], recv_sem.at[item, s])
+                arrived(item, ra[item].at[z], recv_sem.at[item, 2 * nz + z])
+                return p, srcs + [rb[item].at[s], ra[item].at[z]]
+            def chain(z):
+                def run():
+                    p, srcs = base(z)
+                    sb, sa = 3 * nz + z, 4 * nz + z
+                    @pl.when(jnp.logical_and(mz == 0, z > 0))
+                    def _():
+                        combine(acc[item].at[p], srcs)
+                    @pl.when(jnp.logical_and(mz > 0, mz < z))
+                    def _():
+                        arrived(item, below[item].at[z], recv_sem.at[item, sb])
+                        combine(acc[item].at[p], srcs + [below[item].at[z]])
+                    if z > 0:
+                        start(copy(item, acc[item].at[p], below[item].at[z], send_sem.at[item, sb], recv_sem.at[item, sb], up_to), mz < z)
+                    @pl.when(jnp.logical_and(mz == nz - 1, z < nz - 1))
+                    def _():
+                        combine(acc[item].at[p], srcs)
+                    @pl.when(jnp.logical_and(mz < nz - 1, mz > z))
+                    def _():
+                        arrived(item, above[item].at[z], recv_sem.at[item, sa])
+                        combine(acc[item].at[p], srcs + [above[item].at[z]])
+                    if z < nz - 1:
+                        start(copy(item, acc[item].at[p], above[item].at[z], send_sem.at[item, sa], recv_sem.at[item, sa], dn_to), mz > z)
+                return run
+            def last():
+                for z in range(nz):
+                    @pl.when(mz == z)
+                    def _():
+                        p, srcs = piece(z, **{la: me[la], lb: me[lb]}), None
+                        s = z * 2 + me[la]
+                        srcs = [xs[item].at[p * 2 + me["c"]], rc[item].at[p], rb[item].at[s], ra[item].at[z]]
+                        if z > 0:
+                            arrived(item, below[item].at[z], recv_sem.at[item, 3 * nz + z])
+                            srcs.append(below[item].at[z])
+                        if z < nz - 1:
+                            arrived(item, above[item].at[z], recv_sem.at[item, 4 * nz + z])
+                            srcs.append(above[item].at[z])
+                        combine(outs[item], srcs)
+            out = []
+            for n, z in enumerate(zs):
+                out.append((1 + n, stage_b(z, 1)))
+            for n, z in enumerate(zs):
+                out.append((5 + n, stage_b(z, 0)))
+                out.append((5.5 + n, stage_a(z)))
+            for n, z in enumerate(zs):
+                out.append((9.5 + n, chain(z)))
+            out.append((20, last))
+            return out
+        def chain(z, fa, fb):
+            def run():
+                a, b = flip(la, fa), flip(lb, fb)
+                p = piece(z, **{la: a, lb: b})
+                q = a * 2 + b
+                srcs = own(p)
+                sb, sa = z * 4 + q, 4 * nz + z * 4 + q
+                bref, aref = below[item].at[z * 4 + q], above[item].at[z * 4 + q]
+                if z > 0:
+                    @pl.when(mz == 0)
+                    def _():
+                        combine(acc[item].at[p], srcs)
+                    @pl.when(jnp.logical_and(mz > 0, mz < z))
+                    def _():
+                        arrived(item, bref, recv_sem.at[item, sb])
+                        combine(acc[item].at[p], srcs + [bref])
+                    start(copy(item, acc[item].at[p], bref, send_sem.at[item, sb], recv_sem.at[item, sb], up_to), mz < z)
+                if z < nz - 1:
+                    @pl.when(mz == nz - 1)
+                    def _():
+                        combine(acc[item].at[p], srcs)
+                    @pl.when(jnp.logical_and(mz < nz - 1, mz > z))
+                    def _():
+                        arrived(item, aref, recv_sem.at[item, sa])
+                        combine(acc[item].at[p], srcs + [aref])
+                    start(copy(item, acc[item].at[p], aref, send_sem.at[item, sa], recv_sem.at[item, sa], dn_to), mz > z)
+            return run
+        def settle(fa, fb):
+            a, b = flip(la, fa), flip(lb, fb)
+            q = a * 2 + b
+            for z in range(nz):
+                @pl.when(mz == z)
+                def _():
+                    p = piece(z, **{la: a, lb: b})
+                    srcs = [xs[item].at[p * 2 + me["c"]], rc[item].at[p]]
+                    if z > 0:
+                        arrived(item, below[item].at[z * 4 + q], recv_sem.at[item, z * 4 + q])
+                        srcs.append(below[item].at[z * 4 + q])
+                    if z < nz - 1:
+                        arrived(item, above[item].at[z * 4 + q], recv_sem.at[item, 4 * nz + z * 4 + q])
+                        srcs.append(above[item].at[z * 4 + q])
+                    combine(acc[item].at[p], srcs)
+            return piece(mz, **{la: a, lb: b})
+        s0 = 8 * nz
+        def to_b(fa):
+            def run():
+                p = settle(fa, 1)
+                start(copy(item, acc[item].at[p], rb[item].at[fa], send_sem.at[item, s0 + fa], recv_sem.at[item, s0 + fa], dict(me, **{lb: 1 - me[lb]})))
+            return run
+        def to_a():
+            p = settle(1, 0)
+            arrived(item, rb[item].at[1], recv_sem.at[item, s0 + 1])
+            combine(ra[item].at[0], [acc[item].at[p], rb[item].at[1]])
+            start(copy(item, ra[item].at[0], ra[item].at[1], send_sem.at[item, s0 + 2], recv_sem.at[item, s0 + 2], dict(me, **{la: 1 - me[la]})))
+        def last():
+            p = settle(0, 0)
+            arrived(item, rb[item].at[0], recv_sem.at[item, s0])
+            arrived(item, ra[item].at[1], recv_sem.at[item, s0 + 2])
+            combine(outs[item], [acc[item].at[p], rb[item].at[0], ra[item].at[1]])
+        out = []
+        for n, z in enumerate(zs):
+            for m, (fa, fb) in enumerate(((1, 1), (0, 1), (1, 0), (0, 0))):
+                out.append((1 + n * 3 + m * 0.5, chain(z, fa, fb)))
+        out.append((12.6, to_b(1)))
+        out.append((12.7, to_b(0)))
+        out.append((14, to_a))
+        out.append((21, last))
+        return out
+
+    for n, item in enumerate(order_items):
+        steps += [(w + 0.01 * n, f) for w, f in tail(item)]
+    for _, f in sorted(steps, key=lambda s: s[0]):
+        f()
+    for cp, cond in pending:
+        if cond is None:
+            cp.wait_send()
+        else:
+            pl.when(cond)(cp.wait_send)
+
+def scatter_all(xs, nz):
+    k = len(xs)
+    chips = 4 * nz
+    slab = [x.shape[1:] for x in xs]
+    dt = [x.dtype for x in xs]
+    def buf(counts):
+        return [pltpu.VMEM((n,) + s, d) for n, s, d in zip(counts, slab, dt)]
+    scr = buf([chips] * k) + buf([chips] * k)
+    scr += buf([2 if CHAIN_FIRST[i] else nz for i in range(k)])
+    scr += buf([2 if CHAIN_FIRST[i] else 2 * nz for i in range(k)])
+    scr += buf([4 * nz if CHAIN_FIRST[i] else nz for i in range(k)]) * 2
+    sems = 8 * nz + 3
+    scr += [pltpu.SemaphoreType.DMA((k, chips)), pltpu.SemaphoreType.DMA((k, chips)), pltpu.SemaphoreType.DMA((k, sems)), pltpu.SemaphoreType.DMA((k, sems))]
+    return pl.pallas_call(
+        functools.partial(scatter_kernel, nz, k),
+        out_shape=[jax.ShapeDtypeStruct(s, jnp.float32) for s in slab],
+        in_specs=[pl.BlockSpec(memory_space=pltpu.VMEM)] * k,
+        out_specs=[pl.BlockSpec(memory_space=pltpu.VMEM)] * k,
+        scratch_shapes=scr,
+        compiler_params=pltpu.CompilerParams(collective_id=1, has_side_effects=True, vmem_limit_bytes=60 << 20),
+        name="scatter_grads",
+    )(*xs)
+
+
+def kernel_planes(arrays):
+    seq = lax.axis_size("seq")
+    if lax.axis_size("dp") != 2 or seq % 4 or seq > 16:
+        return 0
+    rows = [a.size % c for a, c in zip(arrays, (D, D, FF, D))]
+    return 0 if any(rows) else seq // 4
+
+
 def gather_weights(
     qkv_weight, out_weight, expand_weight, contract_weight, bias_vectors, gain_vectors, ffn_bias
 ):
-    whole = (
-        lax.all_gather(qkv_weight, ("dp", "seq"), axis=0, tiled=True),
-        lax.all_gather(out_weight, ("dp", "seq"), axis=0, tiled=True),
-        lax.all_gather(expand_weight, ("dp", "seq"), axis=0, tiled=True),
-        lax.all_gather(contract_weight, ("dp", "seq"), axis=0, tiled=True),
-        lax.all_gather(bias_vectors, ("dp", "seq"), axis=0, tiled=True),
-        lax.all_gather(gain_vectors, ("dp", "seq"), axis=0, tiled=True),
-        lax.all_gather(ffn_bias, ("dp", "seq"), axis=0, tiled=True),
-    )
+    vectors = jnp.concatenate([bias_vectors, gain_vectors, ffn_bias])
+    planes = kernel_planes((qkv_weight, out_weight, expand_weight, contract_weight))
+    if planes:
+        shards = 8 * planes
+        depth = expand_weight.size // FF
+        tail = jnp.pad(vectors, (0, depth * 128 - vectors.size)).reshape(depth, 128)
+        first = jnp.concatenate(
+            [expand_weight.reshape(depth, FF), out_weight.reshape(depth, D), tail], axis=1
+        )
+        first, contract, qkv = gather_all(
+            (first, contract_weight.reshape(-1, D), qkv_weight.reshape(-1, D)), planes
+        )
+        rows = first.reshape(D, FF + D + 128)
+        expand, out = rows[:, :FF], rows[:, FF : FF + D]
+        vectors = rows[:, FF + D :].reshape(shards, depth * 128)
+        contract = contract.reshape(FF, D)
+        qkv = qkv.reshape(3, D, D)
+    else:
+        gather = functools.partial(lax.all_gather, axis_name=("dp", "seq"), axis=0, tiled=True)
+        qkv = gather(qkv_weight).reshape(3, D, D)
+        out = gather(out_weight).reshape(D, D)
+        expand = gather(expand_weight).reshape(D, FF)
+        contract = gather(contract_weight).reshape(FF, D)
+        vectors = gather(vectors[None])
+    a, b, c = bias_vectors.size, gain_vectors.size, ffn_bias.size
+    vectors = vectors.astype(jnp.float32)
     return (
-        whole[0].reshape(3, D, D),
-        whole[1].reshape(D, D),
-        whole[2].reshape(D, FF),
-        whole[3].reshape(FF, D),
-        whole[4].astype(jnp.float32).reshape(6, D),
-        whole[5].astype(jnp.float32).reshape(2, D),
-        whole[6].astype(jnp.float32),
+        qkv,
+        out,
+        expand,
+        contract,
+        vectors[:, :a].reshape(6, D),
+        vectors[:, a : a + b].reshape(2, D),
+        vectors[:, a + b : a + b + c].reshape(FF),
+    )
+
+
+def scatter_grads(grads, planes):
+    d_qkv, d_out, d_expand, d_contract, d_biases, d_gains, d_ffn_bias = grads
+    shards = lax.axis_size("dp") * lax.axis_size("seq")
+    vectors = jnp.concatenate(
+        [v.reshape(shards, -1) for v in (d_biases, d_gains, d_ffn_bias)], axis=1
+    )
+    if planes:
+        low = [g.astype(jnp.bfloat16) for g in (d_expand, d_contract, d_qkv, d_out)]
+        width = vectors.shape[1]
+        padded = jnp.pad(vectors, ((0, 0), (0, -width % 1024)))
+        parts = [padded.reshape(shards, -1, 128)]
+        parts += [g.reshape(shards, -1, g.shape[-1]) for g in low]
+        vectors, d_expand, d_contract, d_qkv, d_out = scatter_all(parts, planes)
+        vectors = vectors.reshape(-1)[:width]
+    else:
+        d_expand, d_contract, d_qkv, d_out = [
+            lax.psum_scatter(g.reshape(-1), ("dp", "seq"), scatter_dimension=0, tiled=True)
+            for g in (d_expand, d_contract, d_qkv, d_out)
+        ]
+        vectors = lax.psum_scatter(vectors, ("dp", "seq"), scatter_dimension=0, tiled=True)[0]
+    a, b = d_biases.size // shards, d_gains.size // shards
+    return (
+        d_qkv.reshape(-1),
+        d_out.reshape(-1),
+        d_expand.reshape(-1),
+        d_contract.reshape(-1),
+        vectors[:a],
+        vectors[a : a + b],
+        vectors[a + b :],
     )
 
 
@@ -289,7 +758,7 @@
     return (result, saved)
 
 
-def layer_backward(tokens, cotangent, weights, saved):
+def layer_backward(tokens, cotangent, weights, saved, planes):
     qkv, out_w, expand, contract, biases, gains, ffn_bias = weights
     (
         query_heads,
@@ -337,7 +806,7 @@
     )
     d_query = from_heads(d_query_heads).astype(jnp.bfloat16)
     d_proj = jnp.concatenate([d_query[None], d_pair], axis=0)
-    d_qkv = jnp.einsum("rd,erf->edf", rows, d_proj, preferred_element_type=jnp.float32)
+    d_qkv = jnp.einsum("rd,erf->edf", rows, d_proj, preferred_element_type=jnp.float32).reshape(3 * D, D)
     d_tokens = d_sum1 + jnp.einsum("erf,edf->rd", d_proj, qkv, preferred_element_type=jnp.float32)
     d_bias_q = jnp.sum(d_query.astype(jnp.float32), axis=0)
     d_bias_v = jnp.sum(d_pair[1].astype(jnp.float32), axis=0)
@@ -345,16 +814,8 @@
         6 * D
     )
     d_gains = jnp.stack([d_gain1, d_gain2]).reshape(2 * D)
-    shares = (
-        lax.psum_scatter(d_qkv.reshape(3 * D * D), ("dp", "seq"), scatter_dimension=0, tiled=True),
-        lax.psum_scatter(d_out_w.reshape(D * D), ("dp", "seq"), scatter_dimension=0, tiled=True),
-        lax.psum_scatter(d_expand.reshape(D * FF), ("dp", "seq"), scatter_dimension=0, tiled=True),
-        lax.psum_scatter(
-            d_contract.reshape(FF * D), ("dp", "seq"), scatter_dimension=0, tiled=True
-        ),
-        lax.psum_scatter(d_biases, ("dp", "seq"), scatter_dimension=0, tiled=True),
-        lax.psum_scatter(d_gains, ("dp", "seq"), scatter_dimension=0, tiled=True),
-        lax.psum_scatter(d_ffn_bias, ("dp", "seq"), scatter_dimension=0, tiled=True),
+    shares = scatter_grads(
+        (d_qkv, d_out_w, d_expand, d_contract, d_biases, d_gains, d_ffn_bias), planes
     )
     return (d_tokens, shares)
 
@@ -375,11 +836,8 @@
         qkv_weight, out_weight, expand_weight, contract_weight, bias_vectors, gain_vectors, ffn_bias
     )
     result, saved = layer_forward(tokens, random_blocks, weights)
-    weights = gather_weights(
-        qkv_weight, out_weight, expand_weight, contract_weight, bias_vectors, gain_vectors, ffn_bias
-    )
-    unused, saved = layer_forward(tokens, random_blocks, weights)
-    d_tokens, shares = layer_backward(tokens, cotangent, weights, saved)
+    planes = kernel_planes((qkv_weight, out_weight, expand_weight, contract_weight))
+    d_tokens, shares = layer_backward(tokens, cotangent, weights, saved, planes)
     return (
         result.reshape(SEQ_GRP, TOK_SEQ, D),
         d_tokens.reshape(SEQ_GRP, TOK_SEQ, D),

time: 1250 us -> 776 us (0.62)
  waiting for transfers between devices: 635 us -> 141 us
  Pallas kernels: 0 us -> 150 us
  blocking collectives: 93.7 us -> 0 us
  local copies, waits for them, and re-layouts: 325 us -> 274 us
    unnamed x8 -> x2, waiting for transfers between devices: 376 us -> 0.03 us
    pallas_call x0 -> x2, Pallas kernels: none -> 150 us  [the longest x1 87.9 us: scatter_all(): pl.pallas_call(functools.partial(scatter_kernel, nz, k), out_shape=[jax.S...]
    all_gather x4 -> x0, waiting for transfers between devices: 136 us -> none  [the longest x1 57.7 us: gather_weights(): lax.all_gather(expand_weight, ('dp', 'seq'), axis=0, tiled=True)]
    unnamed x2 -> x0, blocking collectives: 83.4 us -> none
    reshape x9, local copies, waits for them, and re-layouts: 48.9 us -> 7.4 us  [the longest x1 1.72 us: gather_weights(): contract_weight.reshape(-1, D)]
    ppermute x2, waiting for transfers between devices: 10.3 us -> 30.1 us  [with_halo(): lax.ppermute(tail, axis, [(i, (i + 1) % count) for i in range(ends)])]
    unnamed x123 -> x117, local copies, waits for them, and re-layouts: 30.2 us -> 11.2 us
    psum x1, waiting for transfers between devices: 32.7 us -> 48.1 us  [return_grads(): ends = lax.psum(ends.astype(jnp.bfloat16), 'seq').astype(jnp.float32)]
  transfers between devices with their start and end apart: 13 -> 9, of which waited for: 9 -> 3; matrix products, arithmetic and copies ran while one was open for 15% -> 17% of each run, Pallas kernels for 0% -> 8%
where the time goes in v1:
time: 776 us; the launch traced here: 761 us
  local copies, waits for them, and re-layouts  274 us (35%)
  Pallas kernels  150 us (19%)
  waiting for transfers between devices  141 us (18%)
  other arithmetic  92.6 us (12%)
  matrix products  55.4 us (7%)
  starting transfers between devices  32.4 us (4%)
  between operations  15.3 us (2%)
    pallas_call x1, Pallas kernels, scatter_all(): pl.pallas_call(functools.partial(scatter_kernel, nz, k), out_shape=[jax.S...  87.9 us
    psum x1, waiting for transfers between devices, spread(): return lax.psum(block, axis)  62.8 us
    pallas_call x1, Pallas kernels, gather_all(): pl.pallas_call(functools.partial(gather_kernel, nz), out_shape=[jax.Shape...  62.6 us
    psum x1, waiting for transfers between devices, return_grads(): ends = lax.psum(ends.astype(jnp.bfloat16), 'seq').astype(jnp.float32)  48.1 us
    ppermute x2, waiting for transfers between devices, with_halo(): lax.ppermute(tail, axis, [(i, (i + 1) % count) for i in range(ends)])  30.1 us
    reshape x2, local copies, waits for them, and re-layouts, return_grads(): parts[:, :, :, :, 0:3].transpose(0, 1, 2, 4, 5, 3, 6)  26.1 us
    scatter x1, local copies, waits for them, and re-layouts, return_grads(): jnp.zeros((shards * cap, 2, BLOCK * HD), jnp.float32).at[slot].set(picked)  21.9 us
    scatter-add x1, other arithmetic, return_grads(): table.at[served.reshape(shards * cap)]  21.8 us
  transfers between devices with their start and end apart: 9, of which 3 were waited for; matrix products, arithmetic and copies ran while one was open for 17% of the time, Pallas kernels for 8%

profile of v1, /device:TPU:8, one launch (start us, length us, event | category | flops | bytes accessed | tf_op | source)
XLA Modules:
  0.0 760.9 jit_solution(14826681265582807293)
XLA Ops:
  11.0 6.3 all-to-all-start
  23.9 62.6 %gather_weights.1 = (bf16[32,24,3968]{2,1,0:T(8,128)(2,1)}, bf16[32,96,768]{2,1,0:T(8,128)(2,1)}, bf16[32,72,768]{2,1,0:T(8,128)(2,1)}) custom-call(bf16[24,3968]{1,0:T(8,128)(2,1)} %pad_maximum_fusion.10.refs_0_, bf16[96,768]{1,0:T(8,128)(2,1)} %reshape.887.refs_1_, bf16[72,768]{1,0:T(8,128)(2,1)} %reshape.888.refs_2_), custom_call_target="tpu_custom_call" | custom-call | tf_op jit(solution)/shard_map/gather_weights/pallas_call | solution.py:200
  113.5 10.8 %gather_fusion = bf16[144,2,4096]{2,1,0:T(2,128)(2,1)} fusion(bf16[48,2,4096]{2,1,0:T(2,128)(2,1)S(1)} %reshape.976, s32[1024]{0:T(1024)S(1)} %pad_clamp_fusion.1), kind=kCustom, calls=%fused_computation | custom fusion | bytes 4719168 | tf_op jit(solution)/shard_map/gather | solution.py:613
  124.3 8.0 %all-to-all-start.1 = ((bf16[16,9,2,4096]{3,2,1,0:T(2,128)(2,1)}), bf16[16,9,2,4096]{3,2,1,0:T(2,128)(2,1)}, u32[]{:S(2)}, u32[]{:S(2)}) async-start(bf16[16,9,2,4096]{3,2,1,0:T(2,128)(2,1)} %bitcast.227), calls=%async_computation.1 | async-start | bytes 4718592 | tf_op jit(solution)/shard_map/all_to_all | solution.py:614
  135.2 4.6 collective-permute-start.1
  150.5 30.1 %collective-permute-done = bf16[2,1,64,768]{3,2,1,0:T(8,128)(2,1)} collective-permute-done((bf16[2,1,64,768]{3,2,1,0:T(8,128)(2,1)}, bf16[2,1,64,768]{3,2,1,0:T(8,128)(2,1)}, u32[]{:S(2)}, u32[]{:S(2)}) %collective-permute-start) | collective-permute-done | bytes 196640 | tf_op jit(solution)/shard_map/ppermute | solution.py:34
  191.9 62.8 %all-reduce.12.cloned.1.call-done = (bf16[2,1,1,64,12,64]{5,4,3,0,2,1:T(8,128)(2,1)}, bf16[2,1,1,64,12,64]{5,4,3,0,2,1:T(8,128)(2,1)}) async-done(((bf16[2,1,1,64,12,64]{5,4,3,0,2,1:T(8,128)(2,1)}, bf16[2,1,1,64,12,64]{5,4,3,0,2,1:T(8,128)(2,1)}), (bf16[2,1,1,64,12,64]{5,4,3,0,2,1:T(8,128)(2,1)}, bf16[2,1,1,64,12,64]{5,4,3,0,2,1:T(8,128)(2,1)})) %all-reduce.12.cloned.1.call-update) | async-done | bytes 393232 | tf_op jit(solution)/shard_map/psum | solution.py:45
  256.6 5.3 maximum_bitcast_fusion
  261.9 12.6 %gather_fusion.1 = bf16[144,2,4096]{2,1,0:T(2,128)(2,1)} fusion(bf16[144,2,4096]{2,1,0:T(2,128)(2,1)} %bitcast.21, s32[1024]{0:T(1024)} %pad_clamp_fusion), kind=kCustom, calls=%fused_computation.1 | custom fusion | bytes 4719168 | tf_op jit(solution)/shard_map/gather | solution.py:615
  274.5 9.3 %reshape.977 = bf16[1,12,4,3,2,64,64]{6,5,4,3,2,1,0:T(8,128)(2,1)} reshape(bf16[144,2,4096]{2,1,0:T(2,128)(2,1)} %gather_fusion.1) | data formatting | bytes 4718592 | tf_op jit(solution)/shard_map/reshape | solution.py:616
  283.8 6.8 copy.165
  295.7 7.0 fusion.94
  302.7 11.3 %copy.106 = bf16[1,1,4,12,8,64,64]{5,4,6,3,2,1,0:T(8,128)(2,1)} copy(bf16[1,1,4,12,8,64,64]{6,3,5,2,0,4,1:T(8,128)(2,1)} %get-tuple-element.98) | data formatting | bytes 6291456 | tf_op jit(solution)/shard_map/slice | solution.py:638
  314.0 8.0 %reshape.901 = bf16[4,12,512,64]{2,3,1,0:T(8,128)(2,1)S(1)} reshape(bf16[1,1,4,12,8,64,64]{5,4,6,3,2,1,0:T(8,128)(2,1)} %copy.106) | data formatting | bytes 6291456 | tf_op jit(solution)/shard_map/reshape.194
  322.1 12.1 %copy.108 = bf16[1,1,4,12,8,64,64]{5,4,6,3,2,1,0:T(8,128)(2,1)} copy(bf16[1,1,4,12,8,64,64]{6,3,5,2,0,4,1:T(8,128)(2,1)} %get-tuple-element.99) | data formatting | bytes 6291456 | tf_op jit(solution)/shard_map/slice | solution.py:644
  334.2 9.3 %reshape.902 = bf16[4,12,512,64]{2,3,1,0:T(8,128)(2,1)} reshape(bf16[1,1,4,12,8,64,64]{5,4,6,3,2,1,0:T(8,128)(2,1)} %copy.108) | data formatting | bytes 6291456 | tf_op jit(solution)/shard_map/reshape.201
  376.3 6.3 multiply_reduce_fusion
  392.8 9.5 %copy.135 = f32[4,12,512,64]{3,2,0,1:T(8,128)} copy(f32[4,12,512,64]{2,3,1,0:T(8,128)} %broadcast_multiply_fusion) | data formatting | bytes 12582912 | tf_op jit(solution)/shard_map/stack | solution.py:669
  402.4 9.6 %copy.136 = f32[4,12,512,64]{3,2,0,1:T(8,128)} copy(f32[4,12,512,64]{2,3,1,0:T(8,128)} %fusion.21) | data formatting | bytes 12582912 | tf_op jit(solution)/shard_map/stack | solution.py:669
  411.9 15.6 %fusion.2 = (f32[1,12,4,3,2,64,64]{6,5,3,2,1,4,0:T(8,128)}, f32[2,1,4,3,64,12,64]{6,4,3,2,5,0,1:T(8,128)}) fusion(f32[1,1,4,12,8,64,64]{6,5,4,2,3,0,1:T(8,128)} %bitcast.217, f32[1,1,4,12,8,64,64]{6,5,4,2,3,0,1:T(8,128)} %bitcast.215), kind=kLoop, calls=%fused_computation.13 | loop fusion | flops 2359296 | bytes 22020096 | tf_op jit(solution)/shard_map/transpose | solution.py:701
  427.5 8.3 %reshape.960 = f32[144,2,4096]{2,0,1:T(8,128)} reshape(f32[1,12,4,3,2,64,64]{6,5,3,2,1,4,0:T(8,128)} %get-tuple-element.96) | data formatting | bytes 9437184 | tf_op jit(solution)/shard_map/reshape | solution.py:701
  435.8 8.2 %copy.124 = f32[144,2,4096]{2,1,0:T(2,128)} copy(f32[144,2,4096]{2,0,1:T(8,128)} %reshape.960) | data formatting | bytes 9437184 | tf_op jit(solution)/shard_map/reshape | solution.py:701
  448.5 21.9 %scatter_fusion = f32[144,2,4096]{2,1,0:T(2,128)} fusion(f32[144,2,4096]{2,1,0:T(2,128)} %broadcast_in_dim.70, s32[144]{0:T(256)S(1)} %bitcast.253, f32[144,2,4096]{2,1,0:T(2,128)} %copy.124), kind=kCustom, calls=%fused_computation.3 | custom fusion | bytes 14156352 | tf_op jit(solution)/shard_map/scatter | solution.py:702
  470.4 6.0 convert_element_type.238
  488.9 16.1 %copy.142 = f32[2,1,4,3,64,12,64]{6,5,4,0,2,3,1:T(8,128)} copy(f32[2,1,4,3,64,12,64]{6,4,3,2,5,0,1:T(8,128)} %get-tuple-element.97) | data formatting | bytes 9437184 | tf_op jit(solution)/shard_map/reshape | solution.py:678
  505.0 10.0 %reshape.981 = f32[2,1,4,3,64,768]{5,4,0,2,3,1:T(8,128)} reshape(f32[2,1,4,3,64,12,64]{6,5,4,0,2,3,1:T(8,128)} %copy.142) | data formatting | bytes 9437184 | tf_op jit(solution)/shard_map/reshape | solution.py:678
  520.6 4.8 collective-permute-start.3
  552.5 48.1 %all-reduce.10.cloned.1.call-done = bf16[2,1,2,64,768]{4,3,0,2,1:T(8,128)(2,1)} async-done(((bf16[2,1,2,64,768]{4,3,0,2,1:T(8,128)(2,1)}), bf16[2,1,2,64,768]{4,3,0,2,1:T(8,128)(2,1)}) %all-reduce.10.cloned.1.call-update) | async-done | bytes 393232 | tf_op jit(solution)/shard_map/psum | solution.py:696
  603.9 6.2 bitcast_convert_fusion
  610.8 21.8 %scatter_fusion.1 = f32[48,2,4096]{2,1,0:T(2,128)S(1)} fusion(f32[48,2,4096]{2,1,0:T(2,128)S(1)} %broadcast_in_dim.69, s32[144]{0:T(256)S(1)} %bitcast.254, f32[144,2,4096]{2,1,0:T(2,128)} %bitcast_convert_fusion), kind=kCustom, calls=%fused_computation.4 | custom fusion | flops 1179648 | bytes 14156352 | tf_op jit(solution)/shard_map/scatter-add | solution.py:711
  638.4 5.8 copy.138
  655.2 87.9 %scatter_grads.1 = (f32[8,128]{1,0:T(8,128)}, f32[24,3072]{1,0:T(8,128)}, f32[96,768]{1,0:T(8,128)}, f32[72,768]{1,0:T(8,128)}, f32[24,768]{1,0:T(8,128)}) custom-call(f32[32,8,128]{2,1,0:T(8,128)} %bitcast.240, bf16[32,24,3072]{2,1,0:T(8,128)(2,1)} %bitcast.219, bf16[32,96,768]{2,1,0:T(8,128)(2,1)} %bitcast.237, bf16[32,72,768]{2,1,0:T(8,128)(2,1)} %bitcast.223, ...), custom_call_target="tpu_custom_call" | custom-call | tf_op jit(solution)/shard_map/scatter_grads/pallas_call | solution.py:477
  (284 shorter events, 192.8 us)
Async XLA Ops:
  7.2 81.2 %copy-start.16 = (bf16[1,256,768]{2,1,0:T(8,128)(2,1)S(1)}, bf16[1,256,768]{2,1,0:T(8,128)(2,1)}, u32[]{:S(2)}) copy-start(bf16[1,256,768]{2,1,0:T(8,128)(2,1)} %param.18) | copy-start | bytes 1179652
  11.0 99.8 %all-to-all-start = ((s32[16,1,9]{2,1,0:T(1,128)}), s32[16,1,9]{2,1,0:T(1,128)S(1)}, u32[]{:S(2)}, u32[]{:S(2)}) async-start(s32[16,1,9]{2,1,0:T(1,128)} %bitcast.18), calls=%async_computation | async-start | bytes 16384 | tf_op jit(solution)/shard_map/all_to_all | solution.py:612
  124.3 137.7 %all-to-all-start.1 = ((bf16[16,9,2,4096]{3,2,1,0:T(2,128)(2,1)}), bf16[16,9,2,4096]{3,2,1,0:T(2,128)(2,1)}, u32[]{:S(2)}, u32[]{:S(2)}) async-start(bf16[16,9,2,4096]{3,2,1,0:T(2,128)(2,1)} %bitcast.227), calls=%async_computation.1 | async-start | bytes 4718592 | tf_op jit(solution)/shard_map/all_to_all | solution.py:614
  132.2 122.5 %all-reduce.12.cloned.1.call-start = ((), (), s32[]{:S(2)}) async-start(), calls=%async_computation.4 | async-start | bytes 2097152 | tf_op jit(solution)/shard_map/psum | solution.py:45
  133.1 47.5 %collective-permute-start = (bf16[2,1,64,768]{3,2,1,0:T(8,128)(2,1)}, bf16[2,1,64,768]{3,2,1,0:T(8,128)(2,1)}, u32[]{:S(2)}, u32[]{:S(2)}) collective-permute-start(bf16[2,1,64,768]{3,2,1,0:T(8,128)(2,1)} %get-tuple-element.112), channel_id=1, source_target_pairs={{0,1},{1,2},{2,3},{3,4},{4,5},{5,6},{6,7},{7,8},{8,9},{9,10},{10,1... | collective-permute-start | bytes 589832 | tf_op jit(solution)/shard_map/ppermute | solution.py:34
  135.2 45.4 %collective-permute-start.1 = (bf16[2,1,64,768]{3,2,1,0:T(8,128)(2,1)}, bf16[2,1,64,768]{3,2,1,0:T(8,128)(2,1)}, u32[]{:S(2)}, u32[]{:S(2)}) collective-permute-start(bf16[2,1,64,768]{3,2,1,0:T(8,128)(2,1)} %get-tuple-element.93), channel_id=1, source_target_pairs={{1,0},{2,1},{3,2},{4,3},{5,4},{6,5},{7,6},{8,7},{9,8},{10,9},{11,1... | collective-permute-start | bytes 589832 | tf_op jit(solution)/shard_map/ppermute | solution.py:36
  142.9 7.0 copy-start.42
  274.5 16.9 %slice-start.2 = ((s8[6291456]{0:T(1024)(128)(4,1)}), s8[2097152]{0:T(1024)(128)(4,1)S(1)}, s32[]{:S(2)}) async-start(s8[6291456]{0:T(1024)(128)(4,1)} %bitcast.220), calls=%async_computation.7 | async-start | bytes 4194304
  283.8 7.6 slice-start.3
  322.1 21.5 %copy-start.1 = (bf16[4,12,512,64]{2,3,1,0:T(8,128)(2,1)}, bf16[4,12,512,64]{2,3,1,0:T(8,128)(2,1)S(1)}, u32[]{:S(2)}) copy-start(bf16[4,12,512,64]{2,3,1,0:T(8,128)(2,1)S(1)} %reshape.901) | copy-start | bytes 9437188
  334.2 9.4 %copy-start.31 = (pred[4,512]{1,0:T(4,128)(4,1)S(1)}, pred[4,512]{1,0:T(4,128)(4,1)}, u32[]{:S(2)}) copy-start(pred[4,512]{1,0:T(4,128)(4,1)} %broadcast_in_dim.33) | copy-start | bytes 6148
  353.2 6.3 copy-start.19
  355.2 15.4 %copy-start.7 = (f32[256,768]{1,0:T(8,128)}, f32[256,768]{1,0:T(8,128)S(1)}, u32[]{:S(2)}) copy-start(f32[256,768]{1,0:T(8,128)S(1)} %get-tuple-element.120) | copy-start | bytes 2359300
  355.3 15.4 %copy-start.33 = (f32[256]{0:T(256)}, f32[256]{0:T(256)S(1)}, u32[]{:S(2)}) copy-start(f32[256]{0:T(256)S(1)} %broadcast_multiply_fusion.6) | copy-start | bytes 3076
  355.5 15.2 %copy-start.38 = (f32[256]{0:T(256)}, f32[256]{0:T(256)S(1)}, u32[]{:S(2)}) copy-start(f32[256]{0:T(256)S(1)} %add_rsqrt_fusion.1) | copy-start | bytes 3076
  361.9 6.6 slice-start.4
  373.9 8.7 %slice-start = ((s8[6291456]{0:T(1024)(128)(4,1)}), s8[2097152]{0:T(1024)(128)(4,1)S(1)}, s32[]{:S(2)}) async-start(s8[6291456]{0:T(1024)(128)(4,1)} %bitcast.213), calls=%async_computation.5 | async-start | bytes 4194304
  376.3 6.3 slice-start.1
  476.4 127.5 %all-to-all-start.2 = ((bf16[16,9,2,4096]{3,2,1,0:T(2,128)(2,1)}), bf16[16,9,2,4096]{3,2,1,0:T(2,128)(2,1)}, u32[]{:S(2)}, u32[]{:S(2)}) async-start(bf16[16,9,2,4096]{3,2,1,0:T(2,128)(2,1)} %bitcast.52), calls=%async_computation.2 | async-start | bytes 4718592 | tf_op jit(solution)/shard_map/all_to_all | solution.py:703
  480.9 119.7 %all-reduce.10.cloned.1.call-start = ((), (), s32[]{:S(2)}) async-start(), calls=%async_computation.3 | async-start | bytes 786432 | tf_op jit(solution)/shard_map/psum | solution.py:696
  518.6 83.1 %collective-permute-start.2 = (bf16[2,1,64,768]{3,2,0,1:T(8,128)(2,1)}, bf16[2,1,64,768]{3,2,0,1:T(8,128)(2,1)}, u32[]{:S(2)}, u32[]{:S(2)}) collective-permute-start(bf16[2,1,64,768]{3,2,0,1:T(8,128)(2,1)} %bitcast.41), channel_id=1, source_target_pairs={{0,1},{1,2},{2,3},{3,4},{4,5},{5,6},{6,7},{7,8},{8,9},{9,10},{10,1... | collective-permute-start | bytes 589832 | tf_op jit(solution)/shard_map/ppermute | solution.py:34
  520.6 81.0 %collective-permute-start.3 = (bf16[2,1,64,768]{3,2,0,1:T(8,128)(2,1)}, bf16[2,1,64,768]{3,2,0,1:T(8,128)(2,1)}, u32[]{:S(2)}, u32[]{:S(2)}) collective-permute-start(bf16[2,1,64,768]{3,2,0,1:T(8,128)(2,1)} %bitcast.45), channel_id=1, source_target_pairs={{1,0},{2,1},{3,2},{4,3},{5,4},{6,5},{7,6},{8,7},{9,8},{10,9},{11,1... | collective-permute-start | bytes 589832 | tf_op jit(solution)/shard_map/ppermute | solution.py:36
  530.2 10.0 %copy-start.35 = (f32[768]{0:T(1024)S(1)}, f32[768]{0:T(1024)}, u32[]{:S(2)}) copy-start(f32[768]{0:T(1024)} %get-tuple-element.75) | copy-start | bytes 9220
  530.2 10.0 %copy-start.11 = (f32[256,768]{1,0:T(8,128)S(1)}, f32[256,768]{1,0:T(8,128)}, u32[]{:S(2)}) copy-start(f32[256,768]{1,0:T(8,128)} %copy-done.10) | copy-start | bytes 2359300
  530.2 10.0 %copy-start.20 = (bf16[256,768]{0,1:T(8,128)(2,1)S(1)}, bf16[256,768]{0,1:T(8,128)(2,1)}, u32[]{:S(2)}) copy-start(bf16[256,768]{0,1:T(8,128)(2,1)} %copy-done.19) | copy-start | bytes 1179652
  530.2 11.5 %copy-start.8 = (f32[256,768]{1,0:T(8,128)S(1)}, f32[256,768]{1,0:T(8,128)}, u32[]{:S(2)}) copy-start(f32[256,768]{1,0:T(8,128)} %copy-done.7) | copy-start | bytes 2359300
  530.2 11.5 %copy-start.34 = (f32[256]{0:T(256)S(1)}, f32[256]{0:T(256)}, u32[]{:S(2)}) copy-start(f32[256]{0:T(256)} %copy-done.33) | copy-start | bytes 3076
  603.9 6.9 copy-start.44
  655.2 91.6 %copy-start.12 = (f32[256,768]{1,0:T(8,128)S(1)}, f32[256,768]{1,0:T(8,128)}, u32[]{:S(2)}) copy-start(f32[256,768]{1,0:T(8,128)} %copy-done.10) | copy-start | bytes 2359300
  655.2 91.6 %copy-start.14 = (bf16[2,1,256,768]{3,2,0,1:T(8,128)(2,1)S(1)}, bf16[2,1,256,768]{3,2,0,1:T(8,128)(2,1)}, u32[]{:S(2)}) copy-start(bf16[2,1,256,768]{3,2,0,1:T(8,128)(2,1)} %copy-done.13) | copy-start | bytes 2359300
  655.2 91.6 %copy-start.21 = (bf16[1,256,768]{2,1,0:T(8,128)(2,1)S(1)}, bf16[1,256,768]{2,1,0:T(8,128)(2,1)}, u32[]{:S(2)}) copy-start(bf16[1,256,768]{2,1,0:T(8,128)(2,1)} %reshape.978) | copy-start | bytes 1179652
  746.9 6.3 copy-start.30
  (34 other events, 118.2 us)
Sparse Core Ops, SparseCore 0:
  142.2 112.4 all-reduce.11
  489.0 111.5 all-reduce.9

commit v2 on v1

--- a/solution.py
+++ b/solution.py
@@ -21,28 +21,6 @@
 
 norm_eps = 1e-12
 masked_score = -1e30
-
-
-def with_halo(cells, sides, width):
-    for axis, dim in sides:
-        count = lax.axis_size(axis)
-        ends = count - 1
-        head = lax.slice_in_dim(cells, 0, width, axis=dim)
-        tail = lax.slice_in_dim(cells, cells.shape[dim] - width, cells.shape[dim], axis=dim)
-        cells = jnp.concatenate(
-            [
-                lax.ppermute(tail, axis, [(i, (i + 1) % count) for i in range(ends)]),
-                cells,
-                lax.ppermute(head, axis, [((i + 1) % count, i) for i in range(ends)]),
-            ],
-            axis=dim,
-        )
-    return cells
-
-
-def spread(block, axis, source):
-    block = jnp.where(lax.axis_index(axis) == source, block, jnp.zeros_like(block))
-    return lax.psum(block, axis)
 
 
 def matmul(left, right):
@@ -565,172 +543,448 @@
     )
 
 
-def to_heads(rows):
-    return rows.reshape(SEQ_GRP, BPD, BLOCK, H, HD).transpose(0, 1, 3, 2, 4)
-
-
-def from_heads(heads):
-    return heads.transpose(0, 1, 3, 2, 4).reshape(SEQ_GRP * TOK_SEQ, D)
-
-
-def key_blocks(pair, picks):
-    shards = lax.axis_size("seq")
+def owner(head, n):
+    return head * n // H
+
+
+def owned(place, n):
+    head = (place * H + n - 1) // n
+    return jnp.minimum(head, H - 1), jnp.logical_and(head < H, owner(head, n) == place)
+
+
+def greet_senders(n, place, mine, to_owners):
+    row = lax.axis_index("dp")
+    bar = pltpu.get_barrier_semaphore()
+
+    def signal(to):
+        @pl.when(to != place)
+        def _():
+            pl.semaphore_signal(bar, inc=1, device_id=(row, to), device_id_type=MESH)
+
+    if to_owners:
+
+        @pl.when(mine)
+        def _():
+            lax.fori_loop(0, n, lambda s, _: (signal(s), 0)[1], 0)
+
+        pl.semaphore_wait(bar, H - jnp.where(mine, 1, 0))
+    else:
+        lax.fori_loop(0, H, lambda h, _: (signal(owner(h, n)), 0)[1], 0)
+
+        @pl.when(mine)
+        def _():
+            pl.semaphore_wait(bar, n - 1)
+
+
+def send_to_owners(n, place, head, mine, pairs, sems):
+    row = lax.axis_index("dp")
+    send_sem, recv_sem, own_sem = sems
+    first = head + 1
+
+    def walk(act):
+        def body(k, _):
+            h = (first + k) % H
+            to = owner(h, n)
+            for i, (src, dst) in enumerate(pairs):
+
+                @pl.when(to != place)
+                def _():
+                    act(
+                        pltpu.make_async_remote_copy(
+                            src_ref=src.at[h],
+                            dst_ref=dst.at[place],
+                            send_sem=send_sem.at[i, h],
+                            recv_sem=recv_sem.at[i, place],
+                            device_id=(row, to),
+                            device_id_type=MESH,
+                        )
+                    )
+
+            return 0
+
+        lax.fori_loop(0, H, body, 0)
+
+    walk(lambda cp: cp.start())
+
+    @pl.when(mine)
+    def _():
+        for i, (src, dst) in enumerate(pairs):
+            cp = pltpu.make_async_copy(src.at[head], dst.at[place], own_sem.at[i])
+            cp.start()
+            cp.wait()
+
+        def body(k, _):
+            s = (place + 1 + k) % n
+            for i, (src, dst) in enumerate(pairs):
+                pltpu.make_async_remote_copy(
+                    src_ref=src.at[0],
+                    dst_ref=dst.at[s],
+                    send_sem=send_sem.at[i, 0],
+                    recv_sem=recv_sem.at[i, s],
+                    device_id=(row, place),
+                    device_id_type=MESH,
+                ).wait_recv()
+            return 0
+
+        lax.fori_loop(0, n - 1, body, 0)
+
+    walk(lambda cp: cp.wait_send())
+
+
+def send_from_owners(n, place, head, mine, src, dst, sems):
+    row = lax.axis_index("dp")
+    send_sem, recv_sem, own_sem = sems
+
+    def walk(act):
+        def body(k, _):
+            to = (place + 1 + k) % n
+            act(
+                pltpu.make_async_remote_copy(
+                    src_ref=src.at[to],
+                    dst_ref=dst.at[head],
+                    send_sem=send_sem.at[0, to],
+                    recv_sem=recv_sem.at[0, head],
+                    device_id=(row, to),
+                    device_id_type=MESH,
+                )
+            )
+            return 0
+
+        lax.fori_loop(0, n - 1, body, 0)
+
+    @pl.when(mine)
+    def _():
+        walk(lambda cp: cp.start())
+        cp = pltpu.make_async_copy(src.at[place], dst.at[head], own_sem.at[0])
+        cp.start()
+        cp.wait()
+
+    def body(k, _):
+        h = (head + k) % H
+
+        @pl.when(owner(h, n) != place)
+        def _():
+            pltpu.make_async_remote_copy(
+                src_ref=src.at[0],
+                dst_ref=dst.at[h],
+                send_sem=send_sem.at[0, 0],
+                recv_sem=recv_sem.at[0, h],
+                device_id=(row, place),
+                device_id_type=MESH,
+            ).wait_recv()
+
+        return 0
+
+    lax.fori_loop(0, H, body, 0)
+
+    @pl.when(mine)
+    def _():
+        walk(lambda cp: cp.wait_send())
+
+
+def swap_halves(tile):
+    return pltpu.roll(tile, HD, tile.ndim - 1)
+
+
+def low_lanes(shape):
+    return lax.broadcasted_iota(jnp.int32, shape, len(shape) - 1) < HD
+
+
+def project_kernel(n, rows_ref, w_ref, bias_ref, picks_ref, out_ref, out_picks_ref, box, *sems):
     place = lax.axis_index("seq")
-    nblocks = BPD * shards
-    rims = with_halo(pair, (("seq", 2),), BLOCK)
-    wide = rims.reshape(2, SEQ_GRP, BPD + 2, BLOCK, D)
-    window = jnp.stack(
-        [wide[:, :, 0:BPD], wide[:, :, 1 : BPD + 1], wide[:, :, 2 : BPD + 2]], axis=3
-    )
-    window = window.reshape(2, SEQ_GRP, BPD, 3, BLOCK, H, HD).transpose(0, 1, 2, 5, 3, 4, 6)
-    first = spread(pair[:, :, :BLOCK], "seq", 0)
-    last = spread(pair[:, :, TOK_SEQ - BLOCK :], "seq", shards - 1)
-    ends = (
-        jnp.stack([first, last], axis=2)
-        .reshape(2, SEQ_GRP, 2, BLOCK, H, HD)
-        .transpose(0, 1, 4, 2, 3, 5)
-    )
-    ends = jnp.broadcast_to(ends[:, :, None], (2, SEQ_GRP, BPD, H, 2, BLOCK, HD))
-    count = SEQ_GRP * H * BPD * 3
-    cap = (count + shards - 1) // shards
-    flat = picks.reshape(count)
-    holder = flat // BPD
-    within = flat % BPD
-    order = jnp.arange(count, dtype=jnp.int32)
-    seq_of = order // (H * BPD * 3)
-    head_of = order // (BPD * 3) % H
-    tile_id = (seq_of * BPD + within) * H + head_of
-    owners = (holder[:, None] == jnp.arange(shards, dtype=jnp.int32)[None, :]).astype(jnp.int32)
-    rank = jnp.sum((jnp.cumsum(owners, axis=0) - owners) * owners, axis=1)
-    slot = holder * cap + rank
-    asked = jnp.zeros((shards * cap,), jnp.int32).at[slot].set(tile_id).reshape(shards, cap)
-    tiles = (
-        pair.reshape(2, SEQ_GRP, BPD, BLOCK, H, HD)
-        .transpose(1, 2, 4, 0, 3, 5)
-        .reshape(SEQ_GRP * BPD * H, 2, BLOCK * HD)
-    )
-    wanted = lax.all_to_all(asked, "seq", split_axis=0, concat_axis=0, tiled=True)
-    picked = tiles[wanted]
-    returned = lax.all_to_all(picked, "seq", split_axis=0, concat_axis=0, tiled=True)
-    mine = returned.reshape(shards * cap, 2, BLOCK * HD)[slot]
-    mine = mine.reshape(SEQ_GRP, H, BPD, 3, 2, BLOCK, HD).transpose(4, 0, 2, 1, 3, 5, 6)
-    listing = jnp.concatenate([window, ends, mine], axis=4).reshape(
-        2, SEQ_GRP, BPD, H, 8 * BLOCK, HD
-    )
-    position = place * BPD + jnp.arange(BPD, dtype=jnp.int32)
-    always = jnp.ones((BPD,), dtype=bool)
-    valid = jnp.stack(
-        [position >= 1, always, position + 1 < nblocks, always, always, always, always, always],
-        axis=1,
-    )
-    valid = jnp.broadcast_to(valid[:, :, None], (BPD, 8, BLOCK)).reshape(BPD, 8 * BLOCK)
-    return (listing, valid, slot, wanted, cap)
-
-
-def score(query, keys, valid):
-    scores = jnp.einsum(
-        "sbhqd,sbhkd->sbhqk", query, keys, preferred_element_type=jnp.float32
-    ) * HD ** (-0.5)
-    return jnp.where(valid[None, :, None, None, :], scores, masked_score)
-
-
-def attend(query, listing, valid):
-    scores = score(query, listing[0], valid)
-    top = jnp.max(scores, axis=-1, keepdims=True)
-    weights = jnp.exp(scores - top)
-    total = jnp.sum(weights, axis=-1, keepdims=True)
-    probs = (weights / total).astype(jnp.bfloat16)
-    attended = jnp.einsum(
-        "sbhqk,sbhkd->sbhqd", probs, listing[1], preferred_element_type=jnp.float32
-    )
-    return (attended, top + jnp.log(total))
-
-
-def attend_back(query, listing, valid, lse, grad_out):
-    probs = jnp.exp(score(query, listing[0], valid) - lse)
-    d_probs = jnp.einsum(
-        "sbhqd,sbhkd->sbhqk", grad_out, listing[1], preferred_element_type=jnp.float32
-    )
-    d_values = jnp.einsum(
-        "sbhqk,sbhqd->sbhkd",
-        probs.astype(jnp.bfloat16),
-        grad_out,
-        preferred_element_type=jnp.float32,
-    )
-    d_scores = (probs * (d_probs - jnp.sum(probs * d_probs, axis=-1, keepdims=True))).astype(
-        jnp.bfloat16
-    )
-    d_query = jnp.einsum(
-        "sbhqk,sbhkd->sbhqd", d_scores, listing[0], preferred_element_type=jnp.float32
-    ) * HD ** (-0.5)
-    d_keys = jnp.einsum(
-        "sbhqk,sbhqd->sbhkd", d_scores, query, preferred_element_type=jnp.float32
-    ) * HD ** (-0.5)
-    return (d_query, jnp.stack([d_keys, d_values]))
-
-
-def return_grads(grads, slot, served, cap):
-    shards = lax.axis_size("seq")
+    head, mine = owned(place, n)
+    greet_senders(n, place, mine, True)
+    rows = rows_ref[...]
+    left = low_lanes((TOK_SEQ, 128))
+    left_q = low_lanes((BLOCK, 128))
+    wide = 256
+    for g in range(D // wide):
+        cols = slice(g * wide, (g + 1) * wide)
+        q = (matmul(rows, w_ref[0, :, cols]) + bias_ref[0:1, cols]) * HD ** (-0.5)
+        k = matmul(rows, w_ref[1, :, cols])
+        v = matmul(rows, w_ref[2, :, cols]) + bias_ref[1:2, cols]
+        for p in range(wide // 128):
+            h = (g * wide + p * 128) // HD
+            lanes = slice(p * 128, (p + 1) * 128)
+            kp, vp, qp = k[:, lanes], v[:, lanes], q[:, lanes]
+            box[h, 0:TOK_SEQ, :] = jnp.where(left, kp, swap_halves(vp)).astype(jnp.bfloat16)
+            box[h + 1, 0:TOK_SEQ, :] = jnp.where(left, swap_halves(kp), vp).astype(jnp.bfloat16)
+            turned = swap_halves(qp)
+            for t in range(BPD // 2):
+                a = slice(2 * t * BLOCK, (2 * t + 1) * BLOCK)
+                b = slice((2 * t + 1) * BLOCK, (2 * t + 2) * BLOCK)
+                to = slice(TOK_SEQ + t * BLOCK, TOK_SEQ + (t + 1) * BLOCK)
+                box[h, to, :] = jnp.where(left_q, qp[a], turned[b]).astype(jnp.bfloat16)
+                box[h + 1, to, :] = jnp.where(left_q, turned[a], qp[b]).astype(jnp.bfloat16)
+    send_to_owners(
+        n, place, head, mine, ((box, out_ref), (picks_ref, out_picks_ref)), sems
+    )
+
+
+def exchange_sems(n, pairs=1):
+    return [
+        pltpu.SemaphoreType.DMA((pairs, max(n, H))),
+        pltpu.SemaphoreType.DMA((pairs, max(n, H))),
+        pltpu.SemaphoreType.DMA((pairs,)),
+    ]
+
+
+ANY = pl.BlockSpec(memory_space=pl.ANY)
+VMEM = pl.BlockSpec(memory_space=pltpu.VMEM)
+SMEM = pl.BlockSpec(memory_space=pltpu.SMEM)
+MSG = TOK_SEQ + TOK_SEQ // 2
+
+
+def project_and_send(rows, qkv, biases, picks):
+    n = lax.axis_size("seq")
+    picks = jnp.pad(picks.reshape(H, 1, BPD * 3), ((0, 0), (0, 7), (0, 128 - BPD * 3)))
+    return pl.pallas_call(
+        functools.partial(project_kernel, n),
+        out_shape=(
+            jax.ShapeDtypeStruct((n, MSG, 128), jnp.bfloat16),
+            jax.ShapeDtypeStruct((n, 8, 128), jnp.int32),
+        ),
+        in_specs=[VMEM, VMEM, VMEM, ANY],
+        out_specs=(ANY, ANY),
+        scratch_shapes=[pltpu.VMEM((H, MSG, 128), jnp.bfloat16)] + exchange_sems(n, 2),
+        compiler_params=pltpu.CompilerParams(
+            collective_id=2, has_side_effects=True, vmem_limit_bytes=48 << 20
+        ),
+        name="project_and_send",
+    )(rows, qkv, biases, picks)
+
+
+def to_owners_kernel(n, src, dst, *sems):
     place = lax.axis_index("seq")
-    count = SEQ_GRP * H * BPD * 3
-    parts = grads.reshape(2, SEQ_GRP, BPD, H, 8, BLOCK, HD)
-    window = (
-        parts[:, :, :, :, 0:3].transpose(0, 1, 2, 4, 5, 3, 6).reshape(2, SEQ_GRP, BPD, 3, BLOCK, D)
-    )
-    wide = sum(
-        (
-            jnp.pad(window[:, :, :, w], ((0, 0), (0, 0), (w, 2 - w), (0, 0), (0, 0)))
-            for w in range(3)
-        )
-    )
-    edges = jnp.concatenate([wide[:, :, 0], wide[:, :, BPD + 1]], axis=2)
-    arrived = with_halo(edges.astype(jnp.bfloat16), (("seq", 2),), BLOCK).astype(edges.dtype)
-    local = wide[:, :, 1 : BPD + 1].reshape(2, SEQ_GRP, TOK_SEQ, D)
-    local = local.at[:, :, :BLOCK].add(arrived[:, :, :BLOCK])
-    local = local.at[:, :, TOK_SEQ - BLOCK :].add(arrived[:, :, 3 * BLOCK :])
-    ends = (
-        jnp.sum(parts[:, :, :, :, 3:5], axis=2)
-        .transpose(0, 1, 3, 4, 2, 5)
-        .reshape(2, SEQ_GRP, 2, BLOCK, D)
-    )
-    ends = lax.psum(ends.astype(jnp.bfloat16), "seq").astype(jnp.float32)
-    local = local.at[:, :, :BLOCK].add(jnp.where(place == 0, ends[:, :, 0], 0.0))
-    local = local.at[:, :, TOK_SEQ - BLOCK :].add(
-        jnp.where(place == shards - 1, ends[:, :, 1], 0.0)
-    )
-    picked = parts[:, :, :, :, 5:8].transpose(1, 3, 2, 4, 0, 5, 6).reshape(count, 2, BLOCK * HD)
-    outbox = jnp.zeros((shards * cap, 2, BLOCK * HD), jnp.float32).at[slot].set(picked)
-    inbox = lax.all_to_all(
-        outbox.reshape(shards, cap, 2, BLOCK * HD).astype(jnp.bfloat16),
-        "seq",
-        split_axis=0,
-        concat_axis=0,
-        tiled=True,
-    ).astype(jnp.float32)
-    table = jnp.zeros((SEQ_GRP * BPD * H, 2, BLOCK * HD), jnp.float32)
-    table = table.at[served.reshape(shards * cap)].add(inbox.reshape(shards * cap, 2, BLOCK * HD))
-    table = (
-        table.reshape(SEQ_GRP, BPD, H, 2, BLOCK, HD)
-        .transpose(3, 0, 1, 4, 2, 5)
-        .reshape(2, SEQ_GRP, TOK_SEQ, D)
-    )
-    return local + table
+    head, mine = owned(place, n)
+    greet_senders(n, place, mine, True)
+    send_to_owners(n, place, head, mine, ((src, dst),), sems)
+
+
+def from_owners_kernel(n, src, dst, *sems):
+    place = lax.axis_index("seq")
+    head, mine = owned(place, n)
+    greet_senders(n, place, mine, False)
+    send_from_owners(n, place, head, mine, src, dst, sems)
+
+
+def exchange(kernel, slots, messages, ident, name):
+    n = lax.axis_size("seq")
+    return pl.pallas_call(
+        functools.partial(kernel, n),
+        out_shape=jax.ShapeDtypeStruct((slots,) + messages.shape[1:], messages.dtype),
+        in_specs=[ANY],
+        out_specs=ANY,
+        scratch_shapes=exchange_sems(n),
+        compiler_params=pltpu.CompilerParams(collective_id=ident, has_side_effects=True),
+        name=name,
+    )(messages)
+
+
+def key_list(i, n, picks_ref):
+    last = n * BPD - 1
+
+    def of(b):
+        s, r = b // BPD, b % BPD
+        picked = [picks_ref[s, 0, r * 3 + j] for j in range(3)]
+        return [jnp.maximum(b - 1, 0), b, jnp.minimum(b + 1, last), 0, last] + picked
+
+    return [
+        [(b // BPD, pl.multiple_of(b % BPD * BLOCK, BLOCK)) for b in of(2 * i + t)]
+        for t in range(2)
+    ]
+
+
+def fill_pair(lists, kv_ref, vk_ref, keys, values):
+    for j in range(8):
+        (sa, ra), (sb, rb) = lists[0][j], lists[1][j]
+        to = slice(j * BLOCK, (j + 1) * BLOCK)
+        keys[to, 0:HD] = kv_ref[sa, pl.ds(ra, BLOCK), 0:HD]
+        keys[to, HD:128] = vk_ref[sb, pl.ds(rb, BLOCK), HD:128]
+        values[to, 0:HD] = vk_ref[sa, pl.ds(ra, BLOCK), 0:HD]
+        values[to, HD:128] = kv_ref[sb, pl.ds(rb, BLOCK), HD:128]
+
+
+def two_blocks(tile):
+    left = low_lanes(tile.shape)
+    zero = jnp.zeros_like(tile)
+    return jnp.concatenate([jnp.where(left, tile, zero), jnp.where(left, zero, tile)], axis=0)
+
+
+def pair_scores(i, n, keys, query):
+    scores = outer_cols(keys, query)
+    left = low_lanes((BLOCK, 128))
+    right = jnp.logical_not(left)
+    end = n * BPD // 2 - 1
+    hide_first = jnp.logical_and(left, i == 0)
+    hide_last = jnp.logical_and(right, i == end)
+    return jnp.concatenate(
+        [
+            jnp.where(hide_first, masked_score, scores[0:BLOCK]),
+            scores[BLOCK : 2 * BLOCK],
+            jnp.where(hide_last, masked_score, scores[2 * BLOCK : 3 * BLOCK]),
+            scores[3 * BLOCK :],
+        ],
+        axis=0,
+    )
+
+
+def pair_place(i):
+    return i // (BPD // 2), pl.multiple_of(i % (BPD // 2) * BLOCK, BLOCK)
+
+
+def turn_pairs(n, kv_ref, vk_ref):
+    def body(s, _):
+        tile = kv_ref[s, 0:TOK_SEQ, :].astype(jnp.float32)
+        vk_ref[s] = swap_halves(tile).astype(jnp.bfloat16)
+        return 0
+
+    lax.fori_loop(0, n, body, 0)
+
+
+def attend_kernel(n, kvq_ref, picks_ref, out_ref, lse_ref, vk_ref, keys, values):
+    place = lax.axis_index("seq")
+    head, mine = owned(place, n)
+
+    @pl.when(mine)
+    def _():
+        turn_pairs(n, kvq_ref, vk_ref)
+
+        def body(i, _):
+            fill_pair(key_list(i, n, picks_ref), kvq_ref, vk_ref, keys, values)
+            s, r = pair_place(i)
+            query = two_blocks(kvq_ref[s, pl.ds(TOK_SEQ + r, BLOCK), :])
+            scores = pair_scores(i, n, keys[...], query)
+            top = jnp.max(scores, axis=0, keepdims=True)
+            weights = jnp.exp(scores - top)
+            total = jnp.sum(weights, axis=0, keepdims=True)
+            probs = (weights * (1.0 / total)).astype(jnp.bfloat16)
+            full = inner_rows(probs, values[...])
+            left = low_lanes((BLOCK, 128))
+            out_ref[s, pl.ds(r, BLOCK), :] = jnp.where(left, full[:BLOCK], full[BLOCK:]).astype(
+                jnp.bfloat16
+            )
+            lse_ref[i] = top + jnp.log(total)
+            return 0
+
+        lax.fori_loop(0, n * BPD // 2, body, 0)
+
+
+def attend_heads(kvq, picks):
+    n = lax.axis_size("seq")
+    return pl.pallas_call(
+        functools.partial(attend_kernel, n),
+        out_shape=(
+            jax.ShapeDtypeStruct((n, TOK_SEQ // 2, 128), jnp.bfloat16),
+            jax.ShapeDtypeStruct((n * BPD // 2, 1, 128), jnp.float32),
+        ),
+        in_specs=[VMEM, SMEM],
+        out_specs=(VMEM, VMEM),
+        scratch_shapes=[
+            pltpu.VMEM((n, TOK_SEQ, 128), jnp.bfloat16),
+            pltpu.VMEM((8 * BLOCK, 128), jnp.bfloat16),
+            pltpu.VMEM((8 * BLOCK, 128), jnp.bfloat16),
+        ],
+        compiler_params=pltpu.CompilerParams(vmem_limit_bytes=48 << 20),
+        name="attend_heads",
+    )(kvq, picks)
+
+
+def attend_back_kernel(
+    n, kvq_ref, picks_ref, lse_ref, grad_ref, out_ref, vk_ref, keys, values, sum_k, sum_v
+):
+    place = lax.axis_index("seq")
+    head, mine = owned(place, n)
+
+    @pl.when(mine)
+    def _():
+        turn_pairs(n, kvq_ref, vk_ref)
+
+        def clear(s, _):
+            sum_k[s] = jnp.zeros((TOK_SEQ, 128), jnp.float32)
+            sum_v[s] = jnp.zeros((TOK_SEQ, 128), jnp.float32)
+            return 0
+
+        lax.fori_loop(0, n, clear, 0)
+
+        def body(i, _):
+            lists = key_list(i, n, picks_ref)
+            fill_pair(lists, kvq_ref, vk_ref, keys, values)
+            s, r = pair_place(i)
+            query = two_blocks(kvq_ref[s, pl.ds(TOK_SEQ + r, BLOCK), :])
+            grad = two_blocks(grad_ref[s, pl.ds(r, BLOCK), :])
+            probs = jnp.exp(pair_scores(i, n, keys[...], query) - lse_ref[i])
+            d_probs = outer_cols(values[...], grad)
+            rows = jnp.sum(probs * d_probs, axis=0, keepdims=True)
+            d_scores = (probs * (d_probs - rows)).astype(jnp.bfloat16)
+            d_values = matmul(probs.astype(jnp.bfloat16), grad)
+            d_keys = matmul(d_scores, query)
+            full = inner_rows(d_scores, keys[...]) * HD ** (-0.5)
+            left = low_lanes((BLOCK, 128))
+            out_ref[s, pl.ds(TOK_SEQ + r, BLOCK), :] = jnp.where(
+                left, full[:BLOCK], full[BLOCK:]
+            ).astype(jnp.bfloat16)
+            for j in range(8):
+                part = slice(j * BLOCK, (j + 1) * BLOCK)
+                for t in range(2):
+                    sb, rb = lists[t][j]
+                    lanes = slice(t * HD, (t + 1) * HD)
+                    sum_k[sb, pl.ds(rb, BLOCK), lanes] += d_keys[part, lanes]
+                    sum_v[sb, pl.ds(rb, BLOCK), lanes] += d_values[part, lanes]
+            return 0
+
+        lax.fori_loop(0, n * BPD // 2, body, 0)
+
+        def close(s, _):
+            left = low_lanes((TOK_SEQ, 128))
+            k, v = sum_k[s], sum_v[s]
+            both = jnp.where(left, k + swap_halves(k), v + swap_halves(v))
+            out_ref[s, 0:TOK_SEQ, :] = both.astype(jnp.bfloat16)
+            return 0
+
+        lax.fori_loop(0, n, close, 0)
+
+
+def attend_heads_back(kvq, picks, lse, grad):
+    n = lax.axis_size("seq")
+    return pl.pallas_call(
+        functools.partial(attend_back_kernel, n),
+        out_shape=jax.ShapeDtypeStruct((n, MSG, 128), jnp.bfloat16),
+        in_specs=[VMEM, SMEM, VMEM, VMEM],
+        out_specs=VMEM,
+        scratch_shapes=[
+            pltpu.VMEM((n, TOK_SEQ, 128), jnp.bfloat16),
+            pltpu.VMEM((8 * BLOCK, 128), jnp.bfloat16),
+            pltpu.VMEM((8 * BLOCK, 128), jnp.bfloat16),
+            pltpu.VMEM((n, TOK_SEQ, 128), jnp.float32),
+            pltpu.VMEM((n, TOK_SEQ, 128), jnp.float32),
+        ],
+        compiler_params=pltpu.CompilerParams(vmem_limit_bytes=56 << 20),
+        name="attend_heads_back",
+    )(kvq, picks, lse, grad)
+
+
+def pack_heads(rows):
+    parts = rows.reshape(BPD // 2, 2, BLOCK, H, HD).transpose(3, 0, 2, 1, 4)
+    return parts.reshape(H, TOK_SEQ // 2, 128)
+
+
+def unpack_heads(parts):
+    parts = parts.reshape(H, BPD // 2, BLOCK, 2, HD).transpose(1, 3, 2, 0, 4)
+    return parts.reshape(TOK_SEQ, D)
+
+
+def unpack_keys(parts):
+    parts = parts.reshape(H, TOK_SEQ, 2, HD).transpose(2, 1, 0, 3)
+    return parts.reshape(2, TOK_SEQ, D)
 
 
 def layer_forward(tokens, picks, weights):
     qkv, out_w, expand, contract, biases, gains, ffn_bias = weights
     rows = tokens.reshape(SEQ_GRP * TOK_SEQ, D)
-    projected = jnp.einsum("rd,edf->erf", rows, qkv, preferred_element_type=jnp.float32)
-    query = (projected[0] + biases[0]).astype(jnp.bfloat16)
-    pair = (
-        jnp.stack([projected[1], projected[2] + biases[1]])
-        .astype(jnp.bfloat16)
-        .reshape(2, SEQ_GRP, TOK_SEQ, D)
-    )
-    listing, valid, slot, served, cap = key_blocks(pair, picks)
-    query_heads = to_heads(query)
-    attended, lse = attend(query_heads, listing, valid)
-    mixed = from_heads(attended.astype(jnp.bfloat16))
+    kvq, picks = project_and_send(rows, qkv, biases, picks)
+    attended, lse = attend_heads(kvq, picks)
+    mixed = unpack_heads(exchange(from_owners_kernel, H, attended, 3, "return_heads"))
     hidden1 = rows.astype(jnp.float32) + matmul(mixed, out_w) + biases[2]
     normed_out1, normed1, inverse1 = normalize(hidden1, gains[0], biases[3])
     lowered = normed_out1.astype(jnp.bfloat16)
@@ -739,9 +993,8 @@
     hidden2 = normed_out1 + matmul(active, contract) + biases[4]
     result, normed2, inverse2 = normalize(hidden2, gains[1], biases[5])
     saved = (
-        query_heads,
-        listing,
-        valid,
+        kvq,
+        picks,
         lse,
         mixed,
         normed1,
@@ -751,9 +1004,6 @@
         active,
         normed2,
         inverse2,
-        slot,
-        served,
-        cap,
     )
     return (result, saved)
 
@@ -761,9 +1011,8 @@
 def layer_backward(tokens, cotangent, weights, saved, planes):
     qkv, out_w, expand, contract, biases, gains, ffn_bias = weights
     (
-        query_heads,
-        listing,
-        valid,
+        kvq,
+        picks,
         lse,
         mixed,
         normed1,
@@ -773,9 +1022,6 @@
         active,
         normed2,
         inverse2,
-        slot,
-        served,
-        cap,
     ) = saved
     rows = tokens.reshape(SEQ_GRP * TOK_SEQ, D)
     grad = cotangent.reshape(SEQ_GRP * TOK_SEQ, D).astype(jnp.float32)
@@ -798,13 +1044,14 @@
     d_bias_out = jnp.sum(d_attn.astype(jnp.float32), axis=0)
     d_out_w = inner_rows(mixed, d_attn)
     d_mixed = outer_cols(d_attn, out_w).astype(jnp.bfloat16)
-    d_query_heads, d_list = attend_back(query_heads, listing, valid, lse, to_heads(d_mixed))
-    d_pair = (
-        return_grads(d_list, slot, served, cap)
-        .astype(jnp.bfloat16)
-        .reshape(2, SEQ_GRP * TOK_SEQ, D)
-    )
-    d_query = from_heads(d_query_heads).astype(jnp.bfloat16)
+    d_heads = exchange(
+        to_owners_kernel, lax.axis_size("seq"), pack_heads(d_mixed), 4, "send_head_grads"
+    )
+    d_heads = exchange(
+        from_owners_kernel, H, attend_heads_back(kvq, picks, lse, d_heads), 5, "return_head_grads"
+    )
+    d_query = unpack_heads(d_heads[:, TOK_SEQ:])
+    d_pair = unpack_keys(d_heads[:, :TOK_SEQ])
     d_proj = jnp.concatenate([d_query[None], d_pair], axis=0)
     d_qkv = jnp.einsum("rd,erf->edf", rows, d_proj, preferred_element_type=jnp.float32).reshape(3 * D, D)
     d_tokens = d_sum1 + jnp.einsum("erf,edf->rd", d_proj, qkv, preferred_element_type=jnp.float32)

time: 776 us -> 407 us (0.52); the launches traced: 761 us -> 401 us
  local copies, waits for them, and re-layouts: 274 us -> 51.9 us
  Pallas kernels: 150 us -> 301 us
  waiting for transfers between devices: 141 us -> 0 us
  other arithmetic: 92.6 us -> 11.6 us
  starting transfers between devices: 32.4 us -> 0 us
  matrix products: 55.4 us -> 34.5 us
  between operations: 15.3 us -> 1.57 us
    pallas_call x0 -> x6, Pallas kernels: none -> 151 us  [the longest x3 70.1 us: exchange(): pl.pallas_call(functools.partial(kernel, n), out_shape=jax.ShapeDtypeStru...]
    psum x2 -> x0, waiting for transfers between devices: 111 us -> none  [the longest x1 62.8 us: spread(): return lax.psum(block, axis)]
    reshape x16 -> x9, local copies, waits for them, and re-layouts: 81.5 us -> 15.9 us  [the longest x4 10.7 us: unpack_heads(): parts = parts.reshape(H, BPD // 2, BLOCK, 2, HD).transpose(1, 3, 2, 0, 4)]
    another operation x19 -> x2, local copies, waits for them, and re-layouts: 55 us -> 4.91 us  [layer_backward(): d_proj = jnp.concatenate([d_query[None], d_pair], axis=0)]
    slice x8 -> x3, local copies, waits for them, and re-layouts: 34.2 us -> 3.41 us  [the longest x1 1.93 us: layer_backward(): d_query = unpack_heads(d_heads[:, TOK_SEQ:])]
    ppermute x4 -> x0, waiting for transfers between devices: 30.1 us -> none  [the longest x2 30.1 us: with_halo(): lax.ppermute(tail, axis, [(i, (i + 1) % count) for i in range(ends)])]
    transpose x3 -> x0, other arithmetic: 24.5 us -> none  [the longest x1 15.6 us: return_grads(): parts[:, :, :, :, 5:8].transpose(1, 3, 2, 4, 0, 5, 6)]
    scatter-add x5 -> x0, other arithmetic: 24 us -> none  [the longest x1 21.8 us: return_grads(): table.at[served.reshape(shards * cap)]]
  transfers between devices with their start and end apart: 9 -> 0, of which waited for: 3 -> 0; matrix products, arithmetic and copies ran while one was open for 17% -> 0% of each run, Pallas kernels for 8% -> 0%
where the time goes in v2:
time: 407 us; the launch traced here: 401 us
  Pallas kernels  301 us (74%)
  local copies, waits for them, and re-layouts  51.9 us (13%)
  matrix products  34.5 us (8%)
  other arithmetic  11.6 us (3%)
    pallas_call x1, Pallas kernels, scatter_all(): pl.pallas_call(functools.partial(scatter_kernel, nz, k), out_shape=[jax.S...  88 us
    pallas_call x3, Pallas kernels, exchange(): pl.pallas_call(functools.partial(kernel, n), out_shape=jax.ShapeDtypeStru...  70.1 us
    pallas_call x1, Pallas kernels, gather_all(): pl.pallas_call(functools.partial(gather_kernel, nz), out_shape=[jax.Shape...  62.1 us
    pallas_call x1, Pallas kernels, project_and_send(): pl.pallas_call(functools.partial(project_kernel, n), out_shape=(jax.Shape...  33.4 us
    pallas_call x1, Pallas kernels, attend_heads_back(): pl.pallas_call(functools.partial(attend_back_kernel, n), out_shape=jax.Sh...  25.5 us
    pallas_call x1, Pallas kernels, attend_heads(): pl.pallas_call(functools.partial(attend_kernel, n), out_shape=(jax.ShapeD...  21.9 us
    dot_general x3, matrix products, inner_rows(): lax.dot_general(left, right, (((0,), (0,)), ((), ())), preferred_element_...  10.9 us
    reshape x4, local copies, waits for them, and re-layouts, unpack_heads(): parts = parts.reshape(H, BPD // 2, BLOCK, 2, HD).transpose(1, 3, 2, 0, 4)  10.7 us

profile of v2, /device:TPU:8, one launch (start us, length us, event | category | flops | bytes accessed | tf_op | source)
XLA Modules:
  0.0 400.6 jit_solution(13074905802051048067)
XLA Ops:
  4.0 1.7 reshape.175.refs_1_
  5.7 1.7 reshape.176.refs_2_
  7.4 62.1 %gather_weights.1 = (bf16[32,24,3968]{2,1,0:T(8,128)(2,1)}, bf16[32,96,768]{2,1,0:T(8,128)(2,1)}, bf16[32,72,768]{2,1,0:T(8,128)(2,1)}) custom-call(bf16[24,3968]{1,0:T(8,128)(2,1)} %pad_maximum_fusion.3.refs_0_, bf16[96,768]{1,0:T(8,128)(2,1)} %reshape.175.refs_1_, bf16[72,768]{1,0:T(8,128)(2,1)} %reshape.176.refs_2_), custom_call_target="tpu_custom_call" | custom-call | tf_op jit(solution)/shard_map/gather_weights/pallas_call | solution.py:178
  70.9 2.0 copy-done.1
  72.9 33.4 %project_and_send.1 = (bf16[16,384,128]{2,1,0:T(8,128)(2,1)S(1)}, s32[16,8,128]{2,1,0:T(8,128)S(1)}) custom-call(bf16[256,768]{1,0:T(8,128)(2,1)S(1)} %bitcast.77, bf16[3,768,768]{2,1,0:T(8,128)(2,1)S(1)} %bitcast.75, f32[6,768]{1,0:T(8,128)S(1)} %reshape.179.bias_ref, s32[12,8,128]{2,1,0:T(8,128)S(1)} %pad.13.picks_ref), custom_call_target="tpu_custom_call" | custom-call | tf_op jit(solution)/shard_map/project_and_send/pallas_call | solution.py:741
  106.3 21.9 %attend_heads.1 = (bf16[16,128,128]{2,1,0:T(8,128)(2,1)S(1)}, f32[32,1,128]{2,1,0:T(1,128)S(1)}) custom-call(bf16[16,384,128]{2,1,0:T(8,128)(2,1)S(1)} %get-tuple-element.23.kvq_ref, s32[16,8,128]{2,1,0:T(8,128)S(1)} %get-tuple-element.24.picks_ref), custom_call_target="tpu_custom_call" | custom-call | tf_op jit(solution)/shard_map/attend_heads/pallas_call | solution.py:875
  129.6 17.1 %return_heads.1 = bf16[12,128,128]{2,1,0:T(8,128)(2,1)} custom-call(bf16[16,128,128]{2,1,0:T(8,128)(2,1)} %copy-done.5), custom_call_target="tpu_custom_call" | custom-call | tf_op jit(solution)/shard_map/return_heads/pallas_call | solution.py:773
  146.7 2.1 reshape.181
  148.9 1.9 copy.25
  150.8 2.6 reshape.182
  153.3 2.0 fusion.54
  156.5 4.0 fusion.4
  160.6 2.1 fusion.55
  165.2 6.4 %convert_reduce_fusion = (f32[3072]{0:T(1024)}, bf16[256,3072]{1,0:T(8,128)(2,1)S(1)}) fusion(f32[256,3072]{1,0:T(8,128)S(1)} %copy-done.25, bf16[3072,768]{1,0:T(8,128)(2,1)} %bitcast.102, f32[256,768]{1,0:T(8,128)S(1)} %get-tuple-element.45), kind=kOutput, calls=%fused_computation.16 | convolution fusion | flops 1225454592 | bytes 10235904 | tf_op jit(solution)/shard_map/dot_general | solution.py:37
  171.6 2.2 multiply_reduce_fusion
  178.4 14.1 %send_head_grads.1.grad_ref = bf16[16,128,128]{2,1,0:T(8,128)(2,1)} custom-call(bf16[12,128,128]{2,1,0:T(8,128)(2,1)} %reshape.186.src), custom_call_target="tpu_custom_call" | custom-call | tf_op jit(solution)/shard_map/send_head_grads/pallas_call | solution.py:773
  192.4 25.5 %attend_heads_back.1.src = bf16[16,384,128]{2,1,0:T(8,128)(2,1)} custom-call(bf16[16,384,128]{2,1,0:T(8,128)(2,1)} %copy-done, s32[16,8,128]{2,1,0:T(8,128)} %copy-done.6, f32[32,1,128]{2,1,0:T(1,128)} %copy-done.7, bf16[16,128,128]{2,1,0:T(8,128)(2,1)} %send_head_grads.1.grad_ref), custom_call_target="tpu_custom_call" | custom-call | tf_op jit(solution)/shard_map/attend_heads_back/pallas_call | solution.py:950
  217.9 39.0 %return_head_grads.1 = bf16[12,384,128]{2,1,0:T(8,128)(2,1)} custom-call(bf16[16,384,128]{2,1,0:T(8,128)(2,1)} %attend_heads_back.1.src), custom_call_target="tpu_custom_call" | custom-call | tf_op jit(solution)/shard_map/return_head_grads/pallas_call | solution.py:773
  260.5 1.9 slice.74
  262.4 3.0 reshape.187
  265.4 3.7 copy.28
  269.1 3.0 broadcast_in_dim_reshape.4
  272.1 1.9 copy.31
  274.0 3.5 fusion.19
  279.9 3.3 convert_reduce_fusion.1
  287.9 5.0 %convolution_convert_fusion.1 = bf16[768,3072]{1,0:T(8,128)(2,1)} fusion(bf16[256,3072]{1,0:T(8,128)(2,1)S(1)} %copy-done.18, f32[256,768]{1,0:T(8,128)} %copy-done.8, f32[768]{0:T(1024)S(1)} %get-tuple-element.42, f32[768]{0:T(1024)S(1)} %mul.144, f32[256]{0:T(256)} %copy-done.22, f32[256]{0:T(256)S(1)} %broadcast_multiply_fusion.5), kind=kOutput, calls=%fused_computation.1 | convolution fusion | flops 1211301888 | bytes 7086080 | tf_op jit(solution)/shard_map/dot_general | solution.py:31
  292.9 4.4 %convolution_convert_fusion = bf16[3072,768]{1,0:T(8,128)(2,1)} fusion(f32[256,768]{1,0:T(8,128)S(1)} %copy-done.20, f32[256,3072]{1,0:T(8,128)S(1)} %copy-done.26), kind=kOutput, calls=%fused_computation | convolution fusion | flops 1217593344 | bytes 8650752 | tf_op jit(solution)/shard_map/dot_general | solution.py:31
  297.3 2.9 convolution_convert_fusion.2
  301.8 88.0 %scatter_grads.1 = (f32[8,128]{1,0:T(8,128)}, f32[24,3072]{1,0:T(8,128)}, f32[96,768]{1,0:T(8,128)}, f32[72,768]{1,0:T(8,128)}, f32[24,768]{1,0:T(8,128)}) custom-call(f32[32,8,128]{2,1,0:T(8,128)} %bitcast.88, bf16[32,24,3072]{2,1,0:T(8,128)(2,1)} %bitcast.78, bf16[32,96,768]{2,1,0:T(8,128)(2,1)} %bitcast.84, bf16[32,72,768]{2,1,0:T(8,128)(2,1)} %bitcast.79, ...), custom_call_target="tpu_custom_call" | custom-call | tf_op jit(solution)/shard_map/scatter_grads/pallas_call | solution.py:455
  389.8 1.6 reshape.196
  393.0 1.7 copy.34
  394.7 1.7 reshape.199
  (123 shorter events, 31.7 us)
Async XLA Ops:
  0.6 70.2 %copy-start.3 = (bf16[1,256,768]{2,1,0:T(8,128)(2,1)S(1)}, bf16[1,256,768]{2,1,0:T(8,128)(2,1)}, u32[]{:S(2)}) copy-start(bf16[1,256,768]{2,1,0:T(8,128)(2,1)} %param.10) | copy-start | bytes 1179652
  0.7 70.1 %copy-start.23 = (s32[1,12,4,3]{1,2,3,0:T(4,128)S(1)}, s32[1,12,4,3]{1,2,3,0:T(4,128)}, u32[]{:S(2)}) copy-start(s32[1,12,4,3]{1,2,3,0:T(4,128)} %param.18) | copy-start | bytes 1732
  70.5 35.9 %copy-start.21 = (f32[32,3072]{1,0:T(8,128)}, f32[32,3072]{1,0:T(8,128)S(1)}, u32[]{:S(2)}) copy-start(f32[32,3072]{1,0:T(8,128)S(1)} %reshape.201) | copy-start | bytes 1179652
  70.9 2.0 copy-start.1
  106.3 47.0 %copy-start = (bf16[16,384,128]{2,1,0:T(8,128)(2,1)}, bf16[16,384,128]{2,1,0:T(8,128)(2,1)S(1)}, u32[]{:S(2)}) copy-start(bf16[16,384,128]{2,1,0:T(8,128)(2,1)S(1)} %get-tuple-element.23.kvq_ref) | copy-start | bytes 4718596
  106.3 47.0 %copy-start.6 = (s32[16,8,128]{2,1,0:T(8,128)}, s32[16,8,128]{2,1,0:T(8,128)S(1)}, u32[]{:S(2)}) copy-start(s32[16,8,128]{2,1,0:T(8,128)S(1)} %get-tuple-element.24.picks_ref) | copy-start | bytes 196612
  128.2 0.8 copy-start.5
  129.0 0.6 copy-start.7
  153.3 7.2 %copy-start.14 = (bf16[256,768]{0,1:T(8,128)(2,1)}, bf16[256,768]{0,1:T(8,128)(2,1)S(1)}, u32[]{:S(2)}) copy-start(bf16[256,768]{0,1:T(8,128)(2,1)S(1)} %reshape.182) | copy-start | bytes 1179652
  155.3 18.4 %copy-start.8 = (f32[256,768]{1,0:T(8,128)}, f32[256,768]{1,0:T(8,128)S(1)}, u32[]{:S(2)}) copy-start(f32[256,768]{1,0:T(8,128)S(1)} %get-tuple-element.52) | copy-start | bytes 2359300
  156.3 4.2 %slice-start.2 = ((s8[4718592]{0:T(1024)(128)(4,1)}), s8[4194304]{0:T(1024)(128)(4,1)S(1)}, s32[]{:S(2)}) async-start(s8[4718592]{0:T(1024)(128)(4,1)} %bitcast.103), calls=%async_computation.2 | async-start | bytes 8388608
  156.5 17.3 %copy-start.22 = (f32[256]{0:T(256)}, f32[256]{0:T(256)S(1)}, u32[]{:S(2)}) copy-start(f32[256]{0:T(256)S(1)} %add_rsqrt_fusion.1) | copy-start | bytes 3076
  156.5 4.0 slice-start.3
  160.5 2.1 copy-start.24
  160.5 2.4 copy-start.12
  163.0 2.2 copy-start.25
  163.9 7.6 %slice-start = ((s8[6094848]{0:T(1024)(128)(4,1)}), s8[4194304]{0:T(1024)(128)(4,1)S(1)}, s32[]{:S(2)}) async-start(s8[6094848]{0:T(1024)(128)(4,1)} %bitcast.92), calls=%async_computation | async-start | bytes 8388608
  165.2 6.4 %copy-start.19 = (f32[256,768]{1,0:T(8,128)}, f32[256,768]{1,0:T(8,128)S(1)}, u32[]{:S(2)}) copy-start(f32[256,768]{1,0:T(8,128)S(1)} %get-tuple-element.45) | copy-start | bytes 2359300
  165.2 6.4 %slice-start.1 = ((s8[6094848]{0:T(1024)(128)(4,1)}), s8[1900544]{0:T(1024)(128)(4,1)S(1)}, s32[]{:S(2)}) async-start(s8[6094848]{0:T(1024)(128)(4,1)} %bitcast.92), calls=%async_computation.1 | async-start | bytes 3801088
  171.6 2.2 copy-start.17
  174.7 0.9 copy-start.9
  258.4 0.9 copy-start.11
  260.5 13.5 %copy-start.2 = (bf16[32,72,768]{2,1,0:T(8,128)(2,1)S(1)}, bf16[32,72,768]{2,1,0:T(8,128)(2,1)}, u32[]{:S(2)}) copy-start(bf16[32,72,768]{2,1,0:T(8,128)(2,1)} %get-tuple-element.21) | copy-start | bytes 10616836
  277.5 10.4 %copy-start.18 = (bf16[256,3072]{1,0:T(8,128)(2,1)S(1)}, bf16[256,3072]{1,0:T(8,128)(2,1)}, u32[]{:S(2)}) copy-start(bf16[256,3072]{1,0:T(8,128)(2,1)} %copy-done.17) | copy-start | bytes 4718596
  287.9 5.0 %copy-start.20 = (f32[256,768]{1,0:T(8,128)S(1)}, f32[256,768]{1,0:T(8,128)}, u32[]{:S(2)}) copy-start(f32[256,768]{1,0:T(8,128)} %copy-done.19) | copy-start | bytes 2359300
  287.9 5.0 %copy-start.26 = (f32[256,3072]{1,0:T(8,128)S(1)}, f32[256,3072]{1,0:T(8,128)}, u32[]{:S(2)}) copy-start(f32[256,3072]{1,0:T(8,128)} %copy-done.24) | copy-start | bytes 9437188
  292.9 4.5 %copy-start.4 = (bf16[1,256,768]{2,1,0:T(8,128)(2,1)S(1)}, bf16[1,256,768]{2,1,0:T(8,128)(2,1)}, u32[]{:S(2)}) copy-start(bf16[1,256,768]{2,1,0:T(8,128)(2,1)} %param.10) | copy-start | bytes 1179652
  292.9 4.5 %copy-start.13 = (bf16[2,256,768]{2,1,0:T(8,128)(2,1)S(1)}, bf16[2,256,768]{2,1,0:T(8,128)(2,1)}, u32[]{:S(2)}) copy-start(bf16[2,256,768]{2,1,0:T(8,128)(2,1)} %copy.32) | copy-start | bytes 2359300
  292.9 4.5 %copy-start.16 = (bf16[1,256,768]{2,1,0:T(8,128)(2,1)S(1)}, bf16[1,256,768]{2,1,0:T(8,128)(2,1)}, u32[]{:S(2)}) copy-start(bf16[1,256,768]{2,1,0:T(8,128)(2,1)} %copy.31) | copy-start | bytes 1179652
  297.3 2.9 copy-start.10
  297.3 2.9 copy-start.15

commit v3 on v2

--- a/solution.py
+++ b/solution.py
@@ -37,10 +37,6 @@
     return lax.dot_general(
         left, right, (((1,), (1,)), ((), ())), preferred_element_type=jnp.float32
     )
-
-
-def gelu_tanh(value):
-    return jax.nn.gelu(value, approximate=True)
 
 
 def normalize(value, gain, shift):
@@ -486,28 +482,27 @@
         first, contract, qkv = gather_all(
             (first, contract_weight.reshape(-1, D), qkv_weight.reshape(-1, D)), planes
         )
-        rows = first.reshape(D, FF + D + 128)
-        expand, out = rows[:, :FF], rows[:, FF : FF + D]
-        vectors = rows[:, FF + D :].reshape(shards, depth * 128)
+        first = first.reshape(D, FF + D + 128)
+        vectors = first[:, FF + D :].reshape(shards, depth * 128)
         contract = contract.reshape(FF, D)
         qkv = qkv.reshape(3, D, D)
     else:
         gather = functools.partial(lax.all_gather, axis_name=("dp", "seq"), axis=0, tiled=True)
         qkv = gather(qkv_weight).reshape(3, D, D)
-        out = gather(out_weight).reshape(D, D)
-        expand = gather(expand_weight).reshape(D, FF)
+        first = jnp.concatenate(
+            [gather(expand_weight).reshape(D, FF), gather(out_weight).reshape(D, D)], axis=1
+        )
         contract = gather(contract_weight).reshape(FF, D)
         vectors = gather(vectors[None])
     a, b, c = bias_vectors.size, gain_vectors.size, ffn_bias.size
     vectors = vectors.astype(jnp.float32)
+    rows = [vectors[:, :a].reshape(6, D), vectors[:, a : a + b].reshape(2, D)]
     return (
         qkv,
-        out,
-        expand,
+        first,
         contract,
-        vectors[:, :a].reshape(6, D),
-        vectors[:, a : a + b].reshape(2, D),
-        vectors[:, a + b : a + b + c].reshape(FF),
+        jnp.concatenate(rows),
+        vectors[:, a + b : a + b + c].reshape(1, FF),
     )
 
 
@@ -527,7 +522,7 @@
         vectors = vectors.reshape(-1)[:width]
     else:
         d_expand, d_contract, d_qkv, d_out = [
-            lax.psum_scatter(g.reshape(-1), ("dp", "seq"), scatter_dimension=0, tiled=True)
+            lax.psum_scatter(g.reshape(-1).astype(jnp.float32), ("dp", "seq"), scatter_dimension=0, tiled=True)
             for g in (d_expand, d_contract, d_qkv, d_out)
         ]
         vectors = lax.psum_scatter(vectors, ("dp", "seq"), scatter_dimension=0, tiled=True)[0]
@@ -576,7 +571,7 @@
             pl.semaphore_wait(bar, n - 1)
 
 
-def send_to_owners(n, place, head, mine, pairs, sems):
+def send_to_owners(n, place, head, mine, pairs, sems, meanwhile=None):
     row = lax.axis_index("dp")
     send_sem, recv_sem, own_sem = sems
     first = head + 1
@@ -605,6 +600,8 @@
         lax.fori_loop(0, H, body, 0)
 
     walk(lambda cp: cp.start())
+    if meanwhile is not None:
+        meanwhile()
 
     @pl.when(mine)
     def _():
@@ -754,13 +751,6 @@
     )(rows, qkv, biases, picks)
 
 
-def to_owners_kernel(n, src, dst, *sems):
-    place = lax.axis_index("seq")
-    head, mine = owned(place, n)
-    greet_senders(n, place, mine, True)
-    send_to_owners(n, place, head, mine, ((src, dst),), sems)
-
-
 def from_owners_kernel(n, src, dst, *sems):
     place = lax.axis_index("seq")
     head, mine = owned(place, n)
@@ -964,9 +954,212 @@
     )(kvq, picks, lse, grad)
 
 
-def pack_heads(rows):
-    parts = rows.reshape(BPD // 2, 2, BLOCK, H, HD).transpose(3, 0, 2, 1, 4)
-    return parts.reshape(H, TOK_SEQ // 2, 128)
+UNITS = 32
+WIDE = 768
+
+
+def greet_row(n, place, mine):
+    row = lax.axis_index("dp")
+    bar = pltpu.get_barrier_semaphore()
+
+    def body(s, _):
+        there = owned(s, n)[1]
+
+        @pl.when(jnp.logical_and(s != place, jnp.logical_or(mine, there)))
+        def _():
+            pl.semaphore_signal(bar, inc=1, device_id=(row, s), device_id_type=MESH)
+
+        return 0
+
+    lax.fori_loop(0, n, body, 0)
+    pl.semaphore_wait(bar, jnp.where(mine, n - 1, H))
+
+
+def unpack_pair(tiles, odd, shape):
+    left = low_lanes(shape)
+    a, b = tiles.astype(jnp.float32), odd.astype(jnp.float32)
+    return (jnp.where(left, a, swap_halves(b)), jnp.where(left, swap_halves(a), b))
+
+
+def mid_kernel(n, *refs):
+    (
+        attended,
+        rows_ref,
+        cot_ref,
+        first_hbm,
+        second_hbm,
+        vec_ref,
+        ffn_ref,
+        result_ref,
+        d_sum1_ref,
+        d_heads,
+        dw1_hbm,
+        dw2_hbm,
+        dwo_hbm,
+        small_ref,
+        d_ffn_ref,
+        inbox,
+        box,
+        w1_ref,
+        wo_ref,
+        w2_ref,
+        slope_ref,
+        active_ref,
+        dw1_ref,
+        dw2_ref,
+        dwo_ref,
+        mixed_ref,
+        load_sem,
+        store_sem,
+    ) = refs[:28]
+    sems_in, sems_out = refs[28:31], refs[31:34]
+    place = lax.axis_index("seq")
+    head, mine = owned(place, n)
+    loads = [
+        pltpu.make_async_copy(first_hbm.at[:, FF : FF + D], wo_ref, load_sem.at[0]),
+        pltpu.make_async_copy(first_hbm.at[:, 0:FF], w1_ref, load_sem.at[1]),
+        pltpu.make_async_copy(second_hbm, w2_ref, load_sem.at[2]),
+    ]
+    for cp in loads:
+        cp.start()
+    greet_row(n, place, mine)
+    send_from_owners(n, place, head, mine, attended, inbox, sems_in)
+
+    for h in range(0, H, 2):
+        for t in range(BPD // 2):
+            part = slice(t * BLOCK, (t + 1) * BLOCK)
+            a, b = unpack_pair(inbox[h, part, :], inbox[h + 1, part, :], (BLOCK, 128))
+            lanes = slice(h * HD, (h + 2) * HD)
+            mixed_ref[2 * t * BLOCK : (2 * t + 1) * BLOCK, lanes] = a.astype(jnp.bfloat16)
+            mixed_ref[(2 * t + 1) * BLOCK : (2 * t + 2) * BLOCK, lanes] = b.astype(jnp.bfloat16)
+    loads[0].wait()
+    hidden1 = rows_ref[...].astype(jnp.float32) + matmul(mixed_ref[...], wo_ref[...]) + vec_ref[2:3]
+    normed_out1, normed1, inverse1 = normalize(hidden1, vec_ref[6:7], vec_ref[3:4])
+    lowered = normed_out1.astype(jnp.bfloat16)
+    loads[1].wait()
+    loads[2].wait()
+
+    def up_step(c, hidden):
+        cols = pl.ds(pl.multiple_of(c * WIDE, WIDE), WIDE)
+        up = matmul(lowered, w1_ref[:, cols]) + ffn_ref[:, cols]
+        square = up * up
+        inner = (2 / jnp.pi) ** 0.5 * (up + 0.044715 * up * square)
+        curve = jnp.tanh(inner)
+        active = (0.5 * up * (1 + curve)).astype(jnp.bfloat16)
+        slope_ref[:, cols] = 0.5 * (1 + curve) + 0.5 * up * (1 - curve * curve) * (
+            (2 / jnp.pi) ** 0.5 * (1 + 3 * 0.044715 * square)
+        )
+        active_ref[:, cols] = active
+        return hidden + matmul(active, w2_ref[cols, :])
+
+    hidden2 = lax.fori_loop(0, FF // WIDE, up_step, normed_out1 + vec_ref[4:5])
+    result, normed2, inverse2 = normalize(hidden2, vec_ref[7:8], vec_ref[5:6])
+    result_ref[...] = result
+    grad = cot_ref[...].astype(jnp.float32)
+    d_sum2 = normalize_back(grad, normed2, inverse2, vec_ref[7:8])
+    d_down = d_sum2.astype(jnp.bfloat16)
+
+    def add_rows(value):
+        return jnp.sum(value, axis=0, keepdims=True)
+
+    small_ref[2:3] = add_rows(d_down.astype(jnp.float32))
+    small_ref[3:4] = add_rows(grad)
+    small_ref[5:6] = add_rows(grad * normed2)
+
+    def stores(c):
+        cols = pl.ds(pl.multiple_of(c * WIDE, WIDE), WIDE)
+        slabs = pl.ds(c * (UNITS * WIDE // FF), UNITS * WIDE // FF)
+        return (
+            pltpu.make_async_copy(dw1_ref.at[:, :, cols], dw1_hbm.at[:, :, cols], store_sem.at[0, c]),
+            pltpu.make_async_copy(dw2_ref.at[slabs], dw2_hbm.at[slabs], store_sem.at[1, c]),
+        )
+
+    def back_step(c, d_norm1):
+        cols = pl.ds(pl.multiple_of(c * WIDE, WIDE), WIDE)
+        slabs = pl.ds(c * (UNITS * WIDE // FF), UNITS * WIDE // FF)
+        d_active = outer_cols(d_down, w2_ref[cols, :])
+        d_up = (d_active * slope_ref[:, cols]).astype(jnp.bfloat16)
+        d_ffn_ref[:, cols] = add_rows(d_up.astype(jnp.float32))
+        dw2 = inner_rows(active_ref[:, cols], d_down)
+        dw2_ref[slabs] = dw2.reshape(UNITS * WIDE // FF, FF // UNITS, D).astype(jnp.bfloat16)
+        dw1 = inner_rows(lowered, d_up)
+        dw1_ref[:, :, cols] = dw1.reshape(UNITS, D // UNITS, WIDE).astype(jnp.bfloat16)
+        for cp in stores(c):
+            cp.start()
+        return d_norm1 + outer_cols(d_up, w1_ref[:, cols])
+
+    d_norm1 = lax.fori_loop(0, FF // WIDE, back_step, d_sum2)
+    small_ref[1:2] = add_rows(d_norm1)
+    small_ref[4:5] = add_rows(d_norm1 * normed1)
+    d_sum1 = normalize_back(d_norm1, normed1, inverse1, vec_ref[6:7])
+    d_sum1_ref[...] = d_sum1
+    d_attn = d_sum1.astype(jnp.bfloat16)
+    small_ref[0:1] = add_rows(d_attn.astype(jnp.float32))
+    d_mixed = outer_cols(d_attn, wo_ref[...])
+    for h in range(0, H, 2):
+        for t in range(BPD // 2):
+            part = slice(t * BLOCK, (t + 1) * BLOCK)
+            lanes = slice(h * HD, (h + 2) * HD)
+            a, b = unpack_pair(
+                d_mixed[2 * t * BLOCK : (2 * t + 1) * BLOCK, lanes],
+                d_mixed[(2 * t + 1) * BLOCK : (2 * t + 2) * BLOCK, lanes],
+                (BLOCK, 128),
+            )
+            box[h, part, :] = a.astype(jnp.bfloat16)
+            box[h + 1, part, :] = b.astype(jnp.bfloat16)
+
+    def late():
+        dwo_ref[...] = (
+            inner_rows(mixed_ref[...], d_attn)
+            .reshape(UNITS, D // UNITS, D)
+            .astype(jnp.bfloat16)
+        )
+        cp = pltpu.make_async_copy(dwo_ref, dwo_hbm, load_sem.at[0])
+        cp.start()
+        cp.wait()
+
+    send_to_owners(n, place, head, mine, ((box, d_heads),), sems_out, late)
+
+    def drain(c, _):
+        for cp in stores(c):
+            cp.wait()
+        return 0
+
+    lax.fori_loop(0, FF // WIDE, drain, 0)
+
+
+def middle(attended, rows, cotangent, first, second, vectors, ffn_bias):
+    n = lax.axis_size("seq")
+    low, full = jnp.bfloat16, jnp.float32
+    part = (TOK_SEQ // 2, 128)
+    units = [(UNITS, D // UNITS, FF), (UNITS, FF // UNITS, D), (UNITS, D // UNITS, D)]
+    shapes = [((TOK_SEQ, D), full), ((TOK_SEQ, D), full), ((n,) + part, low)]
+    shapes += [(u, low) for u in units] + [((8, D), full), ((1, FF), full)]
+    return pl.pallas_call(
+        functools.partial(mid_kernel, n),
+        out_shape=[jax.ShapeDtypeStruct(s, d) for s, d in shapes],
+        in_specs=[ANY, VMEM, VMEM, ANY, ANY, VMEM, VMEM],
+        out_specs=[VMEM, VMEM, ANY, ANY, ANY, ANY, VMEM, VMEM],
+        scratch_shapes=[
+            pltpu.VMEM((H,) + part, low),
+            pltpu.VMEM((H,) + part, low),
+            pltpu.VMEM((D, FF), low),
+            pltpu.VMEM((D, D), low),
+            pltpu.VMEM((FF, D), low),
+            pltpu.VMEM((TOK_SEQ, FF), full),
+            pltpu.VMEM((TOK_SEQ, FF), low),
+            *[pltpu.VMEM(u, low) for u in units],
+            pltpu.VMEM((TOK_SEQ, D), low),
+            pltpu.SemaphoreType.DMA((3,)),
+            pltpu.SemaphoreType.DMA((2, FF // WIDE)),
+            *exchange_sems(n),
+            *exchange_sems(n),
+        ],
+        compiler_params=pltpu.CompilerParams(
+            collective_id=3, has_side_effects=True, vmem_limit_bytes=58 << 20
+        ),
+        name="middle",
+    )(attended, rows, cotangent, first, second, vectors, ffn_bias)
 
 
 def unpack_heads(parts):
@@ -977,94 +1170,6 @@
 def unpack_keys(parts):
     parts = parts.reshape(H, TOK_SEQ, 2, HD).transpose(2, 1, 0, 3)
     return parts.reshape(2, TOK_SEQ, D)
-
-
-def layer_forward(tokens, picks, weights):
-    qkv, out_w, expand, contract, biases, gains, ffn_bias = weights
-    rows = tokens.reshape(SEQ_GRP * TOK_SEQ, D)
-    kvq, picks = project_and_send(rows, qkv, biases, picks)
-    attended, lse = attend_heads(kvq, picks)
-    mixed = unpack_heads(exchange(from_owners_kernel, H, attended, 3, "return_heads"))
-    hidden1 = rows.astype(jnp.float32) + matmul(mixed, out_w) + biases[2]
-    normed_out1, normed1, inverse1 = normalize(hidden1, gains[0], biases[3])
-    lowered = normed_out1.astype(jnp.bfloat16)
-    up = matmul(lowered, expand) + ffn_bias
-    active = gelu_tanh(up).astype(jnp.bfloat16)
-    hidden2 = normed_out1 + matmul(active, contract) + biases[4]
-    result, normed2, inverse2 = normalize(hidden2, gains[1], biases[5])
-    saved = (
-        kvq,
-        picks,
-        lse,
-        mixed,
-        normed1,
-        inverse1,
-        lowered,
-        up,
-        active,
-        normed2,
-        inverse2,
-    )
-    return (result, saved)
-
-
-def layer_backward(tokens, cotangent, weights, saved, planes):
-    qkv, out_w, expand, contract, biases, gains, ffn_bias = weights
-    (
-        kvq,
-        picks,
-        lse,
-        mixed,
-        normed1,
-        inverse1,
-        lowered,
-        up,
-        active,
-        normed2,
-        inverse2,
-    ) = saved
-    rows = tokens.reshape(SEQ_GRP * TOK_SEQ, D)
-    grad = cotangent.reshape(SEQ_GRP * TOK_SEQ, D).astype(jnp.float32)
-    d_gain2 = jnp.sum(grad * normed2, axis=0)
-    d_shift2 = jnp.sum(grad, axis=0)
-    d_sum2 = normalize_back(grad, normed2, inverse2, gains[1])
-    d_down = d_sum2.astype(jnp.bfloat16)
-    d_bias2 = jnp.sum(d_down.astype(jnp.float32), axis=0)
-    d_contract = inner_rows(active, d_down)
-    d_active = outer_cols(d_down, contract)
-    gelu_value, gelu_pull = jax.vjp(gelu_tanh, up)
-    d_up = gelu_pull(d_active)[0].astype(jnp.bfloat16)
-    d_ffn_bias = jnp.sum(d_up.astype(jnp.float32), axis=0)
-    d_expand = inner_rows(lowered, d_up)
-    d_norm1 = d_sum2 + outer_cols(d_up, expand)
-    d_gain1 = jnp.sum(d_norm1 * normed1, axis=0)
-    d_shift1 = jnp.sum(d_norm1, axis=0)
-    d_sum1 = normalize_back(d_norm1, normed1, inverse1, gains[0])
-    d_attn = d_sum1.astype(jnp.bfloat16)
-    d_bias_out = jnp.sum(d_attn.astype(jnp.float32), axis=0)
-    d_out_w = inner_rows(mixed, d_attn)
-    d_mixed = outer_cols(d_attn, out_w).astype(jnp.bfloat16)
-    d_heads = exchange(
-        to_owners_kernel, lax.axis_size("seq"), pack_heads(d_mixed), 4, "send_head_grads"
-    )
-    d_heads = exchange(
-        from_owners_kernel, H, attend_heads_back(kvq, picks, lse, d_heads), 5, "return_head_grads"
-    )
-    d_query = unpack_heads(d_heads[:, TOK_SEQ:])
-    d_pair = unpack_keys(d_heads[:, :TOK_SEQ])
-    d_proj = jnp.concatenate([d_query[None], d_pair], axis=0)
-    d_qkv = jnp.einsum("rd,erf->edf", rows, d_proj, preferred_element_type=jnp.float32).reshape(3 * D, D)
-    d_tokens = d_sum1 + jnp.einsum("erf,edf->rd", d_proj, qkv, preferred_element_type=jnp.float32)
-    d_bias_q = jnp.sum(d_query.astype(jnp.float32), axis=0)
-    d_bias_v = jnp.sum(d_pair[1].astype(jnp.float32), axis=0)
-    d_biases = jnp.stack([d_bias_q, d_bias_v, d_bias_out, d_shift1, d_bias2, d_shift2]).reshape(
-        6 * D
-    )
-    d_gains = jnp.stack([d_gain1, d_gain2]).reshape(2 * D)
-    shares = scatter_grads(
-        (d_qkv, d_out_w, d_expand, d_contract, d_biases, d_gains, d_ffn_bias), planes
-    )
-    return (d_tokens, shares)
 
 
 def on_device(
@@ -1079,23 +1184,32 @@
     random_blocks,
     cotangent,
 ):
-    weights = gather_weights(
+    qkv, first, second, vectors, ffn = gather_weights(
         qkv_weight, out_weight, expand_weight, contract_weight, bias_vectors, gain_vectors, ffn_bias
     )
-    result, saved = layer_forward(tokens, random_blocks, weights)
     planes = kernel_planes((qkv_weight, out_weight, expand_weight, contract_weight))
-    d_tokens, shares = layer_backward(tokens, cotangent, weights, saved, planes)
-    return (
-        result.reshape(SEQ_GRP, TOK_SEQ, D),
-        d_tokens.reshape(SEQ_GRP, TOK_SEQ, D),
-        shares[0],
-        shares[1],
-        shares[2],
-        shares[3],
-        shares[4],
-        shares[5],
-        shares[6],
+    rows = tokens.reshape(TOK_SEQ, D)
+    kvq, picks = project_and_send(rows, qkv, vectors, random_blocks)
+    attended, lse = attend_heads(kvq, picks)
+    result, d_sum1, d_heads, d_expand, d_contract, d_out, small, d_ffn = middle(
+        attended, rows, cotangent.reshape(TOK_SEQ, D), first, second, vectors, ffn
     )
+    d_heads = exchange(
+        from_owners_kernel, H, attend_heads_back(kvq, picks, lse, d_heads), 5, "return_head_grads"
+    )
+    d_query = unpack_heads(d_heads[:, TOK_SEQ:])
+    d_pair = unpack_keys(d_heads[:, :TOK_SEQ])
+    d_proj = jnp.concatenate([d_query[None], d_pair], axis=0)
+    d_qkv = jnp.einsum("rd,erf->edf", rows, d_proj, preferred_element_type=jnp.float32)
+    d_tokens = d_sum1 + jnp.einsum("erf,edf->rd", d_proj, qkv, preferred_element_type=jnp.float32)
+    d_bias_q = jnp.sum(d_query.astype(jnp.float32), axis=0)
+    d_bias_v = jnp.sum(d_pair[1].astype(jnp.float32), axis=0)
+    d_biases = jnp.concatenate([jnp.stack([d_bias_q, d_bias_v]), small[0:4]])
+    shares = scatter_grads(
+        (d_qkv.reshape(3 * D, D), d_out, d_expand, d_contract, d_biases, small[4:6], d_ffn),
+        planes,
+    )
+    return (result[None], d_tokens[None]) + shares
 
 
 def solution(mesh):

time: 407 us -> 351 us (0.86); the launches traced: 401 us -> 350 us
  matrix products: 34.5 us -> 6.46 us
  local copies, waits for them, and re-layouts: 51.9 us -> 24.2 us
  Pallas kernels: 301 us -> 313 us
  other arithmetic: 11.6 us -> 5.55 us
    pallas_call x0 -> x1, Pallas kernels: none -> 43.3 us  [middle(): pl.pallas_call(functools.partial(mid_kernel, n), out_shape=[jax.ShapeDtyp...]
    pallas_call x3 -> x1, Pallas kernels: 70.1 us -> 39.6 us  [exchange(): pl.pallas_call(functools.partial(kernel, n), out_shape=jax.ShapeDtypeStru...]
    dot_general x11 -> x2, matrix products: 34.5 us -> 6.46 us  [the longest x1 3.56 us: on_device(): jnp.einsum('erf,edf->rd', d_proj, qkv, preferred_element_type=jnp.float32)]
    reshape x4 -> x2, local copies, waits for them, and re-layouts: 10.7 us -> 1.06 us  [unpack_heads(): parts = parts.reshape(H, BPD // 2, BLOCK, 2, HD).transpose(1, 3, 2, 0, 4)]
    another operation x13 -> x4, local copies, waits for them, and re-layouts: 8.01 us -> 0.8 us  [the longest x2 0.65 us: on_device(): d_proj = jnp.concatenate([d_query[None], d_pair], axis=0)]
    reduce_sum x8 -> x2, other arithmetic: 9.04 us -> 2.35 us  [the longest x1 2.17 us: on_device(): d_bias_q = jnp.sum(d_query.astype(jnp.float32), axis=0)]
where the time goes in v3:
time: 351 us; the launch traced here: 350 us
  Pallas kernels  313 us (89%)
  local copies, waits for them, and re-layouts  24.2 us (7%)
  matrix products  6.46 us (2%)
  other arithmetic  5.55 us (2%)
    pallas_call x1, Pallas kernels, scatter_all(): pl.pallas_call(functools.partial(scatter_kernel, nz, k), out_shape=[jax.S...  87.3 us
    pallas_call x1, Pallas kernels, gather_all(): pl.pallas_call(functools.partial(gather_kernel, nz), out_shape=[jax.Shape...  62.1 us
    pallas_call x1, Pallas kernels, middle(): pl.pallas_call(functools.partial(mid_kernel, n), out_shape=[jax.ShapeDtyp...  43.3 us
    pallas_call x1, Pallas kernels, exchange(): pl.pallas_call(functools.partial(kernel, n), out_shape=jax.ShapeDtypeStru...  39.6 us
    pallas_call x1, Pallas kernels, project_and_send(): pl.pallas_call(functools.partial(project_kernel, n), out_shape=(jax.Shape...  33.4 us
    pallas_call x1, Pallas kernels, attend_heads_back(): pl.pallas_call(functools.partial(attend_back_kernel, n), out_shape=jax.Sh...  25.3 us
    pallas_call x1, Pallas kernels, attend_heads(): pl.pallas_call(functools.partial(attend_kernel, n), out_shape=(jax.ShapeD...  21.9 us

profile of v3, /device:TPU:8, one launch (start us, length us, event | category | flops | bytes accessed | tf_op | source)
XLA Modules:
  0.0 350.2 jit_solution(17612133031468696826)
XLA Ops:
  0.6 1.0 reshape.111
  1.6 0.9 reshape.112
  2.5 0.8 fusion.9
  3.3 0.7 pad_maximum_fusion.3.refs_0_
  4.0 1.7 reshape.114.refs_1_
  5.7 1.7 reshape.115.refs_2_
  7.4 62.1 %gather_weights.1 = (bf16[32,24,3968]{2,1,0:T(8,128)(2,1)}, bf16[32,96,768]{2,1,0:T(8,128)(2,1)}, bf16[32,72,768]{2,1,0:T(8,128)(2,1)}) custom-call(bf16[24,3968]{1,0:T(8,128)(2,1)} %pad_maximum_fusion.3.refs_0_, bf16[96,768]{1,0:T(8,128)(2,1)} %reshape.114.refs_1_, bf16[72,768]{1,0:T(8,128)(2,1)} %reshape.115.refs_2_), custom_call_target="tpu_custom_call" | custom-call | tf_op jit(solution)/shard_map/gather_weights/pallas_call | solution.py:174
  69.4 1.0 slice_convert_fusion
  70.9 2.0 copy-done.3
  72.9 33.4 %project_and_send.1 = (bf16[16,384,128]{2,1,0:T(8,128)(2,1)S(1)}, s32[16,8,128]{2,1,0:T(8,128)S(1)}) custom-call(bf16[256,768]{1,0:T(8,128)(2,1)S(1)} %bitcast.39, bf16[3,768,768]{2,1,0:T(8,128)(2,1)S(1)} %bitcast.40, f32[8,768]{1,0:T(8,128)S(1)} %pad_maximum_fusion.4.bias_ref.refs_5_, s32[12,8,128]{2,1,0:T(8,128)S(1)} %pad.13.picks_ref), custom_call_target="tpu_custom_call" | custom-call | tf_op jit(solution)/shard_map/project_and_send/pallas_call | solution.py:738
  106.3 21.9 %attend_heads.1 = (bf16[16,128,128]{2,1,0:T(8,128)(2,1)S(1)}, f32[32,1,128]{2,1,0:T(1,128)S(1)}) custom-call(bf16[16,384,128]{2,1,0:T(8,128)(2,1)S(1)} %get-tuple-element.31.kvq_ref, s32[16,8,128]{2,1,0:T(8,128)S(1)} %get-tuple-element.32.picks_ref), custom_call_target="tpu_custom_call" | custom-call | tf_op jit(solution)/shard_map/attend_heads/pallas_call | solution.py:865
  128.3 0.8 copy-done.5
  129.1 0.7 reshape.123.refs_6_
  129.8 43.3 %middle.1 = (f32[256,768]{1,0:T(8,128)}, f32[256,768]{1,0:T(8,128)}, bf16[16,128,128]{2,1,0:T(8,128)(2,1)}, bf16[32,24,3072]{2,1,0:T(8,128)(2,1)}, bf16[32,96,76...) custom-call(bf16[16,128,128]{2,1,0:T(8,128)(2,1)} %copy-done.5, ...), custom_call_target="tpu_custom_call" | custom-call | tf_op jit(solution)/shard_map/middle/pallas_call | solution.py:1138
  173.1 25.3 %attend_heads_back.1.src = bf16[16,384,128]{2,1,0:T(8,128)(2,1)} custom-call(bf16[16,384,128]{2,1,0:T(8,128)(2,1)} %copy-done, s32[16,8,128]{2,1,0:T(8,128)} %copy-done.6, f32[32,1,128]{2,1,0:T(1,128)} %copy-done.8, bf16[16,128,128]{2,1,0:T(8,128)(2,1)} %get-tuple-element.38.grad_ref), custom_call_target="tpu_custom_call" | custom-call | tf_op jit(solution)/shard_map/attend_heads_back/pallas_call | solution.py:940
  198.5 39.6 %return_head_grads.1 = bf16[12,384,128]{2,1,0:T(8,128)(2,1)} custom-call(bf16[16,384,128]{2,1,0:T(8,128)(2,1)} %attend_heads_back.1.src), custom_call_target="tpu_custom_call" | custom-call | tf_op jit(solution)/shard_map/return_head_grads/pallas_call | solution.py:763
  238.1 1.1 slice-done
  239.9 0.7 slice-done.1
  240.9 0.7 copy.24
  242.4 2.9 convolution_convert_fusion
  245.3 2.2 convert_reduce_fusion
  248.5 0.7 reduce.5
  249.3 0.7 copy.29
  250.0 87.3 %scatter_grads.1 = (f32[8,128]{1,0:T(8,128)}, f32[24,3072]{1,0:T(8,128)}, f32[96,768]{1,0:T(8,128)}, f32[72,768]{1,0:T(8,128)}, f32[24,768]{1,0:T(8,128)}) custom-call(f32[32,8,128]{2,1,0:T(8,128)} %bitcast.51, bf16[32,24,3072]{2,1,0:T(8,128)(2,1)} %get-tuple-element.41.refs_1_, bf16[32,96,768]{2,1,0:T(8,128)(2,1)} %get-tuple-element.42.refs_2_, ...), custom_call_target="tpu_custom_call" | custom-call | tf_op jit(solution)/shard_map/scatter_grads/pallas_call | solution.py:451
  337.4 1.7 copy.30
  339.1 1.7 reshape.134
  340.8 1.6 reshape.131
  342.5 1.5 reshape.132
  344.5 0.6 slice.51
  345.1 0.6 slice.52
  345.7 3.6 %fusion.1 = f32[1,256,768]{2,1,0:T(8,128)} fusion(f32[256,768]{1,0:T(8,128)} %get-tuple-element.36, bf16[3,768,768]{2,1,0:T(8,128)(2,1)S(1)} %bitcast.41, bf16[2,256,768]{2,1,0:T(8,128)(2,1)} %copy-done.9, bf16[1,256,768]{2,1,0:T(8,128)(2,1)} %copy-done.10), kind=kOutput, calls=%fused_computation.4 | convolution fusion | flops 906756096 | bytes 6291456 | tf_op jit(solution)/shard_map/erf,edf->rd/dot_general | solution.py:1204
  349.3 0.9 copy.32
  (60 shorter events, 3.9 us)
Async XLA Ops:
  1.6 69.1 %copy-start.14 = (s32[1,12,4,3]{1,2,3,0:T(4,128)S(1)}, s32[1,12,4,3]{1,2,3,0:T(4,128)}, u32[]{:S(2)}) copy-start(s32[1,12,4,3]{1,2,3,0:T(4,128)} %param.18) | copy-start | bytes 1732
  1.6 69.2 %copy-start.1 = (bf16[1,256,768]{2,1,0:T(8,128)(2,1)S(1)}, bf16[1,256,768]{2,1,0:T(8,128)(2,1)}, u32[]{:S(2)}) copy-start(bf16[1,256,768]{2,1,0:T(8,128)(2,1)} %param.10) | copy-start | bytes 1179652
  70.7 35.6 %copy-start.7 = (f32[8,768]{1,0:T(8,128)}, f32[8,768]{1,0:T(8,128)S(1)}, u32[]{:S(2)}) copy-start(f32[8,768]{1,0:T(8,128)S(1)} %pad_maximum_fusion.4.bias_ref.refs_5_) | copy-start | bytes 73732
  70.9 2.0 copy-start.3
  106.3 66.8 %copy-start = (bf16[16,384,128]{2,1,0:T(8,128)(2,1)}, bf16[16,384,128]{2,1,0:T(8,128)(2,1)S(1)}, u32[]{:S(2)}) copy-start(bf16[16,384,128]{2,1,0:T(8,128)(2,1)S(1)} %get-tuple-element.31.kvq_ref) | copy-start | bytes 4718596
  106.3 66.8 %copy-start.6 = (s32[16,8,128]{2,1,0:T(8,128)}, s32[16,8,128]{2,1,0:T(8,128)S(1)}, u32[]{:S(2)}) copy-start(s32[16,8,128]{2,1,0:T(8,128)S(1)} %get-tuple-element.32.picks_ref) | copy-start | bytes 196612
  128.2 0.8 copy-start.5
  129.0 44.1 %copy-start.8 = (f32[32,1,128]{2,1,0:T(1,128)}, f32[32,1,128]{2,1,0:T(1,128)S(1)}, u32[]{:S(2)}) copy-start(f32[32,1,128]{2,1,0:T(1,128)S(1)} %get-tuple-element.37.lse_ref) | copy-start | bytes 49156
  238.1 1.1 slice-start
  239.6 1.0 slice-start.1
  239.8 2.5 copy-start.9
  240.9 1.4 copy-start.2
  242.3 2.9 copy-start.10
  242.3 5.4 %copy-start.12 = (f32[8,768]{1,0:T(8,128)S(1)}, f32[8,768]{1,0:T(8,128)}, u32[]{:S(2)}) copy-start(f32[8,768]{1,0:T(8,128)} %get-tuple-element.39) | copy-start | bytes 73732
  242.3 6.2 %copy-start.13 = (f32[1,3072]{1,0:T(1,128)S(1)}, f32[1,3072]{1,0:T(1,128)}, u32[]{:S(2)}) copy-start(f32[1,3072]{1,0:T(1,128)} %get-tuple-element.40) | copy-start | bytes 36868
  250.0 95.7 %copy-start.4 = (bf16[32,72,768]{2,1,0:T(8,128)(2,1)S(1)}, bf16[32,72,768]{2,1,0:T(8,128)(2,1)}, u32[]{:S(2)}) copy-start(bf16[32,72,768]{2,1,0:T(8,128)(2,1)} %get-tuple-element.29) | copy-start | bytes 10616836
  337.4 6.6 %copy-start.15 = (f32[8,128]{1,0:T(8,128)S(1)}, f32[8,128]{1,0:T(8,128)}, u32[]{:S(2)}) copy-start(f32[8,128]{1,0:T(8,128)} %get-tuple-element.48) | copy-start | bytes 12292
  345.7 3.6 %copy-start.11 = (f32[256,768]{1,0:T(8,128)S(1)}, f32[256,768]{1,0:T(8,128)}, u32[]{:S(2)}) copy-start(f32[256,768]{1,0:T(8,128)} %get-tuple-element.35) | copy-start | bytes 2359300

commit v4 on v3

--- a/solution.py
+++ b/solution.py
@@ -183,9 +183,6 @@
     )(*xs)
 
 
-CHAIN_FIRST = (False, False, False, True, False)
-LINKS = (("x", "y"), ("x", "y"), ("y", "x"), ("x", "y"), ("x", "y"))
-
 def combine(dst, srcs):
     rows, cols = dst.shape
     step = min(cols, max(128, (24 * 1024 // rows) // 128 * 128))
@@ -204,267 +201,13 @@
             return 0
         lax.fori_loop(0, cols // step, body, 0)
 
-def scatter_kernel(nz, k, *refs):
-    xs, outs = refs[:k], refs[k:2 * k]
-    scr = refs[2 * k:]
-    acc, rc, ra, rb, below, above = (scr[i * k:(i + 1) * k] for i in range(6))
-    csend, crecv, send_sem, recv_sem = scr[6 * k:]
-    me = place(nz)
-    mz = me["z"]
-    sib = dict(me, c=1 - me["c"])
-    bar = pltpu.get_barrier_semaphore()
-    for d in ("x", "y", "c"):
-        pl.semaphore_signal(bar, inc=1, device_id=device(dict(me, **{d: 1 - me[d]})), device_id_type=MESH)
-    @pl.when(mz > 0)
-    def _():
-        pl.semaphore_signal(bar, inc=1, device_id=device(dict(me, z=mz - 1)), device_id_type=MESH)
-    @pl.when(mz < nz - 1)
-    def _():
-        pl.semaphore_signal(bar, inc=1, device_id=device(dict(me, z=mz + 1)), device_id_type=MESH)
-    pl.semaphore_wait(bar, 3 + jnp.where(mz > 0, 1, 0) + jnp.where(mz < nz - 1, 1, 0))
-
-    pending = []
-    up_to = dict(me, z=jnp.minimum(mz + 1, nz - 1))
-    dn_to = dict(me, z=jnp.maximum(mz - 1, 0))
-
-    def copy(item, src, dst, ss, rs, to):
-        return pltpu.make_async_remote_copy(src_ref=src, dst_ref=dst, send_sem=ss, recv_sem=rs, device_id=device(to), device_id_type=MESH)
-
-    def start(cp, cond=None):
-        if cond is None:
-            cp.start()
-        else:
-            pl.when(cond)(cp.start)
-        pending.append((cp, cond))
-
-    def arrived(item, ref, sem):
-        copy(item, ref, ref, send_sem.at[item, 0], sem, sib).wait_recv()
-
-    def piece(z, x, y):
-        return (y * nz + z) * 2 + x
-
-    def coords(a, b, item):
-        la, lb = LINKS[item]
-        return {la: a, lb: b}
-
-    def wanted(item):
-        la, lb = LINKS[item]
-        out = []
-        zs = [0, nz - 1, 1, nz - 2][:nz] if nz == 4 else list(range(nz))
-        if CHAIN_FIRST[item]:
-            for z in zs:
-                for fa in (1, 0):
-                    for fb in (1, 0):
-                        out.append((z, fa, fb))
-        else:
-            for fb in (1, 0):
-                for fa in (1, 0):
-                    for z in zs:
-                        out.append((z, fa, fb))
-        return out
-
-    def flip(d, f):
-        return 1 - me[d] if f else me[d]
-
-    order_items = (1, 2, 3, 4, 0)
-    lists = {i: wanted(i) for i in range(k)}
-    for n in range(4 * nz):
-        for item in order_items:
-            z, fa, fb = lists[item][n]
-            la, lb = LINKS[item]
-            p = piece(z, **{la: flip(la, fa), lb: flip(lb, fb)})
-            start(copy(item, xs[item].at[p * 2 + 1 - me["c"]], rc[item].at[p], csend.at[item, p], crecv.at[item, p], sib))
-
-    steps = []
-    def tail(item):
-        la, lb = LINKS[item]
-        def own(p):
-            arrived(item, rc[item].at[p], crecv.at[item, p])
-            return [xs[item].at[p * 2 + me["c"]], rc[item].at[p]]
-        zs = [nz - 1, 0, nz - 2, 1] if nz == 4 else list(reversed(range(nz)))
-        if not CHAIN_FIRST[item]:
-            def stage_b(z, fa):
-                def run():
-                    a = flip(la, fa)
-                    p = piece(z, **{la: a, lb: 1 - me[lb]})
-                    combine(acc[item].at[p], own(p))
-                    s = z * 2 + a
-                    start(copy(item, acc[item].at[p], rb[item].at[s], send_sem.at[item, s], recv_sem.at[item, s], dict(me, **{lb: 1 - me[lb]})))
-                return run
-            def stage_a(z):
-                def run():
-                    a = 1 - me[la]
-                    p = piece(z, **{la: a, lb: me[lb]})
-                    s = z * 2 + a
-                    srcs = own(p)
-                    arrived(item, rb[item].at[s], recv_sem.at[item, s])
-                    combine(acc[item].at[p], srcs + [rb[item].at[s]])
-                    s2 = 2 * nz + z
-                    start(copy(item, acc[item].at[p], ra[item].at[z], send_sem.at[item, s2], recv_sem.at[item, s2], dict(me, **{la: 1 - me[la]})))
-                return run
-            def base(z):
-                p = piece(z, **{la: me[la], lb: me[lb]})
-                s = z * 2 + me[la]
-                srcs = own(p)
-                arrived(item, rb[item].at[s], recv_sem.at[item, s])
-                arrived(item, ra[item].at[z], recv_sem.at[item, 2 * nz + z])
-                return p, srcs + [rb[item].at[s], ra[item].at[z]]
-            def chain(z):
-                def run():
-                    p, srcs = base(z)
-                    sb, sa = 3 * nz + z, 4 * nz + z
-                    @pl.when(jnp.logical_and(mz == 0, z > 0))
-                    def _():
-                        combine(acc[item].at[p], srcs)
-                    @pl.when(jnp.logical_and(mz > 0, mz < z))
-                    def _():
-                        arrived(item, below[item].at[z], recv_sem.at[item, sb])
-                        combine(acc[item].at[p], srcs + [below[item].at[z]])
-                    if z > 0:
-                        start(copy(item, acc[item].at[p], below[item].at[z], send_sem.at[item, sb], recv_sem.at[item, sb], up_to), mz < z)
-                    @pl.when(jnp.logical_and(mz == nz - 1, z < nz - 1))
-                    def _():
-                        combine(acc[item].at[p], srcs)
-                    @pl.when(jnp.logical_and(mz < nz - 1, mz > z))
-                    def _():
-                        arrived(item, above[item].at[z], recv_sem.at[item, sa])
-                        combine(acc[item].at[p], srcs + [above[item].at[z]])
-                    if z < nz - 1:
-                        start(copy(item, acc[item].at[p], above[item].at[z], send_sem.at[item, sa], recv_sem.at[item, sa], dn_to), mz > z)
-                return run
-            def last():
-                for z in range(nz):
-                    @pl.when(mz == z)
-                    def _():
-                        p, srcs = piece(z, **{la: me[la], lb: me[lb]}), None
-                        s = z * 2 + me[la]
-                        srcs = [xs[item].at[p * 2 + me["c"]], rc[item].at[p], rb[item].at[s], ra[item].at[z]]
-                        if z > 0:
-                            arrived(item, below[item].at[z], recv_sem.at[item, 3 * nz + z])
-                            srcs.append(below[item].at[z])
-                        if z < nz - 1:
-                            arrived(item, above[item].at[z], recv_sem.at[item, 4 * nz + z])
-                            srcs.append(above[item].at[z])
-                        combine(outs[item], srcs)
-            out = []
-            for n, z in enumerate(zs):
-                out.append((1 + n, stage_b(z, 1)))
-            for n, z in enumerate(zs):
-                out.append((5 + n, stage_b(z, 0)))
-                out.append((5.5 + n, stage_a(z)))
-            for n, z in enumerate(zs):
-                out.append((9.5 + n, chain(z)))
-            out.append((20, last))
-            return out
-        def chain(z, fa, fb):
-            def run():
-                a, b = flip(la, fa), flip(lb, fb)
-                p = piece(z, **{la: a, lb: b})
-                q = a * 2 + b
-                srcs = own(p)
-                sb, sa = z * 4 + q, 4 * nz + z * 4 + q
-                bref, aref = below[item].at[z * 4 + q], above[item].at[z * 4 + q]
-                if z > 0:
-                    @pl.when(mz == 0)
-                    def _():
-                        combine(acc[item].at[p], srcs)
-                    @pl.when(jnp.logical_and(mz > 0, mz < z))
-                    def _():
-                        arrived(item, bref, recv_sem.at[item, sb])
-                        combine(acc[item].at[p], srcs + [bref])
-                    start(copy(item, acc[item].at[p], bref, send_sem.at[item, sb], recv_sem.at[item, sb], up_to), mz < z)
-                if z < nz - 1:
-                    @pl.when(mz == nz - 1)
-                    def _():
-                        combine(acc[item].at[p], srcs)
-                    @pl.when(jnp.logical_and(mz < nz - 1, mz > z))
-                    def _():
-                        arrived(item, aref, recv_sem.at[item, sa])
-                        combine(acc[item].at[p], srcs + [aref])
-                    start(copy(item, acc[item].at[p], aref, send_sem.at[item, sa], recv_sem.at[item, sa], dn_to), mz > z)
-            return run
-        def settle(fa, fb):
-            a, b = flip(la, fa), flip(lb, fb)
-            q = a * 2 + b
-            for z in range(nz):
-                @pl.when(mz == z)
-                def _():
-                    p = piece(z, **{la: a, lb: b})
-                    srcs = [xs[item].at[p * 2 + me["c"]], rc[item].at[p]]
-                    if z > 0:
-                        arrived(item, below[item].at[z * 4 + q], recv_sem.at[item, z * 4 + q])
-                        srcs.append(below[item].at[z * 4 + q])
-                    if z < nz - 1:
-                        arrived(item, above[item].at[z * 4 + q], recv_sem.at[item, 4 * nz + z * 4 + q])
-                        srcs.append(above[item].at[z * 4 + q])
-                    combine(acc[item].at[p], srcs)
-            return piece(mz, **{la: a, lb: b})
-        s0 = 8 * nz
-        def to_b(fa):
-            def run():
-                p = settle(fa, 1)
-                start(copy(item, acc[item].at[p], rb[item].at[fa], send_sem.at[item, s0 + fa], recv_sem.at[item, s0 + fa], dict(me, **{lb: 1 - me[lb]})))
-            return run
-        def to_a():
-            p = settle(1, 0)
-            arrived(item, rb[item].at[1], recv_sem.at[item, s0 + 1])
-            combine(ra[item].at[0], [acc[item].at[p], rb[item].at[1]])
-            start(copy(item, ra[item].at[0], ra[item].at[1], send_sem.at[item, s0 + 2], recv_sem.at[item, s0 + 2], dict(me, **{la: 1 - me[la]})))
-        def last():
-            p = settle(0, 0)
-            arrived(item, rb[item].at[0], recv_sem.at[item, s0])
-            arrived(item, ra[item].at[1], recv_sem.at[item, s0 + 2])
-            combine(outs[item], [acc[item].at[p], rb[item].at[0], ra[item].at[1]])
-        out = []
-        for n, z in enumerate(zs):
-            for m, (fa, fb) in enumerate(((1, 1), (0, 1), (1, 0), (0, 0))):
-                out.append((1 + n * 3 + m * 0.5, chain(z, fa, fb)))
-        out.append((12.6, to_b(1)))
-        out.append((12.7, to_b(0)))
-        out.append((14, to_a))
-        out.append((21, last))
-        return out
-
-    for n, item in enumerate(order_items):
-        steps += [(w + 0.01 * n, f) for w, f in tail(item)]
-    for _, f in sorted(steps, key=lambda s: s[0]):
-        f()
-    for cp, cond in pending:
-        if cond is None:
-            cp.wait_send()
-        else:
-            pl.when(cond)(cp.wait_send)
-
-def scatter_all(xs, nz):
-    k = len(xs)
-    chips = 4 * nz
-    slab = [x.shape[1:] for x in xs]
-    dt = [x.dtype for x in xs]
-    def buf(counts):
-        return [pltpu.VMEM((n,) + s, d) for n, s, d in zip(counts, slab, dt)]
-    scr = buf([chips] * k) + buf([chips] * k)
-    scr += buf([2 if CHAIN_FIRST[i] else nz for i in range(k)])
-    scr += buf([2 if CHAIN_FIRST[i] else 2 * nz for i in range(k)])
-    scr += buf([4 * nz if CHAIN_FIRST[i] else nz for i in range(k)]) * 2
-    sems = 8 * nz + 3
-    scr += [pltpu.SemaphoreType.DMA((k, chips)), pltpu.SemaphoreType.DMA((k, chips)), pltpu.SemaphoreType.DMA((k, sems)), pltpu.SemaphoreType.DMA((k, sems))]
-    return pl.pallas_call(
-        functools.partial(scatter_kernel, nz, k),
-        out_shape=[jax.ShapeDtypeStruct(s, jnp.float32) for s in slab],
-        in_specs=[pl.BlockSpec(memory_space=pltpu.VMEM)] * k,
-        out_specs=[pl.BlockSpec(memory_space=pltpu.VMEM)] * k,
-        scratch_shapes=scr,
-        compiler_params=pltpu.CompilerParams(collective_id=1, has_side_effects=True, vmem_limit_bytes=60 << 20),
-        name="scatter_grads",
-    )(*xs)
-
-
 def kernel_planes(arrays):
     seq = lax.axis_size("seq")
-    if lax.axis_size("dp") != 2 or seq % 4 or seq > 16:
+    if lax.axis_size("dp") != 2 or seq % 4:
         return 0
-    rows = [a.size % c for a, c in zip(arrays, (D, D, FF, D))]
-    return 0 if any(rows) else seq // 4
+    if seq // 4 not in (2, 4) or 2 * seq != UNITS:
+        return 0
+    return seq // 4
 
 
 def gather_weights(
@@ -506,38 +249,6 @@
     )
 
 
-def scatter_grads(grads, planes):
-    d_qkv, d_out, d_expand, d_contract, d_biases, d_gains, d_ffn_bias = grads
-    shards = lax.axis_size("dp") * lax.axis_size("seq")
-    vectors = jnp.concatenate(
-        [v.reshape(shards, -1) for v in (d_biases, d_gains, d_ffn_bias)], axis=1
-    )
-    if planes:
-        low = [g.astype(jnp.bfloat16) for g in (d_expand, d_contract, d_qkv, d_out)]
-        width = vectors.shape[1]
-        padded = jnp.pad(vectors, ((0, 0), (0, -width % 1024)))
-        parts = [padded.reshape(shards, -1, 128)]
-        parts += [g.reshape(shards, -1, g.shape[-1]) for g in low]
-        vectors, d_expand, d_contract, d_qkv, d_out = scatter_all(parts, planes)
-        vectors = vectors.reshape(-1)[:width]
-    else:
-        d_expand, d_contract, d_qkv, d_out = [
-            lax.psum_scatter(g.reshape(-1).astype(jnp.float32), ("dp", "seq"), scatter_dimension=0, tiled=True)
-            for g in (d_expand, d_contract, d_qkv, d_out)
-        ]
-        vectors = lax.psum_scatter(vectors, ("dp", "seq"), scatter_dimension=0, tiled=True)[0]
-    a, b = d_biases.size // shards, d_gains.size // shards
-    return (
-        d_qkv.reshape(-1),
-        d_out.reshape(-1),
-        d_expand.reshape(-1),
-        d_contract.reshape(-1),
-        vectors[:a],
-        vectors[a : a + b],
-        vectors[a + b :],
-    )
-
-
 def owner(head, n):
     return head * n // H
 
@@ -628,34 +339,36 @@
     walk(lambda cp: cp.wait_send())
 
 
-def send_from_owners(n, place, head, mine, src, dst, sems):
+def walk_from_owners(n, place, head, src, dst, sems, act):
     row = lax.axis_index("dp")
-    send_sem, recv_sem, own_sem = sems
-
-    def walk(act):
-        def body(k, _):
-            to = (place + 1 + k) % n
-            act(
-                pltpu.make_async_remote_copy(
-                    src_ref=src.at[to],
-                    dst_ref=dst.at[head],
-                    send_sem=send_sem.at[0, to],
-                    recv_sem=recv_sem.at[0, head],
-                    device_id=(row, to),
-                    device_id_type=MESH,
-                )
+
+    def body(k, _):
+        to = (place + 1 + k) % n
+        act(
+            pltpu.make_async_remote_copy(
+                src_ref=src.at[to],
+                dst_ref=dst.at[head],
+                send_sem=sems[0].at[0, to],
+                recv_sem=sems[1].at[0, head],
+                device_id=(row, to),
+                device_id_type=MESH,
             )
-            return 0
-
-        lax.fori_loop(0, n - 1, body, 0)
-
+        )
+        return 0
+
+    lax.fori_loop(0, n - 1, body, 0)
+
+
+def start_from_owners(n, place, head, mine, src, dst, sems):
     @pl.when(mine)
     def _():
-        walk(lambda cp: cp.start())
-        cp = pltpu.make_async_copy(src.at[place], dst.at[head], own_sem.at[0])
+        walk_from_owners(n, place, head, src, dst, sems, lambda cp: cp.start())
+        cp = pltpu.make_async_copy(src.at[place], dst.at[head], sems[2].at[0])
         cp.start()
         cp.wait()
 
+
+def wait_from_owners(n, place, head, src, dst, sems):
     def body(k, _):
         h = (head + k) % H
 
@@ -664,9 +377,9 @@
             pltpu.make_async_remote_copy(
                 src_ref=src.at[0],
                 dst_ref=dst.at[h],
-                send_sem=send_sem.at[0, 0],
-                recv_sem=recv_sem.at[0, h],
-                device_id=(row, place),
+                send_sem=sems[0].at[0, 0],
+                recv_sem=sems[1].at[0, h],
+                device_id=(lax.axis_index("dp"), place),
                 device_id_type=MESH,
             ).wait_recv()
 
@@ -674,9 +387,17 @@
 
     lax.fori_loop(0, H, body, 0)
 
+
+def finish_from_owners(n, place, head, mine, src, dst, sems):
     @pl.when(mine)
     def _():
-        walk(lambda cp: cp.wait_send())
+        walk_from_owners(n, place, head, src, dst, sems, lambda cp: cp.wait_send())
+
+
+def send_from_owners(n, place, head, mine, src, dst, sems):
+    start_from_owners(n, place, head, mine, src, dst, sems)
+    wait_from_owners(n, place, head, src, dst, sems)
+    finish_from_owners(n, place, head, mine, src, dst, sems)
 
 
 def swap_halves(tile):
@@ -1162,6 +883,478 @@
     )(attended, rows, cotangent, first, second, vectors, ffn_bias)
 
 
+def add_flat(out_ref, base, srcs):
+    rows, cols = srcs[0].shape
+    for k in range(cols // 128):
+        lanes = slice(k * 128, (k + 1) * 128)
+        total = srcs[0][:, lanes].astype(jnp.float32)
+        for s in srcs[1:]:
+            total = total + s[:, lanes].astype(jnp.float32)
+        out_ref[pl.ds(base + k, rows, stride=cols // 128), :] = total
+
+
+class Reduction:
+    def __init__(self, nz, me, links, z_first, own, give, emit, bufs, sems, pending):
+        self.nz, self.me, self.links, self.z_first = nz, me, links, z_first
+        self.own, self.give, self.emit = own, give, emit
+        self.rc, self.ra, self.rb, self.below, self.above = bufs
+        self.csend, self.crecv, self.send, self.recv = sems
+        self.pending = pending
+
+    @staticmethod
+    def buffers(nz, slab, z_first):
+        chips = 4 * nz
+        counts = (chips, 2, 2, chips, chips) if z_first else (chips, nz, 2 * nz, nz, nz)
+        return [pltpu.VMEM((c,) + slab, jnp.bfloat16) for c in counts]
+
+    @staticmethod
+    def semaphores(nz, z_first):
+        count = 8 * nz + 3 if z_first else 5 * nz
+        return [pltpu.SemaphoreType.DMA((c,)) for c in (4 * nz, 4 * nz, count, count)]
+
+    def start(self, src, dst, slot, to, cond=None):
+        cp = pltpu.make_async_remote_copy(
+            src_ref=src,
+            dst_ref=dst,
+            send_sem=self.send.at[slot],
+            recv_sem=self.recv.at[slot],
+            device_id=device(to),
+            device_id_type=MESH,
+        )
+        if cond is None:
+            cp.start()
+        else:
+            pl.when(cond)(cp.start)
+        self.pending.append((cp, cond))
+
+    def arrived(self, ref, sem):
+        pltpu.make_async_remote_copy(
+            src_ref=ref,
+            dst_ref=ref,
+            send_sem=self.send.at[0],
+            recv_sem=sem,
+            device_id=device(dict(self.me, c=1 - self.me["c"])),
+            device_id_type=MESH,
+        ).wait_recv()
+
+    def flip(self, which, f):
+        d = self.links[which]
+        return 1 - self.me[d] if f else self.me[d]
+
+    def piece(self, z, a, b):
+        c = {self.links[0]: a, self.links[1]: b}
+        return (c["y"] * self.nz + z) * 2 + c["x"]
+
+    def across(self, which):
+        d = self.links[which]
+        return dict(self.me, **{d: 1 - self.me[d]})
+
+    def hand_over(self):
+        nz = self.nz
+        zs = sorted(range(nz), key=lambda z: -abs(2 * z - nz + 1))
+        if self.z_first:
+            order = [(z, fa, fb) for z in zs for fa, fb in ((1, 1), (0, 1), (1, 0), (0, 0))]
+        else:
+            order = [(z, fa, fb) for fb in (1, 0) for fa in (1, 0) for z in zs]
+
+        def one(z, fa, fb):
+            def run():
+                p = self.piece(z, self.flip(0, fa), self.flip(1, fb))
+                cp = pltpu.make_async_remote_copy(
+                    src_ref=self.give(p),
+                    dst_ref=self.rc.at[p],
+                    send_sem=self.csend.at[p],
+                    recv_sem=self.crecv.at[p],
+                    device_id=device(dict(self.me, c=1 - self.me["c"])),
+                    device_id_type=MESH,
+                )
+                cp.start()
+                self.pending.append((cp, None))
+
+            return run
+
+        return [one(*o) for o in order]
+
+    def mine(self, p):
+        self.arrived(self.rc.at[p], self.crecv.at[p])
+        return [self.own(p), self.rc.at[p]]
+
+    def relay(self, z, p, srcs, bref, aref, sb, sa):
+        nz, mz, acc = self.nz, self.me["z"], self.rc.at[p]
+        if z > 0:
+
+            @pl.when(mz == 0)
+            def _():
+                combine(acc, srcs)
+
+            @pl.when(jnp.logical_and(mz > 0, mz < z))
+            def _():
+                self.arrived(bref, self.recv.at[sb])
+                combine(acc, srcs + [bref])
+
+            self.start(acc, bref, sb, dict(self.me, z=jnp.minimum(mz + 1, nz - 1)), mz < z)
+        if z < nz - 1:
+
+            @pl.when(mz == nz - 1)
+            def _():
+                combine(acc, srcs)
+
+            @pl.when(jnp.logical_and(mz < nz - 1, mz > z))
+            def _():
+                self.arrived(aref, self.recv.at[sa])
+                combine(acc, srcs + [aref])
+
+            self.start(acc, aref, sa, dict(self.me, z=jnp.maximum(mz - 1, 0)), mz > z)
+
+    def ends(self, z, bref, aref, sb, sa):
+        out = []
+        if z > 0:
+            self.arrived(bref, self.recv.at[sb])
+            out.append(bref)
+        if z < self.nz - 1:
+            self.arrived(aref, self.recv.at[sa])
+            out.append(aref)
+        return out
+
+    def steps(self):
+        return self.steps_z_first() if self.z_first else self.steps_z_last()
+
+    def steps_z_last(self):
+        nz, me = self.nz, self.me
+        zs = sorted(range(nz), key=lambda z: -abs(2 * z - nz + 1))
+
+        def along_b(z, fa):
+            def run():
+                a = self.flip(0, fa)
+                p = self.piece(z, a, self.flip(1, 1))
+                combine(self.rc.at[p], self.mine(p))
+                s = z * 2 + a
+                self.start(self.rc.at[p], self.rb.at[s], s, self.across(1))
+
+            return run
+
+        def along_a(z):
+            def run():
+                a = self.flip(0, 1)
+                p = self.piece(z, a, self.flip(1, 0))
+                s = z * 2 + a
+                srcs = self.mine(p)
+                self.arrived(self.rb.at[s], self.recv.at[s])
+                combine(self.rc.at[p], srcs + [self.rb.at[s]])
+                self.start(self.rc.at[p], self.ra.at[z], 2 * nz + z, self.across(0))
+
+            return run
+
+        def chain(z):
+            def run():
+                p = self.piece(z, self.flip(0, 0), self.flip(1, 0))
+                s = z * 2 + self.flip(0, 0)
+                srcs = self.mine(p)
+                self.arrived(self.rb.at[s], self.recv.at[s])
+                self.arrived(self.ra.at[z], self.recv.at[2 * nz + z])
+                srcs += [self.rb.at[s], self.ra.at[z]]
+                bref, aref = self.below.at[z], self.above.at[z]
+                self.relay(z, p, srcs, bref, aref, 3 * nz + z, 4 * nz + z)
+
+            return run
+
+        def last():
+            for z in range(nz):
+
+                @pl.when(me["z"] == z)
+                def _():
+                    p = self.piece(z, self.flip(0, 0), self.flip(1, 0))
+                    s = z * 2 + self.flip(0, 0)
+                    srcs = [self.own(p), self.rc.at[p], self.rb.at[s], self.ra.at[z]]
+                    bref, aref = self.below.at[z], self.above.at[z]
+                    self.emit(srcs + self.ends(z, bref, aref, 3 * nz + z, 4 * nz + z))
+
+        out = [(1 + i, along_b(z, 1)) for i, z in enumerate(zs)]
+        out += [(5 + i, along_b(z, 0)) for i, z in enumerate(zs)]
+        out += [(5.5 + i, along_a(z)) for i, z in enumerate(zs)]
+        out += [(9.5 + i, chain(z)) for i, z in enumerate(zs)]
+        return out + [(20, last)]
+
+    def steps_z_first(self):
+        nz, me = self.nz, self.me
+        zs = sorted(range(nz), key=lambda z: -abs(2 * z - nz + 1))
+        s0 = 8 * nz
+
+        def slots(z, fa, fb):
+            q = self.flip(0, fa) * 2 + self.flip(1, fb)
+            return self.below.at[z * 4 + q], self.above.at[z * 4 + q], z * 4 + q, 4 * nz + z * 4 + q
+
+        def chain(z, fa, fb):
+            def run():
+                p = self.piece(z, self.flip(0, fa), self.flip(1, fb))
+                self.relay(z, p, self.mine(p), *slots(z, fa, fb))
+
+            return run
+
+        def settle(fa, fb):
+            for z in range(nz):
+
+                @pl.when(me["z"] == z)
+                def _():
+                    p = self.piece(z, self.flip(0, fa), self.flip(1, fb))
+                    srcs = [self.own(p), self.rc.at[p]] + self.ends(z, *slots(z, fa, fb))
+                    combine(self.rc.at[p], srcs)
+
+            return self.rc.at[self.piece(me["z"], self.flip(0, fa), self.flip(1, fb))]
+
+        def along_b(fa):
+            def run():
+                self.start(settle(fa, 1), self.rb.at[fa], s0 + fa, self.across(1))
+
+            return run
+
+        def along_a():
+            ref = settle(1, 0)
+            self.arrived(self.rb.at[1], self.recv.at[s0 + 1])
+            combine(self.ra.at[0], [ref, self.rb.at[1]])
+            self.start(self.ra.at[0], self.ra.at[1], s0 + 2, self.across(0))
+
+        def last():
+            ref = settle(0, 0)
+            self.arrived(self.rb.at[0], self.recv.at[s0])
+            self.arrived(self.ra.at[1], self.recv.at[s0 + 2])
+            self.emit([ref, self.rb.at[0], self.ra.at[1]])
+
+        out = []
+        for i, z in enumerate(zs):
+            for m, (fa, fb) in enumerate(((1, 1), (0, 1), (1, 0), (0, 0))):
+                out.append((1 + i * 2.5 + m * 0.5, chain(z, fa, fb)))
+        return out + [(11.1, along_b(1)), (11.2, along_b(0)), (12.5, along_a), (21, last)]
+
+
+FFN_KINDS = (
+    ("expand", 0, D // UNITS, ("x", "y"), False),
+    ("contract", FF // UNITS // 3, FF // UNITS, ("y", "x"), False),
+    ("contract", 0, FF // UNITS // 3, ("x", "y"), False),
+    ("out", 0, D // UNITS, ("x", "y"), False),
+)
+QKV_KINDS = (
+    (0, ("x", "y"), False),
+    (1, ("y", "x"), False),
+    (2, ("x", "y"), True),
+)
+QKV_UNITS = 3 * UNITS
+UNIT = D // UNITS
+
+
+def finish_kernel(n, nz, *refs):
+    heads, rows_ref, w_hbm, d_sum1_ref, dw1, dw2, dwo, small_ref, ffn_ref = refs[:9]
+    d_tokens_ref, qkv_out, out_out, expand_out, contract_out, vec_out = refs[9:15]
+    inbox, proj, w_ref, own1, own2, owno, ownq, value, land = refs[15:24]
+    load_sem, vsend, vrecv = refs[24:27]
+    sems_in = refs[27:30]
+    rest = list(refs[30:])
+    place_row = lax.axis_index("seq")
+    head, mine = owned(place_row, n)
+    me = place(nz)
+
+    loads = [
+        pltpu.make_async_copy(src, dst, load_sem.at[i])
+        for i, (src, dst) in enumerate(((dw1, own1), (dw2, own2), (dwo, owno), (w_hbm, w_ref)))
+    ]
+    for cp in loads:
+        cp.start()
+    bar = pltpu.get_barrier_semaphore()
+
+    def greet(k, _):
+        to = (place_row + 1 + k) % n
+        pl.semaphore_signal(bar, inc=1, device_id=(me["y"], to), device_id_type=MESH)
+        return 0
+
+    lax.fori_loop(0, n - 1, greet, 0)
+    pl.semaphore_signal(bar, inc=1, device_id=(1 - me["y"], place_row), device_id_type=MESH)
+    pl.semaphore_wait(bar, n)
+
+    start_from_owners(n, place_row, head, mine, heads, inbox, sems_in)
+    pending = []
+    core = me["c"]
+
+    def take(count):
+        out = rest[:count]
+        del rest[:count]
+        return out
+
+    sources = {"expand": (dw1, own1), "contract": (dw2, own2), "out": (dwo, owno)}
+    targets = {"expand": expand_out, "contract": contract_out, "out": out_out}
+
+    def ffn_item(kind, lo, hi, links, z_first):
+        far, near = sources[kind]
+        whole = lo == 0 and hi == far.shape[1]
+
+        def at(ref, t):
+            return ref.at[t] if whole else ref.at[t, lo:hi]
+
+        cols = far.shape[2] // 128
+        return Reduction(
+            nz,
+            me,
+            links,
+            z_first,
+            lambda p: at(near, p * 2 + core),
+            lambda p: at(far, p * 2 + 1 - core),
+            lambda srcs: add_flat(targets[kind], lo * cols, srcs),
+            take(5),
+            take(4),
+            pending,
+        )
+
+    def qkv_item(j, links, z_first):
+        return Reduction(
+            nz,
+            me,
+            links,
+            z_first,
+            lambda p: ownq.at[(p * 2 + core) * 3 + j],
+            lambda p: ownq.at[(p * 2 + 1 - core) * 3 + j],
+            lambda srcs: add_flat(qkv_out, j * UNIT * (D // 128), srcs),
+            take(5),
+            take(4),
+            pending,
+        )
+
+    ffn = [ffn_item(*k) for k in FFN_KINDS]
+    qkv = [qkv_item(*k) for k in QKV_KINDS]
+
+    def hand_all(items):
+        for group in zip(*[i.hand_over() for i in items]):
+            for f in group:
+                f()
+
+    def ordered(items):
+        steps = [(w + 0.01 * i, f) for i, item in enumerate(items) for w, f in item.steps()]
+        return sorted(steps, key=lambda s: s[0])
+
+    hand_all(ffn)
+    for cp in loads[:3]:
+        cp.wait()
+    ffn_steps = ordered(ffn)
+    for w, f in ffn_steps:
+        if w < 20:
+            f()
+
+    wait_from_owners(n, place_row, head, heads, inbox, sems_in)
+    loads[3].wait()
+    half = TOK_SEQ // 2
+    for h in range(0, H, 2):
+        lanes = slice(h * HD, (h + 2) * HD)
+        k, v = unpack_pair(inbox[h, 0:TOK_SEQ, :], inbox[h + 1, 0:TOK_SEQ, :], (TOK_SEQ, 128))
+        proj[1, :, lanes] = k.astype(jnp.bfloat16)
+        proj[2, :, lanes] = v.astype(jnp.bfloat16)
+        for t in range(BPD // 2):
+            part = slice(TOK_SEQ + t * BLOCK, TOK_SEQ + (t + 1) * BLOCK)
+            a, b = unpack_pair(inbox[h, part, :], inbox[h + 1, part, :], (BLOCK, 128))
+            proj[0, 2 * t * BLOCK : (2 * t + 1) * BLOCK, lanes] = a.astype(jnp.bfloat16)
+            proj[0, (2 * t + 1) * BLOCK : (2 * t + 2) * BLOCK, lanes] = b.astype(jnp.bfloat16)
+
+    def weight_grad(e, _):
+        grad = inner_rows(rows_ref[...], proj[e])
+        ownq[pl.ds(e * UNITS, UNITS)] = grad.reshape(UNITS, UNIT, D).astype(jnp.bfloat16)
+        return 0
+
+    lax.fori_loop(0, 3, weight_grad, 0)
+    hand_all(qkv)
+
+    def add_rows(x):
+        return jnp.sum(x.astype(jnp.float32), axis=0, keepdims=True)
+
+    value[0, 0:1] = add_rows(proj[0])
+    value[0, 1:2] = add_rows(proj[2])
+    value[0, 2:8] = small_ref[0:6]
+    for c in range(FF // D):
+        value[0, 8 + c : 9 + c] = ffn_ref[:, c * D : (c + 1) * D]
+    partners = [dict(me, c=1 - core), dict(me, x=1 - me["x"]), dict(me, y=1 - me["y"])]
+    step = 1
+    while step < nz:
+        partners.append(dict(me, z=me["z"] + step - 2 * step * ((me["z"] // step) % 2)))
+        step *= 2
+
+    def vector_copy(i):
+        return pltpu.make_async_remote_copy(
+            src_ref=value.at[i],
+            dst_ref=land.at[i],
+            send_sem=vsend.at[i],
+            recv_sem=vrecv.at[i],
+            device_id=device(partners[i]),
+            device_id_type=MESH,
+        )
+
+    vector_copy(0).start()
+    for w, f in ffn_steps:
+        if w >= 20:
+            f()
+    d_tokens = d_sum1_ref[...]
+    for e in range(3):
+        d_tokens = d_tokens + outer_cols(proj[e], w_ref[e])
+    d_tokens_ref[...] = d_tokens
+    stage = 0
+    for w, f in ordered(qkv):
+        f()
+        if w > 3 + 2 * stage and stage < len(partners):
+            vector_copy(stage).wait_recv()
+            total = value[stage] + land[stage]
+            stage += 1
+            if stage < len(partners):
+                value[stage] = total
+                vector_copy(stage).start()
+            else:
+                vec_out[...] = total
+    for i in range(len(partners)):
+        vector_copy(i).wait_send()
+    finish_from_owners(n, place_row, head, mine, heads, inbox, sems_in)
+    for cp, cond in pending:
+        if cond is None:
+            cp.wait_send()
+        else:
+            pl.when(cond)(cp.wait_send)
+
+
+def finish(heads, rows, qkv, d_sum1, d_expand, d_contract, d_out, small, d_ffn, nz):
+    n = lax.axis_size("seq")
+    low, full = jnp.bfloat16, jnp.float32
+    flat = [(3 * UNIT * D // 128, 128), (UNIT * D // 128, 128)]
+    flat += [(UNIT * FF // 128, 128)] * 2
+    stages = 3 + (nz - 1).bit_length()
+    extra = []
+    for kind, lo, hi, links, z_first in FFN_KINDS:
+        width = FF if kind == "expand" else D
+        extra += Reduction.buffers(nz, (hi - lo, width), z_first)
+        extra += Reduction.semaphores(nz, z_first)
+    for j, links, z_first in QKV_KINDS:
+        extra += Reduction.buffers(nz, (UNIT, D), z_first)
+        extra += Reduction.semaphores(nz, z_first)
+    return pl.pallas_call(
+        functools.partial(finish_kernel, n, nz),
+        out_shape=[jax.ShapeDtypeStruct(s, full) for s in [(TOK_SEQ, D)] + flat + [(16, D)]],
+        in_specs=[ANY, VMEM, ANY, VMEM, ANY, ANY, ANY, VMEM, VMEM],
+        out_specs=[VMEM] * 6,
+        scratch_shapes=[
+            pltpu.VMEM((H, MSG, 128), low),
+            pltpu.VMEM((3, TOK_SEQ, D), low),
+            pltpu.VMEM((3, D, D), low),
+            pltpu.VMEM(d_expand.shape, low),
+            pltpu.VMEM(d_contract.shape, low),
+            pltpu.VMEM(d_out.shape, low),
+            pltpu.VMEM((QKV_UNITS, UNIT, D), low),
+            pltpu.VMEM((stages, 16, D), full),
+            pltpu.VMEM((stages, 16, D), full),
+            pltpu.SemaphoreType.DMA((4,)),
+            pltpu.SemaphoreType.DMA((stages,)),
+            pltpu.SemaphoreType.DMA((stages,)),
+            *exchange_sems(n),
+            *extra,
+        ],
+        compiler_params=pltpu.CompilerParams(
+            collective_id=5, has_side_effects=True, vmem_limit_bytes=60 << 20
+        ),
+        name="finish",
+    )(heads, rows, qkv, d_sum1, d_expand, d_contract, d_out, small, d_ffn)
+
+
 def unpack_heads(parts):
     parts = parts.reshape(H, BPD // 2, BLOCK, 2, HD).transpose(1, 3, 2, 0, 4)
     return parts.reshape(TOK_SEQ, D)
@@ -1194,22 +1387,41 @@
     result, d_sum1, d_heads, d_expand, d_contract, d_out, small, d_ffn = middle(
         attended, rows, cotangent.reshape(TOK_SEQ, D), first, second, vectors, ffn
     )
-    d_heads = exchange(
-        from_owners_kernel, H, attend_heads_back(kvq, picks, lse, d_heads), 5, "return_head_grads"
-    )
-    d_query = unpack_heads(d_heads[:, TOK_SEQ:])
-    d_pair = unpack_keys(d_heads[:, :TOK_SEQ])
-    d_proj = jnp.concatenate([d_query[None], d_pair], axis=0)
-    d_qkv = jnp.einsum("rd,erf->edf", rows, d_proj, preferred_element_type=jnp.float32)
-    d_tokens = d_sum1 + jnp.einsum("erf,edf->rd", d_proj, qkv, preferred_element_type=jnp.float32)
-    d_bias_q = jnp.sum(d_query.astype(jnp.float32), axis=0)
-    d_bias_v = jnp.sum(d_pair[1].astype(jnp.float32), axis=0)
-    d_biases = jnp.concatenate([jnp.stack([d_bias_q, d_bias_v]), small[0:4]])
-    shares = scatter_grads(
-        (d_qkv.reshape(3 * D, D), d_out, d_expand, d_contract, d_biases, small[4:6], d_ffn),
-        planes,
-    )
-    return (result[None], d_tokens[None]) + shares
+    d_heads = attend_heads_back(kvq, picks, lse, d_heads)
+    shards = lax.axis_size("dp") * lax.axis_size("seq")
+    if planes:
+        d_tokens, d_qkv, d_out, d_expand, d_contract, totals = finish(
+            d_heads, rows, qkv, d_sum1, d_expand, d_contract, d_out, small, d_ffn, planes
+        )
+        me = lax.axis_index("dp") * lax.axis_size("seq") + lax.axis_index("seq")
+        vectors = (totals[0:6], totals[6:8], totals[8 : 8 + FF // D])
+        vectors = [
+            lax.dynamic_slice(v.reshape(-1), (me * (v.size // shards),), (v.size // shards,))
+            for v in vectors
+        ]
+    else:
+        d_heads = exchange(from_owners_kernel, H, d_heads, 4, "return_head_grads")
+        d_query = unpack_heads(d_heads[:, TOK_SEQ:])
+        d_pair = unpack_keys(d_heads[:, :TOK_SEQ])
+        d_proj = jnp.concatenate([d_query[None], d_pair], axis=0)
+        d_qkv = jnp.einsum("rd,erf->edf", rows, d_proj, preferred_element_type=jnp.float32)
+        d_tokens = d_sum1 + jnp.einsum(
+            "erf,edf->rd", d_proj, qkv, preferred_element_type=jnp.float32
+        )
+        d_bias_q = jnp.sum(d_query.astype(jnp.float32), axis=0)
+        d_bias_v = jnp.sum(d_pair[1].astype(jnp.float32), axis=0)
+        d_biases = jnp.concatenate([jnp.stack([d_bias_q, d_bias_v]), small[0:4]])
+        *vectors, d_qkv, d_out, d_expand, d_contract = [
+            lax.psum_scatter(
+                g.astype(jnp.float32).reshape(-1),
+                ("dp", "seq"),
+                scatter_dimension=0,
+                tiled=True,
+            )
+            for g in (d_biases, small[4:6], d_ffn, d_qkv, d_out, d_expand, d_contract)
+        ]
+    grads = [g.reshape(-1) for g in (d_qkv, d_out, d_expand, d_contract)]
+    return (result[None], d_tokens[None], *grads, *vectors)
 
 
 def solution(mesh):

time: 351 us -> 328 us (0.934)
  Pallas kernels: 313 us -> 297 us
  matrix products: 6.46 us -> 0 us
    pallas_call x2 -> x1, Pallas kernels: 127 us -> 111 us  [finish(): pl.pallas_call(functools.partial(finish_kernel, n, nz), out_shape=[jax.Sh...]
    unnamed x36 -> x25, local copies, waits for them, and re-layouts: 6.15 us -> 13.6 us
    dot_general x2 -> x0, matrix products: 6.46 us -> none  [the longest x1 3.56 us: on_device(): jnp.einsum('erf,edf->rd', d_proj, qkv, preferred_element_type=jnp.float32)]
    reshape x9 -> x3, local copies, waits for them, and re-layouts: 6.42 us -> 0.03 us  [on_device(): v.reshape(-1)]
where the time goes in v4:
time: 328 us; the launch traced here: 324 us
  Pallas kernels  297 us (91%)
  local copies, waits for them, and re-layouts  24.1 us (7%)
    pallas_call x1, Pallas kernels, finish(): pl.pallas_call(functools.partial(finish_kernel, n, nz), out_shape=[jax.Sh...  111 us
    pallas_call x1, Pallas kernels, gather_all(): pl.pallas_call(functools.partial(gather_kernel, nz), out_shape=[jax.Shape...  62.1 us
    pallas_call x1, Pallas kernels, middle(): pl.pallas_call(functools.partial(mid_kernel, n), out_shape=[jax.ShapeDtyp...  43.3 us
    pallas_call x1, Pallas kernels, project_and_send(): pl.pallas_call(functools.partial(project_kernel, n), out_shape=(jax.Shape...  33.4 us
    pallas_call x1, Pallas kernels, attend_heads_back(): pl.pallas_call(functools.partial(attend_back_kernel, n), out_shape=jax.Sh...  25.3 us
    pallas_call x1, Pallas kernels, attend_heads(): pl.pallas_call(functools.partial(attend_kernel, n), out_shape=(jax.ShapeD...  22 us
    unnamed x25, local copies, waits for them, and re-layouts  13.6 us

profile of v4, /device:TPU:8, one launch (start us, length us, event | category | flops | bytes accessed | tf_op | source)
XLA Modules:
  0.0 324.3 jit_solution(6503146763858429662)
XLA Ops:
  0.6 1.0 reshape.85
  1.6 0.8 reshape.86
  2.4 0.8 fusion.5
  3.2 0.7 pad_maximum_fusion.refs_0_
  3.9 1.7 reshape.88.refs_1_
  5.6 1.7 reshape.89.refs_2_
  7.3 62.1 %gather_weights.1 = (bf16[32,24,3968]{2,1,0:T(8,128)(2,1)}, bf16[32,96,768]{2,1,0:T(8,128)(2,1)}, bf16[32,72,768]{2,1,0:T(8,128)(2,1)}) custom-call(bf16[24,3968]{1,0:T(8,128)(2,1)} %pad_maximum_fusion.refs_0_, bf16[96,768]{1,0:T(8,128)(2,1)} %reshape.88.refs_1_, bf16[72,768]{1,0:T(8,128)(2,1)} %reshape.89.refs_2_), custom_call_target="tpu_custom_call" | custom-call | tf_op jit(solution)/shard_map/gather_weights/pallas_call | solution.py:174
  69.3 1.0 slice_convert_fusion
  70.7 0.7 copy.20
  71.4 0.1 copy.21
  71.5 2.0 copy-done
  73.5 1.0 copy-done.2
  74.5 33.4 %project_and_send.1 = (bf16[16,384,128]{2,1,0:T(8,128)(2,1)S(1)}, s32[16,8,128]{2,1,0:T(8,128)S(1)}) custom-call(bf16[256,768]{1,0:T(8,128)(2,1)S(1)} %bitcast.18, bf16[3,768,768]{2,1,0:T(8,128)(2,1)S(1)} %bitcast.15, f32[8,768]{1,0:T(8,128)S(1)} %pad_maximum_fusion.1.bias_ref.refs_5_, s32[12,8,128]{2,1,0:T(8,128)S(1)} %pad.9.picks_ref), custom_call_target="tpu_custom_call" | custom-call | tf_op jit(solution)/shard_map/project_and_send/pallas_call | solution.py:459
  107.9 22.0 %attend_heads.1 = (bf16[16,128,128]{2,1,0:T(8,128)(2,1)S(1)}, f32[32,1,128]{2,1,0:T(1,128)S(1)}) custom-call(bf16[16,384,128]{2,1,0:T(8,128)(2,1)S(1)} %get-tuple-element.32.kvq_ref, s32[16,8,128]{2,1,0:T(8,128)S(1)} %get-tuple-element.33.picks_ref), custom_call_target="tpu_custom_call" | custom-call | tf_op jit(solution)/shard_map/attend_heads/pallas_call | solution.py:586
  129.9 0.8 copy-done.3
  130.7 0.6 copy-done.6
  131.4 0.7 reshape.97.refs_6_
  132.1 43.3 %middle.1 = (f32[256,768]{1,0:T(8,128)}, f32[256,768]{1,0:T(8,128)}, bf16[16,128,128]{2,1,0:T(8,128)(2,1)}, bf16[32,24,3072]{2,1,0:T(8,128)(2,1)}, bf16[32,96,76...) custom-call(bf16[16,128,128]{2,1,0:T(8,128)(2,1)} %copy-done.3, ...), custom_call_target="tpu_custom_call" | custom-call | tf_op jit(solution)/shard_map/middle/pallas_call | solution.py:859
  175.4 25.3 %attend_heads_back.1.refs_0_ = bf16[16,384,128]{2,1,0:T(8,128)(2,1)} custom-call(bf16[16,384,128]{2,1,0:T(8,128)(2,1)} %copy-done.1, s32[16,8,128]{2,1,0:T(8,128)} %copy-done.4, f32[32,1,128]{2,1,0:T(1,128)} %copy-done.6, bf16[16,128,128]{2,1,0:T(8,128)(2,1)} %get-tuple-element.38.grad_ref), custom_call_target="tpu_custom_call" | custom-call | tf_op jit(solution)/shard_map/attend_heads_back/pallas_call | solution.py:661
  200.7 111.0 %finish.1 = (f32[256,768]{1,0:T(8,128)}, f32[432,128]{1,0:T(8,128)}, f32[144,128]{1,0:T(8,128)}, f32[576,128]{1,0:T(8,128)}, f32[576,128]{1,0:T(8,128)}, /*index=5*/f32[16,768]{1,0:T(8,128)}) custom-call(bf16[16,384,128]{2,1,0:T(8,128)(2,1)} %attend_heads_back.1.refs_0_, bf16[256,768]{1,0:T(8,128)(2,1)} %bitcast.17, bf16[3,768,768]{2,1,0:T(8,128)(2,1)} %bitcast.14, ...), custom_call_target="tpu_custom_call" | custom-call | tf_op jit(solution)/shard_map/finish/pallas_call | solution.py:1330
  311.7 0.8 slice.25
  312.5 0.6 dynamic_slice.9
  313.1 0.7 slice.27
  313.9 0.6 dynamic_slice.11
  314.5 0.7 slice.26
  315.2 0.6 dynamic_slice.10
  315.8 0.9 copy.28
  316.7 2.1 copy.29
  318.8 1.6 copy.30
  320.4 1.5 copy.31
  321.9 1.7 copy.32
  323.6 0.7 copy.33
  (25 shorter events, 0.5 us)
Async XLA Ops:
  70.7 61.4 %copy-start.5 = (f32[8,768]{1,0:T(8,128)}, f32[8,768]{1,0:T(8,128)S(1)}, u32[]{:S(2)}) copy-start(f32[8,768]{1,0:T(8,128)S(1)} %pad_maximum_fusion.1.bias_ref.refs_5_) | copy-start | bytes 73732
  71.5 2.0 copy-start
  73.5 1.0 copy-start.2
  107.9 67.4 %copy-start.1 = (bf16[16,384,128]{2,1,0:T(8,128)(2,1)}, bf16[16,384,128]{2,1,0:T(8,128)(2,1)S(1)}, u32[]{:S(2)}) copy-start(bf16[16,384,128]{2,1,0:T(8,128)(2,1)S(1)} %get-tuple-element.32.kvq_ref) | copy-start | bytes 4718596
  107.9 67.4 %copy-start.4 = (s32[16,8,128]{2,1,0:T(8,128)}, s32[16,8,128]{2,1,0:T(8,128)S(1)}, u32[]{:S(2)}) copy-start(s32[16,8,128]{2,1,0:T(8,128)S(1)} %get-tuple-element.33.picks_ref) | copy-start | bytes 196612
  129.9 0.8 copy-start.3
  130.7 0.6 copy-start.6
  200.7 115.1 %copy-start.7 = (f32[256,768]{1,0:T(8,128)S(1)}, f32[256,768]{1,0:T(8,128)}, u32[]{:S(2)}) copy-start(f32[256,768]{1,0:T(8,128)} %get-tuple-element.36) | copy-start | bytes 2359300
  311.7 11.9 %copy-start.8 = (f32[576,128]{1,0:T(8,128)S(1)}, f32[576,128]{1,0:T(8,128)}, u32[]{:S(2)}) copy-start(f32[576,128]{1,0:T(8,128)} %get-tuple-element.49) | copy-start | bytes 884740

commit v5 on v4

--- a/solution.py
+++ b/solution.py
@@ -75,113 +75,6 @@
         rank = sorted(range(n), key=lambda s: (abs(s - i), s))
         out = jnp.where(m == i, rank[j], out)
     return out
-
-ORDERS = (("z", "x", "y"), ("z", "y", "x"), ("x", "y", "z"))
-
-def gather_kernel(nz, *refs):
-    k = len(ORDERS)
-    xs, gs = refs[:k], refs[k:2 * k]
-    own_sem, send_sem, recv_sem, csend, crecv = refs[2 * k:]
-    me = place(nz)
-    size = {"y": 2, "z": nz, "x": 2}
-    sib = dict(me, c=1 - me["c"])
-    bar = pltpu.get_barrier_semaphore()
-    for d in ("x", "y", "c"):
-        pl.semaphore_signal(bar, inc=1, device_id=device(dict(me, **{d: 1 - me[d]})), device_id_type=MESH)
-    @pl.when(me["z"] > 0)
-    def _():
-        pl.semaphore_signal(bar, inc=1, device_id=device(dict(me, z=me["z"] - 1)), device_id_type=MESH)
-    @pl.when(me["z"] < nz - 1)
-    def _():
-        pl.semaphore_signal(bar, inc=1, device_id=device(dict(me, z=me["z"] + 1)), device_id_type=MESH)
-    inside = jnp.where(me["z"] > 0, 1, 0) + jnp.where(me["z"] < nz - 1, 1, 0)
-    pl.semaphore_wait(bar, 3 + inside)
-
-    pending = []
-    def remote(item, src_ref, slot, sem_slot, way, to, cond=None):
-        cp = pltpu.make_async_remote_copy(src_ref=src_ref, dst_ref=gs[item].at[slot], send_sem=send_sem.at[item, sem_slot, way],
-            recv_sem=recv_sem.at[item, sem_slot], device_id=device(to), device_id_type=MESH)
-        if cond is None:
-            cp.start()
-        else:
-            pl.when(cond)(cp.start)
-        pending.append((cp, cond))
-
-    work = []
-    for item in range(k):
-        order = ORDERS[item]
-        n0, n1, n2 = (size[d] for d in order)
-        for i2 in range(n2):
-            for i1 in range(n1):
-                for i0 in range(n0):
-                    work.append((i0 + i1 + i2, item, i0, i1, i2))
-    work.sort(key=lambda w: w[0])
-    local = []
-    for depth, item, i0, i1, i2 in work:
-        order = ORDERS[item]
-        src = dict(me)
-        for d, i in zip(order, (i0, i1, i2)):
-            src[d] = nearest(me[d], size[d], i)
-        c = chip(src, nz)
-        slot = c * 2 + me["c"]
-        own = depth == 0
-        ref = xs[item] if own else gs[item].at[slot]
-        if not own:
-            pltpu.make_async_remote_copy(src_ref=ref, dst_ref=ref, send_sem=send_sem.at[item, c, 0], recv_sem=recv_sem.at[item, c],
-                device_id=device(sib), device_id_type=MESH).wait_recv()
-        stage = 2 if i2 else (1 if i1 else 0)
-        for t in range(stage, 3):
-            d = order[t]
-            onward = t == stage and not own
-            if d == "z":
-                if nz > 1:
-                    up = me["z"] < nz - 1
-                    dn = me["z"] > 0
-                    if onward:
-                        up = jnp.logical_and(up, src["z"] <= me["z"])
-                        dn = jnp.logical_and(dn, src["z"] >= me["z"])
-                    remote(item, ref, slot, c, 0, dict(me, z=jnp.minimum(me["z"] + 1, nz - 1)), up)
-                    remote(item, ref, slot, c, 1, dict(me, z=jnp.maximum(me["z"] - 1, 0)), dn)
-            elif not (onward and (i0, i1, i2)[t]):
-                remote(item, ref, slot, c, 2 if d == "x" else 3, dict(me, **{d: 1 - me[d]}))
-        cp = pltpu.make_async_remote_copy(src_ref=ref, dst_ref=gs[item].at[slot], send_sem=csend.at[item, c],
-            recv_sem=crecv.at[item, c], device_id=device(sib), device_id_type=MESH)
-        cp.start()
-        pending.append((cp, None))
-        if own:
-            lc = pltpu.make_async_copy(xs[item], gs[item].at[slot], own_sem.at[item])
-            lc.start()
-            local.append(lc)
-    for lc in local:
-        lc.wait()
-    for item in range(k):
-        def body(c, _):
-            ref = gs[item].at[c * 2 + 1 - me["c"]]
-            pltpu.make_async_remote_copy(src_ref=ref, dst_ref=ref, send_sem=csend.at[item, c], recv_sem=crecv.at[item, c],
-                device_id=device(sib), device_id_type=MESH).wait_recv()
-            return 0
-        lax.fori_loop(0, 4 * nz, body, 0)
-    for cp, cond in pending:
-        if cond is None:
-            cp.wait_send()
-        else:
-            pl.when(cond)(cp.wait_send)
-
-def gather_all(xs, nz):
-    n = 8 * nz
-    k = len(xs)
-    chips = 4 * nz
-    return pl.pallas_call(
-        functools.partial(gather_kernel, nz),
-        out_shape=[jax.ShapeDtypeStruct((n,) + x.shape, x.dtype) for x in xs],
-        in_specs=[pl.BlockSpec(memory_space=pl.ANY)] * k,
-        out_specs=[pl.BlockSpec(memory_space=pl.ANY)] * k,
-        scratch_shapes=[pltpu.SemaphoreType.DMA((k,)), pltpu.SemaphoreType.DMA((k, chips, 4)), pltpu.SemaphoreType.DMA((k, chips)),
-            pltpu.SemaphoreType.DMA((k, chips)), pltpu.SemaphoreType.DMA((k, chips))],
-        compiler_params=pltpu.CompilerParams(collective_id=0, has_side_effects=True),
-        name="gather_weights",
-    )(*xs)
-
 
 def combine(dst, srcs):
     rows, cols = dst.shape
@@ -201,54 +94,6 @@
             return 0
         lax.fori_loop(0, cols // step, body, 0)
 
-def kernel_planes(arrays):
-    seq = lax.axis_size("seq")
-    if lax.axis_size("dp") != 2 or seq % 4:
-        return 0
-    if seq // 4 not in (2, 4) or 2 * seq != UNITS:
-        return 0
-    return seq // 4
-
-
-def gather_weights(
-    qkv_weight, out_weight, expand_weight, contract_weight, bias_vectors, gain_vectors, ffn_bias
-):
-    vectors = jnp.concatenate([bias_vectors, gain_vectors, ffn_bias])
-    planes = kernel_planes((qkv_weight, out_weight, expand_weight, contract_weight))
-    if planes:
-        shards = 8 * planes
-        depth = expand_weight.size // FF
-        tail = jnp.pad(vectors, (0, depth * 128 - vectors.size)).reshape(depth, 128)
-        first = jnp.concatenate(
-            [expand_weight.reshape(depth, FF), out_weight.reshape(depth, D), tail], axis=1
-        )
-        first, contract, qkv = gather_all(
-            (first, contract_weight.reshape(-1, D), qkv_weight.reshape(-1, D)), planes
-        )
-        first = first.reshape(D, FF + D + 128)
-        vectors = first[:, FF + D :].reshape(shards, depth * 128)
-        contract = contract.reshape(FF, D)
-        qkv = qkv.reshape(3, D, D)
-    else:
-        gather = functools.partial(lax.all_gather, axis_name=("dp", "seq"), axis=0, tiled=True)
-        qkv = gather(qkv_weight).reshape(3, D, D)
-        first = jnp.concatenate(
-            [gather(expand_weight).reshape(D, FF), gather(out_weight).reshape(D, D)], axis=1
-        )
-        contract = gather(contract_weight).reshape(FF, D)
-        vectors = gather(vectors[None])
-    a, b, c = bias_vectors.size, gain_vectors.size, ffn_bias.size
-    vectors = vectors.astype(jnp.float32)
-    rows = [vectors[:, :a].reshape(6, D), vectors[:, a : a + b].reshape(2, D)]
-    return (
-        qkv,
-        first,
-        contract,
-        jnp.concatenate(rows),
-        vectors[:, a + b : a + b + c].reshape(1, FF),
-    )
-
-
 def owner(head, n):
     return head * n // H
 
@@ -282,42 +127,44 @@
             pl.semaphore_wait(bar, n - 1)
 
 
-def send_to_owners(n, place, head, mine, pairs, sems, meanwhile=None):
+def walk_to_owners(n, place, head, pairs, sems, act):
     row = lax.axis_index("dp")
-    send_sem, recv_sem, own_sem = sems
-    first = head + 1
-
-    def walk(act):
-        def body(k, _):
-            h = (first + k) % H
-            to = owner(h, n)
-            for i, (src, dst) in enumerate(pairs):
-
-                @pl.when(to != place)
-                def _():
-                    act(
-                        pltpu.make_async_remote_copy(
-                            src_ref=src.at[h],
-                            dst_ref=dst.at[place],
-                            send_sem=send_sem.at[i, h],
-                            recv_sem=recv_sem.at[i, place],
-                            device_id=(row, to),
-                            device_id_type=MESH,
-                        )
+
+    def body(k, _):
+        h = (head + 1 + k) % H
+        to = owner(h, n)
+        for i, (src, dst) in enumerate(pairs):
+
+            @pl.when(to != place)
+            def _():
+                act(
+                    pltpu.make_async_remote_copy(
+                        src_ref=src.at[h],
+                        dst_ref=dst(place),
+                        send_sem=sems[0].at[i, h],
+                        recv_sem=sems[1].at[i, place],
+                        device_id=(row, to),
+                        device_id_type=MESH,
                     )
-
-            return 0
-
-        lax.fori_loop(0, H, body, 0)
-
-    walk(lambda cp: cp.start())
-    if meanwhile is not None:
-        meanwhile()
+                )
+
+        return 0
+
+    lax.fori_loop(0, H, body, 0)
+
+
+def finish_to_owners(n, place, head, pairs, sems):
+    walk_to_owners(n, place, head, pairs, sems, lambda cp: cp.wait_send())
+
+
+def send_to_owners(n, place, head, mine, pairs, sems, meanwhile, wait_sends=True):
+    walk_to_owners(n, place, head, pairs, sems, lambda cp: cp.start())
+    meanwhile()
 
     @pl.when(mine)
     def _():
         for i, (src, dst) in enumerate(pairs):
-            cp = pltpu.make_async_copy(src.at[head], dst.at[place], own_sem.at[i])
+            cp = pltpu.make_async_copy(src.at[head], dst(place), sems[2].at[i])
             cp.start()
             cp.wait()
 
@@ -326,17 +173,18 @@
             for i, (src, dst) in enumerate(pairs):
                 pltpu.make_async_remote_copy(
                     src_ref=src.at[0],
-                    dst_ref=dst.at[s],
-                    send_sem=send_sem.at[i, 0],
-                    recv_sem=recv_sem.at[i, s],
-                    device_id=(row, place),
+                    dst_ref=dst(s),
+                    send_sem=sems[0].at[i, 0],
+                    recv_sem=sems[1].at[i, s],
+                    device_id=(lax.axis_index("dp"), place),
                     device_id_type=MESH,
                 ).wait_recv()
             return 0
 
         lax.fori_loop(0, n - 1, body, 0)
 
-    walk(lambda cp: cp.wait_send())
+    if wait_sends:
+        finish_to_owners(n, place, head, pairs, sems)
 
 
 def walk_from_owners(n, place, head, src, dst, sems, act):
@@ -408,37 +256,6 @@
     return lax.broadcasted_iota(jnp.int32, shape, len(shape) - 1) < HD
 
 
-def project_kernel(n, rows_ref, w_ref, bias_ref, picks_ref, out_ref, out_picks_ref, box, *sems):
-    place = lax.axis_index("seq")
-    head, mine = owned(place, n)
-    greet_senders(n, place, mine, True)
-    rows = rows_ref[...]
-    left = low_lanes((TOK_SEQ, 128))
-    left_q = low_lanes((BLOCK, 128))
-    wide = 256
-    for g in range(D // wide):
-        cols = slice(g * wide, (g + 1) * wide)
-        q = (matmul(rows, w_ref[0, :, cols]) + bias_ref[0:1, cols]) * HD ** (-0.5)
-        k = matmul(rows, w_ref[1, :, cols])
-        v = matmul(rows, w_ref[2, :, cols]) + bias_ref[1:2, cols]
-        for p in range(wide // 128):
-            h = (g * wide + p * 128) // HD
-            lanes = slice(p * 128, (p + 1) * 128)
-            kp, vp, qp = k[:, lanes], v[:, lanes], q[:, lanes]
-            box[h, 0:TOK_SEQ, :] = jnp.where(left, kp, swap_halves(vp)).astype(jnp.bfloat16)
-            box[h + 1, 0:TOK_SEQ, :] = jnp.where(left, swap_halves(kp), vp).astype(jnp.bfloat16)
-            turned = swap_halves(qp)
-            for t in range(BPD // 2):
-                a = slice(2 * t * BLOCK, (2 * t + 1) * BLOCK)
-                b = slice((2 * t + 1) * BLOCK, (2 * t + 2) * BLOCK)
-                to = slice(TOK_SEQ + t * BLOCK, TOK_SEQ + (t + 1) * BLOCK)
-                box[h, to, :] = jnp.where(left_q, qp[a], turned[b]).astype(jnp.bfloat16)
-                box[h + 1, to, :] = jnp.where(left_q, turned[a], qp[b]).astype(jnp.bfloat16)
-    send_to_owners(
-        n, place, head, mine, ((box, out_ref), (picks_ref, out_picks_ref)), sems
-    )
-
-
 def exchange_sems(n, pairs=1):
     return [
         pltpu.SemaphoreType.DMA((pairs, max(n, H))),
@@ -451,25 +268,6 @@
 VMEM = pl.BlockSpec(memory_space=pltpu.VMEM)
 SMEM = pl.BlockSpec(memory_space=pltpu.SMEM)
 MSG = TOK_SEQ + TOK_SEQ // 2
-
-
-def project_and_send(rows, qkv, biases, picks):
-    n = lax.axis_size("seq")
-    picks = jnp.pad(picks.reshape(H, 1, BPD * 3), ((0, 0), (0, 7), (0, 128 - BPD * 3)))
-    return pl.pallas_call(
-        functools.partial(project_kernel, n),
-        out_shape=(
-            jax.ShapeDtypeStruct((n, MSG, 128), jnp.bfloat16),
-            jax.ShapeDtypeStruct((n, 8, 128), jnp.int32),
-        ),
-        in_specs=[VMEM, VMEM, VMEM, ANY],
-        out_specs=(ANY, ANY),
-        scratch_shapes=[pltpu.VMEM((H, MSG, 128), jnp.bfloat16)] + exchange_sems(n, 2),
-        compiler_params=pltpu.CompilerParams(
-            collective_id=2, has_side_effects=True, vmem_limit_bytes=48 << 20
-        ),
-        name="project_and_send",
-    )(rows, qkv, biases, picks)
 
 
 def from_owners_kernel(n, src, dst, *sems):
@@ -500,20 +298,17 @@
         picked = [picks_ref[s, 0, r * 3 + j] for j in range(3)]
         return [jnp.maximum(b - 1, 0), b, jnp.minimum(b + 1, last), 0, last] + picked
 
-    return [
-        [(b // BPD, pl.multiple_of(b % BPD * BLOCK, BLOCK)) for b in of(2 * i + t)]
-        for t in range(2)
-    ]
+    return [of(2 * i), of(2 * i + 1)]
 
 
 def fill_pair(lists, kv_ref, vk_ref, keys, values):
     for j in range(8):
-        (sa, ra), (sb, rb) = lists[0][j], lists[1][j]
+        a, b = lists[0][j], lists[1][j]
         to = slice(j * BLOCK, (j + 1) * BLOCK)
-        keys[to, 0:HD] = kv_ref[sa, pl.ds(ra, BLOCK), 0:HD]
-        keys[to, HD:128] = vk_ref[sb, pl.ds(rb, BLOCK), HD:128]
-        values[to, 0:HD] = vk_ref[sa, pl.ds(ra, BLOCK), 0:HD]
-        values[to, HD:128] = kv_ref[sb, pl.ds(rb, BLOCK), HD:128]
+        keys[to, 0:HD] = kv_ref[a][:, 0:HD]
+        keys[to, HD:128] = vk_ref[b][:, HD:128]
+        values[to, 0:HD] = vk_ref[a][:, 0:HD]
+        values[to, HD:128] = kv_ref[b][:, HD:128]
 
 
 def two_blocks(tile):
@@ -540,139 +335,94 @@
     )
 
 
-def pair_place(i):
-    return i // (BPD // 2), pl.multiple_of(i % (BPD // 2) * BLOCK, BLOCK)
-
-
 def turn_pairs(n, kv_ref, vk_ref):
-    def body(s, _):
-        tile = kv_ref[s, 0:TOK_SEQ, :].astype(jnp.float32)
-        vk_ref[s] = swap_halves(tile).astype(jnp.bfloat16)
+    def body(b, _):
+        for t in range(BPD):
+            tile = kv_ref[b * BPD + t].astype(jnp.float32)
+            vk_ref[b * BPD + t] = swap_halves(tile).astype(jnp.bfloat16)
         return 0
 
     lax.fori_loop(0, n, body, 0)
 
 
-def attend_kernel(n, kvq_ref, picks_ref, out_ref, lse_ref, vk_ref, keys, values):
-    place = lax.axis_index("seq")
-    head, mine = owned(place, n)
-
-    @pl.when(mine)
-    def _():
-        turn_pairs(n, kvq_ref, vk_ref)
-
-        def body(i, _):
-            fill_pair(key_list(i, n, picks_ref), kvq_ref, vk_ref, keys, values)
-            s, r = pair_place(i)
-            query = two_blocks(kvq_ref[s, pl.ds(TOK_SEQ + r, BLOCK), :])
-            scores = pair_scores(i, n, keys[...], query)
-            top = jnp.max(scores, axis=0, keepdims=True)
-            weights = jnp.exp(scores - top)
-            total = jnp.sum(weights, axis=0, keepdims=True)
-            probs = (weights * (1.0 / total)).astype(jnp.bfloat16)
-            full = inner_rows(probs, values[...])
-            left = low_lanes((BLOCK, 128))
-            out_ref[s, pl.ds(r, BLOCK), :] = jnp.where(left, full[:BLOCK], full[BLOCK:]).astype(
-                jnp.bfloat16
-            )
-            lse_ref[i] = top + jnp.log(total)
-            return 0
-
-        lax.fori_loop(0, n * BPD // 2, body, 0)
-
-
-def attend_heads(kvq, picks):
-    n = lax.axis_size("seq")
-    return pl.pallas_call(
-        functools.partial(attend_kernel, n),
-        out_shape=(
-            jax.ShapeDtypeStruct((n, TOK_SEQ // 2, 128), jnp.bfloat16),
-            jax.ShapeDtypeStruct((n * BPD // 2, 1, 128), jnp.float32),
-        ),
-        in_specs=[VMEM, SMEM],
-        out_specs=(VMEM, VMEM),
-        scratch_shapes=[
-            pltpu.VMEM((n, TOK_SEQ, 128), jnp.bfloat16),
-            pltpu.VMEM((8 * BLOCK, 128), jnp.bfloat16),
-            pltpu.VMEM((8 * BLOCK, 128), jnp.bfloat16),
-        ],
-        compiler_params=pltpu.CompilerParams(vmem_limit_bytes=48 << 20),
-        name="attend_heads",
-    )(kvq, picks)
-
-
 def attend_back_kernel(
-    n, kvq_ref, picks_ref, lse_ref, grad_ref, out_ref, vk_ref, keys, values, sum_k, sum_v
+    n, kv_ref, q_ref, picks_ref, lse_ref, grad_ref, out_ref, vk_ref, keys, values, sum_k, sum_v
 ):
     place = lax.axis_index("seq")
     head, mine = owned(place, n)
 
     @pl.when(mine)
     def _():
-        turn_pairs(n, kvq_ref, vk_ref)
+        turn_pairs(n, kv_ref, vk_ref)
 
         def clear(s, _):
-            sum_k[s] = jnp.zeros((TOK_SEQ, 128), jnp.float32)
-            sum_v[s] = jnp.zeros((TOK_SEQ, 128), jnp.float32)
+            for t in range(BPD):
+                sum_k[s * BPD + t] = jnp.zeros((BLOCK, 128), jnp.float32)
+                sum_v[s * BPD + t] = jnp.zeros((BLOCK, 128), jnp.float32)
             return 0
 
         lax.fori_loop(0, n, clear, 0)
-
-        def body(i, _):
-            lists = key_list(i, n, picks_ref)
-            fill_pair(lists, kvq_ref, vk_ref, keys, values)
-            s, r = pair_place(i)
-            query = two_blocks(kvq_ref[s, pl.ds(TOK_SEQ + r, BLOCK), :])
-            grad = two_blocks(grad_ref[s, pl.ds(r, BLOCK), :])
-            probs = jnp.exp(pair_scores(i, n, keys[...], query) - lse_ref[i])
-            d_probs = outer_cols(values[...], grad)
-            rows = jnp.sum(probs * d_probs, axis=0, keepdims=True)
-            d_scores = (probs * (d_probs - rows)).astype(jnp.bfloat16)
-            d_values = matmul(probs.astype(jnp.bfloat16), grad)
-            d_keys = matmul(d_scores, query)
-            full = inner_rows(d_scores, keys[...]) * HD ** (-0.5)
-            left = low_lanes((BLOCK, 128))
-            out_ref[s, pl.ds(TOK_SEQ + r, BLOCK), :] = jnp.where(
-                left, full[:BLOCK], full[BLOCK:]
-            ).astype(jnp.bfloat16)
-            for j in range(8):
-                part = slice(j * BLOCK, (j + 1) * BLOCK)
-                for t in range(2):
-                    sb, rb = lists[t][j]
-                    lanes = slice(t * HD, (t + 1) * HD)
-                    sum_k[sb, pl.ds(rb, BLOCK), lanes] += d_keys[part, lanes]
-                    sum_v[sb, pl.ds(rb, BLOCK), lanes] += d_values[part, lanes]
+        left = low_lanes((BLOCK, 128))
+
+        def body(s, _):
+            lists = [key_list(s * (BPD // 2) + t, n, picks_ref) for t in range(BPD // 2)]
+            for t in range(BPD // 2):
+                fill_pair(lists[t], kv_ref, vk_ref, keys.at[t], values.at[t])
+            parts = []
+            for t in range(BPD // 2):
+                i = s * (BPD // 2) + t
+                part = slice(t * BLOCK, (t + 1) * BLOCK)
+                query = two_blocks(q_ref[s, part, :])
+                grad = two_blocks(grad_ref[s, part, :])
+                probs = jnp.exp(pair_scores(i, n, keys[t], query) - lse_ref[i])
+                d_probs = outer_cols(values[t], grad)
+                rows = jnp.sum(probs * d_probs, axis=0, keepdims=True)
+                d_scores = (probs * (d_probs - rows)).astype(jnp.bfloat16)
+                d_values = matmul(probs.astype(jnp.bfloat16), grad)
+                d_keys = matmul(d_scores, query)
+                full = inner_rows(d_scores, keys[t]) * HD ** (-0.5)
+                to = slice(TOK_SEQ + t * BLOCK, TOK_SEQ + (t + 1) * BLOCK)
+                out_ref[s, to, :] = jnp.where(left, full[:BLOCK], full[BLOCK:]).astype(jnp.bfloat16)
+                parts.append((d_keys, d_values))
+            for t in range(BPD // 2):
+                for j in range(8):
+                    part = slice(j * BLOCK, (j + 1) * BLOCK)
+                    for u in range(2):
+                        b = lists[t][u][j]
+                        lanes = slice(u * HD, (u + 1) * HD)
+                        sum_k[b, :, lanes] += parts[t][0][part, lanes]
+                        sum_v[b, :, lanes] += parts[t][1][part, lanes]
             return 0
 
-        lax.fori_loop(0, n * BPD // 2, body, 0)
+        lax.fori_loop(0, n, body, 0)
 
         def close(s, _):
-            left = low_lanes((TOK_SEQ, 128))
-            k, v = sum_k[s], sum_v[s]
-            both = jnp.where(left, k + swap_halves(k), v + swap_halves(v))
-            out_ref[s, 0:TOK_SEQ, :] = both.astype(jnp.bfloat16)
+            for t in range(BPD):
+                k, v = sum_k[s * BPD + t], sum_v[s * BPD + t]
+                both = jnp.where(left, k + swap_halves(k), v + swap_halves(v))
+                out_ref[s, t * BLOCK : (t + 1) * BLOCK, :] = both.astype(jnp.bfloat16)
             return 0
 
         lax.fori_loop(0, n, close, 0)
 
 
-def attend_heads_back(kvq, picks, lse, grad):
+def attend_heads_back(kv, queries, picks, lse, grad):
     n = lax.axis_size("seq")
     return pl.pallas_call(
         functools.partial(attend_back_kernel, n),
         out_shape=jax.ShapeDtypeStruct((n, MSG, 128), jnp.bfloat16),
-        in_specs=[VMEM, SMEM, VMEM, VMEM],
+        in_specs=[VMEM, VMEM, SMEM, VMEM, VMEM],
         out_specs=VMEM,
         scratch_shapes=[
-            pltpu.VMEM((n, TOK_SEQ, 128), jnp.bfloat16),
-            pltpu.VMEM((8 * BLOCK, 128), jnp.bfloat16),
-            pltpu.VMEM((8 * BLOCK, 128), jnp.bfloat16),
-            pltpu.VMEM((n, TOK_SEQ, 128), jnp.float32),
-            pltpu.VMEM((n, TOK_SEQ, 128), jnp.float32),
+            pltpu.VMEM((n * BPD, BLOCK, 128), jnp.bfloat16),
+            pltpu.VMEM((BPD // 2, 8 * BLOCK, 128), jnp.bfloat16),
+            pltpu.VMEM((BPD // 2, 8 * BLOCK, 128), jnp.bfloat16),
+            pltpu.VMEM((n * BPD, BLOCK, 128), jnp.float32),
+            pltpu.VMEM((n * BPD, BLOCK, 128), jnp.float32),
         ],
         compiler_params=pltpu.CompilerParams(vmem_limit_bytes=56 << 20),
         name="attend_heads_back",
-    )(kvq, picks, lse, grad)
+    )(kv, queries, picks, lse, grad)
 
 
 UNITS = 32
@@ -700,187 +450,6 @@
     left = low_lanes(shape)
     a, b = tiles.astype(jnp.float32), odd.astype(jnp.float32)
     return (jnp.where(left, a, swap_halves(b)), jnp.where(left, swap_halves(a), b))
-
-
-def mid_kernel(n, *refs):
-    (
-        attended,
-        rows_ref,
-        cot_ref,
-        first_hbm,
-        second_hbm,
-        vec_ref,
-        ffn_ref,
-        result_ref,
-        d_sum1_ref,
-        d_heads,
-        dw1_hbm,
-        dw2_hbm,
-        dwo_hbm,
-        small_ref,
-        d_ffn_ref,
-        inbox,
-        box,
-        w1_ref,
-        wo_ref,
-        w2_ref,
-        slope_ref,
-        active_ref,
-        dw1_ref,
-        dw2_ref,
-        dwo_ref,
-        mixed_ref,
-        load_sem,
-        store_sem,
-    ) = refs[:28]
-    sems_in, sems_out = refs[28:31], refs[31:34]
-    place = lax.axis_index("seq")
-    head, mine = owned(place, n)
-    loads = [
-        pltpu.make_async_copy(first_hbm.at[:, FF : FF + D], wo_ref, load_sem.at[0]),
-        pltpu.make_async_copy(first_hbm.at[:, 0:FF], w1_ref, load_sem.at[1]),
-        pltpu.make_async_copy(second_hbm, w2_ref, load_sem.at[2]),
-    ]
-    for cp in loads:
-        cp.start()
-    greet_row(n, place, mine)
-    send_from_owners(n, place, head, mine, attended, inbox, sems_in)
-
-    for h in range(0, H, 2):
-        for t in range(BPD // 2):
-            part = slice(t * BLOCK, (t + 1) * BLOCK)
-            a, b = unpack_pair(inbox[h, part, :], inbox[h + 1, part, :], (BLOCK, 128))
-            lanes = slice(h * HD, (h + 2) * HD)
-            mixed_ref[2 * t * BLOCK : (2 * t + 1) * BLOCK, lanes] = a.astype(jnp.bfloat16)
-            mixed_ref[(2 * t + 1) * BLOCK : (2 * t + 2) * BLOCK, lanes] = b.astype(jnp.bfloat16)
-    loads[0].wait()
-    hidden1 = rows_ref[...].astype(jnp.float32) + matmul(mixed_ref[...], wo_ref[...]) + vec_ref[2:3]
-    normed_out1, normed1, inverse1 = normalize(hidden1, vec_ref[6:7], vec_ref[3:4])
-    lowered = normed_out1.astype(jnp.bfloat16)
-    loads[1].wait()
-    loads[2].wait()
-
-    def up_step(c, hidden):
-        cols = pl.ds(pl.multiple_of(c * WIDE, WIDE), WIDE)
-        up = matmul(lowered, w1_ref[:, cols]) + ffn_ref[:, cols]
-        square = up * up
-        inner = (2 / jnp.pi) ** 0.5 * (up + 0.044715 * up * square)
-        curve = jnp.tanh(inner)
-        active = (0.5 * up * (1 + curve)).astype(jnp.bfloat16)
-        slope_ref[:, cols] = 0.5 * (1 + curve) + 0.5 * up * (1 - curve * curve) * (
-            (2 / jnp.pi) ** 0.5 * (1 + 3 * 0.044715 * square)
-        )
-        active_ref[:, cols] = active
-        return hidden + matmul(active, w2_ref[cols, :])
-
-    hidden2 = lax.fori_loop(0, FF // WIDE, up_step, normed_out1 + vec_ref[4:5])
-    result, normed2, inverse2 = normalize(hidden2, vec_ref[7:8], vec_ref[5:6])
-    result_ref[...] = result
-    grad = cot_ref[...].astype(jnp.float32)
-    d_sum2 = normalize_back(grad, normed2, inverse2, vec_ref[7:8])
-    d_down = d_sum2.astype(jnp.bfloat16)
-
-    def add_rows(value):
-        return jnp.sum(value, axis=0, keepdims=True)
-
-    small_ref[2:3] = add_rows(d_down.astype(jnp.float32))
-    small_ref[3:4] = add_rows(grad)
-    small_ref[5:6] = add_rows(grad * normed2)
-
-    def stores(c):
-        cols = pl.ds(pl.multiple_of(c * WIDE, WIDE), WIDE)
-        slabs = pl.ds(c * (UNITS * WIDE // FF), UNITS * WIDE // FF)
-        return (
-            pltpu.make_async_copy(dw1_ref.at[:, :, cols], dw1_hbm.at[:, :, cols], store_sem.at[0, c]),
-            pltpu.make_async_copy(dw2_ref.at[slabs], dw2_hbm.at[slabs], store_sem.at[1, c]),
-        )
-
-    def back_step(c, d_norm1):
-        cols = pl.ds(pl.multiple_of(c * WIDE, WIDE), WIDE)
-        slabs = pl.ds(c * (UNITS * WIDE // FF), UNITS * WIDE // FF)
-        d_active = outer_cols(d_down, w2_ref[cols, :])
-        d_up = (d_active * slope_ref[:, cols]).astype(jnp.bfloat16)
-        d_ffn_ref[:, cols] = add_rows(d_up.astype(jnp.float32))
-        dw2 = inner_rows(active_ref[:, cols], d_down)
-        dw2_ref[slabs] = dw2.reshape(UNITS * WIDE // FF, FF // UNITS, D).astype(jnp.bfloat16)
-        dw1 = inner_rows(lowered, d_up)
-        dw1_ref[:, :, cols] = dw1.reshape(UNITS, D // UNITS, WIDE).astype(jnp.bfloat16)
-        for cp in stores(c):
-            cp.start()
-        return d_norm1 + outer_cols(d_up, w1_ref[:, cols])
-
-    d_norm1 = lax.fori_loop(0, FF // WIDE, back_step, d_sum2)
-    small_ref[1:2] = add_rows(d_norm1)
-    small_ref[4:5] = add_rows(d_norm1 * normed1)
-    d_sum1 = normalize_back(d_norm1, normed1, inverse1, vec_ref[6:7])
-    d_sum1_ref[...] = d_sum1
-    d_attn = d_sum1.astype(jnp.bfloat16)
-    small_ref[0:1] = add_rows(d_attn.astype(jnp.float32))
-    d_mixed = outer_cols(d_attn, wo_ref[...])
-    for h in range(0, H, 2):
-        for t in range(BPD // 2):
-            part = slice(t * BLOCK, (t + 1) * BLOCK)
-            lanes = slice(h * HD, (h + 2) * HD)
-            a, b = unpack_pair(
-                d_mixed[2 * t * BLOCK : (2 * t + 1) * BLOCK, lanes],
-                d_mixed[(2 * t + 1) * BLOCK : (2 * t + 2) * BLOCK, lanes],
-                (BLOCK, 128),
-            )
-            box[h, part, :] = a.astype(jnp.bfloat16)
-            box[h + 1, part, :] = b.astype(jnp.bfloat16)
-
-    def late():
-        dwo_ref[...] = (
-            inner_rows(mixed_ref[...], d_attn)
-            .reshape(UNITS, D // UNITS, D)
-            .astype(jnp.bfloat16)
-        )
-        cp = pltpu.make_async_copy(dwo_ref, dwo_hbm, load_sem.at[0])
-        cp.start()
-        cp.wait()
-
-    send_to_owners(n, place, head, mine, ((box, d_heads),), sems_out, late)
-
-    def drain(c, _):
-        for cp in stores(c):
-            cp.wait()
-        return 0
-
-    lax.fori_loop(0, FF // WIDE, drain, 0)
-
-
-def middle(attended, rows, cotangent, first, second, vectors, ffn_bias):
-    n = lax.axis_size("seq")
-    low, full = jnp.bfloat16, jnp.float32
-    part = (TOK_SEQ // 2, 128)
-    units = [(UNITS, D // UNITS, FF), (UNITS, FF // UNITS, D), (UNITS, D // UNITS, D)]
-    shapes = [((TOK_SEQ, D), full), ((TOK_SEQ, D), full), ((n,) + part, low)]
-    shapes += [(u, low) for u in units] + [((8, D), full), ((1, FF), full)]
-    return pl.pallas_call(
-        functools.partial(mid_kernel, n),
-        out_shape=[jax.ShapeDtypeStruct(s, d) for s, d in shapes],
-        in_specs=[ANY, VMEM, VMEM, ANY, ANY, VMEM, VMEM],
-        out_specs=[VMEM, VMEM, ANY, ANY, ANY, ANY, VMEM, VMEM],
-        scratch_shapes=[
-            pltpu.VMEM((H,) + part, low),
-            pltpu.VMEM((H,) + part, low),
-            pltpu.VMEM((D, FF), low),
-            pltpu.VMEM((D, D), low),
-            pltpu.VMEM((FF, D), low),
-            pltpu.VMEM((TOK_SEQ, FF), full),
-            pltpu.VMEM((TOK_SEQ, FF), low),
-            *[pltpu.VMEM(u, low) for u in units],
-            pltpu.VMEM((TOK_SEQ, D), low),
-            pltpu.SemaphoreType.DMA((3,)),
-            pltpu.SemaphoreType.DMA((2, FF // WIDE)),
-            *exchange_sems(n),
-            *exchange_sems(n),
-        ],
-        compiler_params=pltpu.CompilerParams(
-            collective_id=3, has_side_effects=True, vmem_limit_bytes=58 << 20
-        ),
-        name="middle",
-    )(attended, rows, cotangent, first, second, vectors, ffn_bias)
 
 
 def add_flat(out_ref, base, srcs):
@@ -1127,6 +696,589 @@
         return out + [(11.1, along_b(1)), (11.2, along_b(0)), (12.5, along_a), (21, last)]
 
 
+class Spread:
+    def __init__(self, nz, me, order, at, sems, pending):
+        self.nz, self.me, self.order, self.at = nz, me, order, at
+        self.send, self.recv, self.csend, self.crecv = sems
+        self.pending = pending
+
+    @staticmethod
+    def semaphores(nz):
+        chips = 4 * nz
+        return [pltpu.SemaphoreType.DMA((chips, 4))] + [pltpu.SemaphoreType.DMA((chips,))] * 3
+
+    def copy(self, slot, send, recv, to):
+        ref = self.at(slot)
+        return pltpu.make_async_remote_copy(
+            src_ref=ref,
+            dst_ref=ref,
+            send_sem=send,
+            recv_sem=recv,
+            device_id=device(to),
+            device_id_type=MESH,
+        )
+
+    def start(self, cp, cond=None):
+        if cond is None:
+            cp.start()
+        else:
+            pl.when(cond)(cp.start)
+        self.pending.append((cp, cond))
+
+    def one(self, steps):
+        nz, me = self.nz, self.me
+        size = {"y": 2, "z": nz, "x": 2}
+        own = not any(steps)
+
+        def run():
+            src = dict(me)
+            for d, i in zip(self.order, steps):
+                src[d] = nearest(me[d], size[d], i)
+            c = chip(src, nz)
+            slot = c * 2 + me["c"]
+            if not own:
+                self.copy(slot, self.send.at[c, 0], self.recv.at[c], me).wait_recv()
+            stage = 2 if steps[2] else (1 if steps[1] else 0)
+            for t in range(stage, 3):
+                d = self.order[t]
+                onward = t == stage and not own
+                if d == "z":
+                    up, down = me["z"] < nz - 1, me["z"] > 0
+                    if onward:
+                        up = jnp.logical_and(up, src["z"] <= me["z"])
+                        down = jnp.logical_and(down, src["z"] >= me["z"])
+                    above = dict(me, z=jnp.minimum(me["z"] + 1, nz - 1))
+                    below = dict(me, z=jnp.maximum(me["z"] - 1, 0))
+                    self.start(self.copy(slot, self.send.at[c, 0], self.recv.at[c], above), up)
+                    self.start(self.copy(slot, self.send.at[c, 1], self.recv.at[c], below), down)
+                elif not (onward and steps[t]):
+                    way = 2 if d == "x" else 3
+                    to = dict(me, **{d: 1 - me[d]})
+                    self.start(self.copy(slot, self.send.at[c, way], self.recv.at[c], to))
+            sibling = dict(me, c=1 - me["c"])
+            self.start(self.copy(slot, self.csend.at[c], self.crecv.at[c], sibling))
+
+        return run
+
+    def steps(self):
+        size = {"y": 2, "z": self.nz, "x": 2}
+        n0, n1, n2 = (size[d] for d in self.order)
+        return [
+            (i0 + i1 + i2, self.one((i0, i1, i2)))
+            for i2 in range(n2)
+            for i1 in range(n1)
+            for i0 in range(n0)
+        ]
+
+    def finish(self):
+        def body(c, _):
+            slot = c * 2 + 1 - self.me["c"]
+            self.copy(slot, self.csend.at[c], self.crecv.at[c], self.me).wait_recv()
+            return 0
+
+        lax.fori_loop(0, 4 * self.nz, body, 0)
+
+
+def run_in_order(items, low, high):
+    steps = [(w, i, f) for i, item in enumerate(items) for w, f in item.steps()]
+    for w, _, f in sorted(steps, key=lambda s: s[:2]):
+        if low <= w < high:
+            f()
+
+
+def exchange_partners(me, nz):
+    partners = [dict(me, **{d: 1 - me[d]}) for d in ("c", "x", "y")]
+    step = 1
+    while step < nz:
+        partners.append(dict(me, z=me["z"] + step - 2 * step * ((me["z"] // step) % 2)))
+        step *= 2
+    return partners
+
+
+def vector_copy(i, value, land, sems, partners):
+    return pltpu.make_async_remote_copy(
+        src_ref=value.at[i],
+        dst_ref=land.at[i],
+        send_sem=sems[0].at[i],
+        recv_sem=sems[1].at[i],
+        device_id=device(partners[i]),
+        device_id_type=MESH,
+    )
+
+
+def greet_row_and_y(n, me, place_row):
+    bar = pltpu.get_barrier_semaphore()
+
+    def greet(k, _):
+        to = (place_row + 1 + k) % n
+        pl.semaphore_signal(bar, inc=1, device_id=(me["y"], to), device_id_type=MESH)
+        return 0
+
+    lax.fori_loop(0, n - 1, greet, 0)
+    pl.semaphore_signal(bar, inc=1, device_id=(1 - me["y"], place_row), device_id_type=MESH)
+    return lambda: pl.semaphore_wait(bar, n)
+
+
+UNIT = D // UNITS
+THIRD = FF // UNITS // 3
+QKV_ORDERS = (("z", "x", "y"), ("z", "y", "x"), ("x", "y", "z"))
+REST = (
+    ("second", THIRD, FF // UNITS, ("z", "y", "x")),
+    ("first", 0, UNIT, ("z", "x", "y")),
+    ("second", 0, THIRD, ("z", "x", "y")),
+)
+
+
+def from_flat(flat, cols, rows):
+    step = cols // 128
+    return [flat[pl.ds(k, rows, stride=step), :] for k in range(step)]
+
+
+def as_matrix(units):
+    count, rows, cols = units.shape
+    return units.astype(jnp.float32).reshape(count * rows, cols).astype(jnp.bfloat16)
+
+
+def kernel_planes():
+    seq = lax.axis_size("seq")
+    if lax.axis_size("dp") != 2 or 2 * seq != UNITS or seq % 4:
+        return 0
+    return seq // 4
+
+
+def front_kernel(n, nz, *refs):
+    rows_ref, cot_ref, picks_ref, vec_in, qkv_in, first_in, out_in, second_in = refs[:8]
+    (
+        result_ref,
+        d_sum1_ref,
+        kv_hbm,
+        q_hbm,
+        picks_hbm,
+        lse_ref,
+        d_heads,
+        dw1_hbm,
+        dw2_hbm,
+        dwo_hbm,
+        small_ref,
+        d_ffn_ref,
+        w_hbm,
+    ) = refs[8:21]
+    (
+        w_ref,
+        first_ref,
+        second_ref,
+        flat,
+        value,
+        land,
+        box_kv,
+        box_q,
+        kv_ref,
+        q_ref,
+        vk_ref,
+        picks_smem,
+        keys,
+        values,
+        attended,
+        inbox,
+        grad_box,
+        slope_ref,
+        active_ref,
+        dw1_ref,
+        dw2_ref,
+        dwo_ref,
+        mixed_ref,
+        load_sem,
+        store_sem,
+        keep_sem,
+        vsend,
+        vrecv,
+    ) = refs[21:49]
+    sems_qkv, sems_in, sems_out = refs[49:52], refs[52:55], refs[55:58]
+    rest = list(refs[58:])
+    place_row = lax.axis_index("seq")
+    head, mine = owned(place_row, n)
+    pending = []
+
+    if nz:
+        me = place(nz)
+        slot = index(me, nz)
+        hold = greet_row_and_y(n, me, place_row)
+        stages = 3 + (nz - 1).bit_length()
+
+        def take():
+            out = rest[:4]
+            del rest[:4]
+            return out
+
+        def widen(src):
+            count = src.shape[0]
+            flat[0:count] = src[...].astype(jnp.float32)
+
+        widen(qkv_in)
+        for j in range(3):
+            step = D // 128
+            for k in range(step):
+                col = flat[pl.ds(j * UNIT * step + k, UNIT, stride=step), :]
+                w_ref[slot * 3 + j, :, k * 128 : (k + 1) * 128] = col.astype(jnp.bfloat16)
+        value[0] = vec_in[...]
+        hold()
+        qkv_items = [
+            Spread(nz, me, order, lambda s, j=j: w_ref.at[s * 3 + j], take(), pending)
+            for j, order in enumerate(QKV_ORDERS)
+        ]
+        buffers = {"first": first_ref, "second": second_ref}
+
+        def part(kind, lo, hi):
+            ref = buffers[kind]
+            if hi - lo == ref.shape[1]:
+                return lambda s: ref.at[s]
+            return lambda s: ref.at[s, lo:hi]
+
+        rest_items = [
+            Spread(nz, me, order, part(kind, lo, hi), take(), pending)
+            for kind, lo, hi, order in REST
+        ]
+        partners = exchange_partners(me, nz)
+        vsems = (vsend, vrecv)
+        vector_copy(0, value, land, vsems, partners).start()
+        run_in_order(qkv_items, 0, 1)
+        for src, dst, at, cols, count in (
+            (first_in, first_ref, 0, FF, UNIT),
+            (out_in, first_ref, FF, D, UNIT),
+            (second_in, second_ref, 0, D, FF // UNITS),
+        ):
+            widen(src)
+            for k, col in enumerate(from_flat(flat, cols, count)):
+                dst[slot, :, at + k * 128 : at + (k + 1) * 128] = col.astype(jnp.bfloat16)
+
+        def vector_stage(i):
+            vector_copy(i, value, land, vsems, partners).wait_recv()
+            value[i + 1] = value[i] + land[i]
+            if i + 1 < stages:
+                vector_copy(i + 1, value, land, vsems, partners).start()
+
+        for depth in range(1, nz + 2):
+            vector_stage(min(depth - 1, stages)) if depth <= stages else None
+            run_in_order(qkv_items, depth, depth + 1)
+            if depth == 2:
+                run_in_order(rest_items, 0, 1)
+        for i in range(nz + 1, stages):
+            vector_stage(i)
+        for item in qkv_items:
+            item.finish()
+        vec = value.at[stages]
+    else:
+        greet_row(n, place_row, mine)
+        loads = [
+            pltpu.make_async_copy(src, dst, load_sem.at[i])
+            for i, (src, dst) in enumerate(
+                ((qkv_in, w_ref), (first_in, first_ref), (second_in, second_ref))
+            )
+        ]
+        for cp in loads:
+            cp.start()
+        for cp in loads:
+            cp.wait()
+        vec = vec_in
+
+    def rest_steps(low, high):
+        if nz:
+            run_in_order(rest_items, low, high)
+
+    rows = rows_ref[...]
+    left = low_lanes((TOK_SEQ, 128))
+    left_q = low_lanes((BLOCK, 128))
+    wide = 256
+    for g in range(D // wide):
+        cols = slice(g * wide, (g + 1) * wide)
+
+        def project(e):
+            return matmul(rows, as_matrix(w_ref[e * UNITS : (e + 1) * UNITS, :, cols]))
+
+        q = (project(0) + vec[0:1, cols]) * HD ** (-0.5)
+        k = project(1)
+        v = project(2) + vec[1:2, cols]
+        for p in range(wide // 128):
+            h = (g * wide + p * 128) // HD
+            lanes = slice(p * 128, (p + 1) * 128)
+            kp, vp, qp = k[:, lanes], v[:, lanes], q[:, lanes]
+            even, odd = jnp.where(left, kp, swap_halves(vp)), jnp.where(left, swap_halves(kp), vp)
+            for t in range(BPD):
+                part = slice(t * BLOCK, (t + 1) * BLOCK)
+                box_kv[h, t] = even[part].astype(jnp.bfloat16)
+                box_kv[h + 1, t] = odd[part].astype(jnp.bfloat16)
+            turned = swap_halves(qp)
+            for t in range(BPD // 2):
+                a = slice(2 * t * BLOCK, (2 * t + 1) * BLOCK)
+                b = slice((2 * t + 1) * BLOCK, (2 * t + 2) * BLOCK)
+                to = slice(t * BLOCK, (t + 1) * BLOCK)
+                box_q[h, to, :] = jnp.where(left_q, qp[a], turned[b]).astype(jnp.bfloat16)
+                box_q[h + 1, to, :] = jnp.where(left_q, turned[a], qp[b]).astype(jnp.bfloat16)
+    parcels = (
+        (box_kv, lambda s: kv_ref.at[pl.ds(s * BPD, BPD)]),
+        (box_q, lambda s: q_ref.at[s]),
+        (picks_ref, lambda s: picks_hbm.at[s]),
+    )
+    send_to_owners(
+        n,
+        place_row,
+        head,
+        mine,
+        parcels,
+        sems_qkv,
+        lambda: rest_steps(1, 3),
+        wait_sends=False,
+    )
+
+    keep = (
+        pltpu.make_async_copy(kv_ref, kv_hbm, keep_sem.at[0]),
+        pltpu.make_async_copy(q_ref, q_hbm, keep_sem.at[3]),
+    )
+    keep_w = pltpu.make_async_copy(w_ref, w_hbm, keep_sem.at[2])
+    keep_w.start()
+    groups = 4
+
+    @pl.when(mine)
+    def _():
+        for copy in keep:
+            copy.start()
+        cp = pltpu.make_async_copy(picks_hbm, picks_smem, keep_sem.at[1])
+        cp.start()
+        cp.wait()
+        turn_pairs(n, kv_ref, vk_ref)
+
+    def attend_some(k, _):
+        s = (place_row + 1 + k) % n
+        for t in range(BPD // 2):
+            i = s * (BPD // 2) + t
+            fill_pair(key_list(i, n, picks_smem), kv_ref, vk_ref, keys.at[t], values.at[t])
+        for t in range(BPD // 2):
+            i = s * (BPD // 2) + t
+            part = slice(t * BLOCK, (t + 1) * BLOCK)
+            query = two_blocks(q_ref[s, part, :])
+            scores = pair_scores(i, n, keys[t], query)
+            top = jnp.max(scores, axis=0, keepdims=True)
+            weights = jnp.exp(scores - top)
+            total = jnp.sum(weights, axis=0, keepdims=True)
+            probs = (weights * (1.0 / total)).astype(jnp.bfloat16)
+            full = inner_rows(probs, values[t])
+            attended[s, part, :] = jnp.where(left_q, full[:BLOCK], full[BLOCK:]).astype(
+                jnp.bfloat16
+            )
+            lse_ref[i] = top + jnp.log(total)
+
+        @pl.when(s != place_row)
+        def _():
+            pltpu.make_async_remote_copy(
+                src_ref=attended.at[s],
+                dst_ref=inbox.at[head],
+                send_sem=sems_in[0].at[0, s],
+                recv_sem=sems_in[1].at[0, head],
+                device_id=(lax.axis_index("dp"), s),
+                device_id_type=MESH,
+            ).start()
+
+        return 0
+
+    for g in range(groups):
+
+        @pl.when(mine)
+        def _():
+            lax.fori_loop(g * (n // groups), (g + 1) * (n // groups), attend_some, 0)
+
+        rest_steps(3 + g, 4 + g if g < groups - 1 else 99)
+
+    @pl.when(mine)
+    def _():
+        cp = pltpu.make_async_copy(attended.at[place_row], inbox.at[head], sems_in[2].at[0])
+        cp.start()
+        cp.wait()
+
+    if nz:
+        for item in rest_items:
+            item.finish()
+    wait_from_owners(n, place_row, head, attended, inbox, sems_in)
+
+    for h in range(0, H, 2):
+        for t in range(BPD // 2):
+            part = slice(t * BLOCK, (t + 1) * BLOCK)
+            a, b = unpack_pair(inbox[h, part, :], inbox[h + 1, part, :], (BLOCK, 128))
+            lanes = slice(h * HD, (h + 2) * HD)
+            mixed_ref[2 * t * BLOCK : (2 * t + 1) * BLOCK, lanes] = a.astype(jnp.bfloat16)
+            mixed_ref[(2 * t + 1) * BLOCK : (2 * t + 2) * BLOCK, lanes] = b.astype(jnp.bfloat16)
+    out_w = as_matrix(first_ref[:, :, FF : FF + D])
+    hidden1 = rows_ref[...].astype(jnp.float32) + matmul(mixed_ref[...], out_w) + vec[2:3]
+    normed_out1, normed1, inverse1 = normalize(hidden1, vec[6:7], vec[3:4])
+    lowered = normed_out1.astype(jnp.bfloat16)
+    per = UNITS * WIDE // FF
+
+    def second_rows(c):
+        return second_ref[pl.ds(c * per, per)].reshape(WIDE, D)
+
+    def up_step(c, hidden):
+        cols = pl.ds(pl.multiple_of(c * WIDE, WIDE), WIDE)
+        up = matmul(lowered, as_matrix(first_ref[:, :, cols])) + vec[pl.ds(8 + c, 1)]
+        square = up * up
+        inner = (2 / jnp.pi) ** 0.5 * (up + 0.044715 * up * square)
+        curve = jnp.tanh(inner)
+        active = (0.5 * up * (1 + curve)).astype(jnp.bfloat16)
+        slope_ref[:, cols] = 0.5 * (1 + curve) + 0.5 * up * (1 - curve * curve) * (
+            (2 / jnp.pi) ** 0.5 * (1 + 3 * 0.044715 * square)
+        )
+        active_ref[:, cols] = active
+        return hidden + matmul(active, second_rows(c))
+
+    hidden2 = lax.fori_loop(0, FF // WIDE, up_step, normed_out1 + vec[4:5])
+    result, normed2, inverse2 = normalize(hidden2, vec[7:8], vec[5:6])
+    result_ref[...] = result
+    grad = cot_ref[...].astype(jnp.float32)
+    d_sum2 = normalize_back(grad, normed2, inverse2, vec[7:8])
+    d_down = d_sum2.astype(jnp.bfloat16)
+
+    def add_rows(x):
+        return jnp.sum(x, axis=0, keepdims=True)
+
+    small_ref[2:3] = add_rows(d_down.astype(jnp.float32))
+    small_ref[3:4] = add_rows(grad)
+    small_ref[5:6] = add_rows(grad * normed2)
+
+    def stores(c):
+        cols = pl.ds(pl.multiple_of(c * WIDE, WIDE), WIDE)
+        slabs = pl.ds(c * per, per)
+        return (
+            pltpu.make_async_copy(dw1_ref.at[:, :, cols], dw1_hbm.at[:, :, cols], store_sem.at[0, c]),
+            pltpu.make_async_copy(dw2_ref.at[slabs], dw2_hbm.at[slabs], store_sem.at[1, c]),
+        )
+
+    def back_step(c, d_norm1):
+        cols = pl.ds(pl.multiple_of(c * WIDE, WIDE), WIDE)
+        d_active = outer_cols(d_down, second_rows(c))
+        d_up = (d_active * slope_ref[:, cols]).astype(jnp.bfloat16)
+        d_ffn_ref[:, cols] = add_rows(d_up.astype(jnp.float32))
+        dw2 = inner_rows(active_ref[:, cols], d_down)
+        dw2_ref[pl.ds(c * per, per)] = dw2.reshape(per, FF // UNITS, D).astype(jnp.bfloat16)
+        dw1 = inner_rows(lowered, d_up)
+        dw1_ref[:, :, cols] = dw1.reshape(UNITS, UNIT, WIDE).astype(jnp.bfloat16)
+        for cp in stores(c):
+            cp.start()
+        return d_norm1 + outer_cols(d_up, as_matrix(first_ref[:, :, cols]))
+
+    d_norm1 = lax.fori_loop(0, FF // WIDE, back_step, d_sum2)
+    small_ref[1:2] = add_rows(d_norm1)
+    small_ref[4:5] = add_rows(d_norm1 * normed1)
+    d_sum1 = normalize_back(d_norm1, normed1, inverse1, vec[6:7])
+    d_sum1_ref[...] = d_sum1
+    d_attn = d_sum1.astype(jnp.bfloat16)
+    small_ref[0:1] = add_rows(d_attn.astype(jnp.float32))
+    d_mixed = outer_cols(d_attn, as_matrix(first_ref[:, :, FF : FF + D]))
+    for h in range(0, H, 2):
+        for t in range(BPD // 2):
+            part = slice(t * BLOCK, (t + 1) * BLOCK)
+            lanes = slice(h * HD, (h + 2) * HD)
+            a, b = unpack_pair(
+                d_mixed[2 * t * BLOCK : (2 * t + 1) * BLOCK, lanes],
+                d_mixed[(2 * t + 1) * BLOCK : (2 * t + 2) * BLOCK, lanes],
+                (BLOCK, 128),
+            )
+            grad_box[h, part, :] = a.astype(jnp.bfloat16)
+            grad_box[h + 1, part, :] = b.astype(jnp.bfloat16)
+
+    store_out = pltpu.make_async_copy(dwo_ref, dwo_hbm, load_sem.at[0])
+
+    def late():
+        dwo = inner_rows(mixed_ref[...], d_attn).reshape(UNITS, UNIT, D)
+        dwo_ref[...] = dwo.astype(jnp.bfloat16)
+        store_out.start()
+
+    send_to_owners(n, place_row, head, mine, ((grad_box, lambda s: d_heads.at[s]),), sems_out, late)
+    store_out.wait()
+
+    def drain(c, _):
+        for cp in stores(c):
+            cp.wait()
+        return 0
+
+    lax.fori_loop(0, FF // WIDE, drain, 0)
+
+    @pl.when(mine)
+    def _():
+        for copy in keep:
+            copy.wait()
+
+    keep_w.wait()
+    finish_from_owners(n, place_row, head, mine, attended, inbox, sems_in)
+    finish_to_owners(n, place_row, head, parcels, sems_qkv)
+    if nz:
+        for i in range(stages):
+            vector_copy(i, value, land, vsems, partners).wait_send()
+    for cp, cond in pending:
+        if cond is None:
+            cp.wait_send()
+        else:
+            pl.when(cond)(cp.wait_send)
+
+
+def front(rows, cotangent, picks, vec, qkv, first, out, second, nz):
+    n = lax.axis_size("seq")
+    low, full = jnp.bfloat16, jnp.float32
+    picks = jnp.pad(picks.reshape(H, 1, BPD * 3), ((0, 0), (0, 7), (0, 128 - BPD * 3)))
+    part = (TOK_SEQ // 2, 128)
+    pairs = n * BPD // 2
+    units = [(UNITS, UNIT, FF), (UNITS, FF // UNITS, D), (UNITS, UNIT, D)]
+    shapes = [((TOK_SEQ, D), full), ((TOK_SEQ, D), full)]
+    shapes += [((n * BPD, BLOCK, 128), low), ((n,) + part, low)]
+    shapes += [((n, 8, 128), jnp.int32), ((pairs, 1, 128), full), ((n,) + part, low)]
+    shapes += [(u, low) for u in units] + [((8, D), full), ((1, FF), full)]
+    shapes += [((3 * UNITS, UNIT, D), low)]
+    stages = 3 + (max(nz, 1) - 1).bit_length()
+    where = VMEM if nz else ANY
+    extra = []
+    for _ in range(6 if nz else 0):
+        extra += Spread.semaphores(nz)
+    return pl.pallas_call(
+        functools.partial(front_kernel, n, nz),
+        out_shape=[jax.ShapeDtypeStruct(s, d) for s, d in shapes],
+        in_specs=[VMEM, VMEM, ANY, VMEM, where, where, where, where],
+        out_specs=[VMEM, VMEM, ANY, ANY, ANY, VMEM, ANY, ANY, ANY, ANY, VMEM, VMEM, ANY],
+        scratch_shapes=[
+            pltpu.VMEM((3 * UNITS, UNIT, D), low),
+            pltpu.VMEM((UNITS, UNIT, FF + D), low),
+            pltpu.VMEM((UNITS, FF // UNITS, D), low),
+            pltpu.VMEM((UNIT * FF // 128, 128), full),
+            pltpu.VMEM((stages + 1, 16, D), full),
+            pltpu.VMEM((stages, 16, D), full),
+            pltpu.VMEM((H, BPD, BLOCK, 128), low),
+            pltpu.VMEM((H,) + part, low),
+            pltpu.VMEM((n * BPD, BLOCK, 128), low),
+            pltpu.VMEM((n,) + part, low),
+            pltpu.VMEM((n * BPD, BLOCK, 128), low),
+            pltpu.SMEM((n, 8, 128), jnp.int32),
+            pltpu.VMEM((BPD // 2, 8 * BLOCK, 128), low),
+            pltpu.VMEM((BPD // 2, 8 * BLOCK, 128), low),
+            pltpu.VMEM((n,) + part, low),
+            pltpu.VMEM((H,) + part, low),
+            pltpu.VMEM((H,) + part, low),
+            pltpu.VMEM((TOK_SEQ, FF), full),
+            pltpu.VMEM((TOK_SEQ, FF), low),
+            *[pltpu.VMEM(u, low) for u in units],
+            pltpu.VMEM((TOK_SEQ, D), low),
+            pltpu.SemaphoreType.DMA((3,)),
+            pltpu.SemaphoreType.DMA((2, FF // WIDE)),
+            pltpu.SemaphoreType.DMA((4,)),
+            pltpu.SemaphoreType.DMA((stages,)),
+            pltpu.SemaphoreType.DMA((stages,)),
+            *exchange_sems(n, 3),
+            *exchange_sems(n),
+            *exchange_sems(n),
+            *extra,
+        ],
+        compiler_params=pltpu.CompilerParams(
+            collective_id=0, has_side_effects=True, vmem_limit_bytes=60 << 20
+        ),
+        name="front",
+    )(rows, cotangent, picks, vec, qkv, first, out, second)
+
+
 FFN_KINDS = (
     ("expand", 0, D // UNITS, ("x", "y"), False),
     ("contract", FF // UNITS // 3, FF // UNITS, ("y", "x"), False),
@@ -1139,7 +1291,6 @@
     (2, ("x", "y"), True),
 )
 QKV_UNITS = 3 * UNITS
-UNIT = D // UNITS
 
 
 def finish_kernel(n, nz, *refs):
@@ -1289,7 +1440,7 @@
             f()
     d_tokens = d_sum1_ref[...]
     for e in range(3):
-        d_tokens = d_tokens + outer_cols(proj[e], w_ref[e])
+        d_tokens = d_tokens + outer_cols(proj[e], as_matrix(w_ref[e * UNITS : (e + 1) * UNITS]))
     d_tokens_ref[...] = d_tokens
     stage = 0
     for w, f in ordered(qkv):
@@ -1335,7 +1486,7 @@
         scratch_shapes=[
             pltpu.VMEM((H, MSG, 128), low),
             pltpu.VMEM((3, TOK_SEQ, D), low),
-            pltpu.VMEM((3, D, D), low),
+            pltpu.VMEM((QKV_UNITS, UNIT, D), low),
             pltpu.VMEM(d_expand.shape, low),
             pltpu.VMEM(d_contract.shape, low),
             pltpu.VMEM(d_out.shape, low),
@@ -1377,23 +1528,51 @@
     random_blocks,
     cotangent,
 ):
-    qkv, first, second, vectors, ffn = gather_weights(
-        qkv_weight, out_weight, expand_weight, contract_weight, bias_vectors, gain_vectors, ffn_bias
+    shards = lax.axis_size("dp") * lax.axis_size("seq")
+    me = lax.axis_index("dp") * lax.axis_size("seq") + lax.axis_index("seq")
+    planes = kernel_planes()
+    rows = tokens.reshape(TOK_SEQ, D)
+    weights = (qkv_weight, expand_weight, out_weight, contract_weight)
+    vectors = (bias_vectors, gain_vectors, ffn_bias)
+    if planes:
+        placed = [
+            lax.dynamic_update_slice(
+                jnp.zeros((v.size * shards,), jnp.float32), v.astype(jnp.float32), (me * v.size,)
+            )
+            for v in vectors
+        ]
+        qkv, first, out, second = [w.reshape(-1, 128) for w in weights]
+    else:
+        gather = functools.partial(lax.all_gather, axis_name=("dp", "seq"), axis=0, tiled=True)
+        placed = [gather(v).astype(jnp.float32) for v in vectors]
+        qkv, first, out, second = [gather(w) for w in weights]
+        qkv = qkv.reshape(3 * UNITS, UNIT, D)
+        first, out = first.reshape(UNITS, UNIT, FF), out.reshape(UNITS, UNIT, D)
+        first = jnp.concatenate([first, out], axis=2)
+        second = second.reshape(UNITS, FF // UNITS, D)
+    vec = jnp.pad(jnp.concatenate(placed).reshape(-1, D), ((0, 4), (0, 0)))
+    (
+        result,
+        d_sum1,
+        kv,
+        queries,
+        picks,
+        lse,
+        d_heads,
+        d_expand,
+        d_contract,
+        d_out,
+        small,
+        d_ffn,
+        w_all,
+    ) = front(
+        rows, cotangent.reshape(TOK_SEQ, D), random_blocks, vec, qkv, first, out, second, planes
     )
-    planes = kernel_planes((qkv_weight, out_weight, expand_weight, contract_weight))
-    rows = tokens.reshape(TOK_SEQ, D)
-    kvq, picks = project_and_send(rows, qkv, vectors, random_blocks)
-    attended, lse = attend_heads(kvq, picks)
-    result, d_sum1, d_heads, d_expand, d_contract, d_out, small, d_ffn = middle(
-        attended, rows, cotangent.reshape(TOK_SEQ, D), first, second, vectors, ffn
-    )
-    d_heads = attend_heads_back(kvq, picks, lse, d_heads)
-    shards = lax.axis_size("dp") * lax.axis_size("seq")
+    d_heads = attend_heads_back(kv, queries, picks, lse, d_heads)
     if planes:
         d_tokens, d_qkv, d_out, d_expand, d_contract, totals = finish(
-            d_heads, rows, qkv, d_sum1, d_expand, d_contract, d_out, small, d_ffn, planes
+            d_heads, rows, w_all, d_sum1, d_expand, d_contract, d_out, small, d_ffn, planes
         )
-        me = lax.axis_index("dp") * lax.axis_size("seq") + lax.axis_index("seq")
         vectors = (totals[0:6], totals[6:8], totals[8 : 8 + FF // D])
         vectors = [
             lax.dynamic_slice(v.reshape(-1), (me * (v.size // shards),), (v.size // shards,))
@@ -1406,7 +1585,7 @@
         d_proj = jnp.concatenate([d_query[None], d_pair], axis=0)
         d_qkv = jnp.einsum("rd,erf->edf", rows, d_proj, preferred_element_type=jnp.float32)
         d_tokens = d_sum1 + jnp.einsum(
-            "erf,edf->rd", d_proj, qkv, preferred_element_type=jnp.float32
+            "erf,edf->rd", d_proj, qkv.reshape(3, D, D), preferred_element_type=jnp.float32
         )
         d_bias_q = jnp.sum(d_query.astype(jnp.float32), axis=0)
         d_bias_v = jnp.sum(d_pair[1].astype(jnp.float32), axis=0)

time: 328 us -> 287 us (0.88)
  Pallas kernels: 297 us -> 269 us
  local copies, waits for them, and re-layouts: 24.1 us -> 12.9 us
    pallas_call x4 -> x1, Pallas kernels: 161 us -> 140 us  [front(): pl.pallas_call(functools.partial(front_kernel, n, nz), out_shape=[jax.Sha...]
    unnamed x25 -> x15, local copies, waits for them, and re-layouts: 13.6 us -> 7.4 us
    reshape x8 -> x2, local copies, waits for them, and re-layouts: 6.13 us -> 0.11 us  [the longest x1 0.1 us: front(): picks.reshape(H, 1, BPD * 3)]
    pallas_call x1, Pallas kernels: 25.3 us -> 20.8 us  [attend_heads_back(): pl.pallas_call(functools.partial(attend_back_kernel, n), out_shape=jax.Sh...]
where the time goes in v5:
time: 287 us; the launch traced here: 285 us
  Pallas kernels  269 us (94%)
  local copies, waits for them, and re-layouts  12.9 us (4%)
    pallas_call x1, Pallas kernels, front(): pl.pallas_call(functools.partial(front_kernel, n, nz), out_shape=[jax.Sha...  140 us
    pallas_call x1, Pallas kernels, finish(): pl.pallas_call(functools.partial(finish_kernel, n, nz), out_shape=[jax.Sh...  109 us
    pallas_call x1, Pallas kernels, attend_heads_back(): pl.pallas_call(functools.partial(attend_back_kernel, n), out_shape=jax.Sh...  20.8 us
    unnamed x15, local copies, waits for them, and re-layouts  7.4 us

profile of v5, /device:TPU:8, one launch (start us, length us, event | category | flops | bytes accessed | tf_op | source)
XLA Modules:
  0.0 284.9 jit_solution(13052014492725691337)
XLA Ops:
  0.6 0.7 copy.20
  1.3 0.1 copy.21
  1.4 0.7 convert_dynamic-update-slice_fusion.2
  2.2 0.8 convert_dynamic-update-slice_fusion.1
  3.0 0.8 convert_dynamic-update-slice_fusion
  3.7 0.6 pad.9.refs_3_
  4.4 0.6 pad.8.refs_2_
  5.0 139.5 %front.1 = (f32[256,768]{1,0:T(8,128)}, f32[256,768]{1,0:T(8,128)}, bf16[64,64,128]{2,1,0:T(8,128)(2,1)}, bf16[16,128,128]{2,1,0:T(8,128)(2,1)}, s32[16,8,128]{2...) custom-call(bf16[256,768]{1,0:T(8,128)(2,1)} %bitcast.13, ...), custom_call_target="tpu_custom_call" | custom-call | tf_op jit(solution)/shard_map/front/pallas_call | solution.py:1238
  144.5 20.8 %attend_heads_back.1.refs_0_ = bf16[16,384,128]{2,1,0:T(8,128)(2,1)} custom-call(bf16[64,64,128]{2,1,0:T(8,128)(2,1)} %get-tuple-element.29.kv_ref, bf16[16,128,128]{2,1,0:T(8,128)(2,1)} %get-tuple-element.30.q_ref, s32[16,8,128]{2,1,0:T(8,128)} %get-tuple-element.31.picks_ref, f32[32,1,128]{2,1,0:T(1,128)} %get-tuple-element.32.lse_ref, ...), custom_call_target="tpu_custom_call" | custom-call | tf_op jit(solution)/shard_map/attend_heads_back/pallas_call | solution.py:411
  165.4 0.0 copy-start
  165.4 108.7 %finish.1 = (f32[256,768]{1,0:T(8,128)}, f32[432,128]{1,0:T(8,128)}, f32[144,128]{1,0:T(8,128)}, f32[576,128]{1,0:T(8,128)}, f32[576,128]{1,0:T(8,128)}, /*index=5*/f32[16,768]{1,0:T(8,128)}) custom-call(bf16[16,384,128]{2,1,0:T(8,128)(2,1)} %attend_heads_back.1.refs_0_, bf16[256,768]{1,0:T(8,128)(2,1)} %bitcast.14, ...), custom_call_target="tpu_custom_call" | custom-call | tf_op jit(solution)/shard_map/finish/pallas_call | solution.py:1481
  274.0 0.0 copy-start.3
  274.1 0.0 copy-start.2
  274.1 0.0 copy-start.1
  274.1 0.8 slice.10
  274.9 0.6 dynamic_slice.10
  275.5 0.7 slice.11
  276.2 0.7 slice.9
  277.0 0.6 dynamic_slice.9
  277.6 0.6 dynamic_slice.11
  278.2 0.0 copy-done
  278.2 0.9 copy.31
  279.1 2.1 copy.32
  281.1 1.6 copy.33
  282.8 0.0 copy-done.3
  282.8 0.6 copy.34
  283.4 0.0 copy-done.2
  283.4 0.7 copy.35
  284.2 0.0 copy-done.1
  284.2 0.7 copy.36
  (8 shorter events, 0.1 us)
Async XLA Ops:
  165.4 112.8 %copy-start = (f32[256,768]{1,0:T(8,128)S(1)}, f32[256,768]{1,0:T(8,128)}, u32[]{:S(2)}) copy-start(f32[256,768]{1,0:T(8,128)} %get-tuple-element.28) | copy-start | bytes 2359300
  274.0 8.7 %copy-start.3 = (f32[144,128]{1,0:T(8,128)S(1)}, f32[144,128]{1,0:T(8,128)}, u32[]{:S(2)}) copy-start(f32[144,128]{1,0:T(8,128)} %get-tuple-element.43) | copy-start | bytes 221188
  274.1 9.4 %copy-start.2 = (f32[576,128]{1,0:T(8,128)S(1)}, f32[576,128]{1,0:T(8,128)}, u32[]{:S(2)}) copy-start(f32[576,128]{1,0:T(8,128)} %get-tuple-element.44) | copy-start | bytes 884740
  274.1 10.1 %copy-start.1 = (f32[576,128]{1,0:T(8,128)S(1)}, f32[576,128]{1,0:T(8,128)}, u32[]{:S(2)}) copy-start(f32[576,128]{1,0:T(8,128)} %get-tuple-element.45) | copy-start | bytes 884740

commit v6 on v5

--- a/solution.py
+++ b/solution.py
@@ -103,30 +103,6 @@
     return jnp.minimum(head, H - 1), jnp.logical_and(head < H, owner(head, n) == place)
 
 
-def greet_senders(n, place, mine, to_owners):
-    row = lax.axis_index("dp")
-    bar = pltpu.get_barrier_semaphore()
-
-    def signal(to):
-        @pl.when(to != place)
-        def _():
-            pl.semaphore_signal(bar, inc=1, device_id=(row, to), device_id_type=MESH)
-
-    if to_owners:
-
-        @pl.when(mine)
-        def _():
-            lax.fori_loop(0, n, lambda s, _: (signal(s), 0)[1], 0)
-
-        pl.semaphore_wait(bar, H - jnp.where(mine, 1, 0))
-    else:
-        lax.fori_loop(0, H, lambda h, _: (signal(owner(h, n)), 0)[1], 0)
-
-        @pl.when(mine)
-        def _():
-            pl.semaphore_wait(bar, n - 1)
-
-
 def walk_to_owners(n, place, head, pairs, sems, act):
     row = lax.axis_index("dp")
 
@@ -242,12 +218,6 @@
         walk_from_owners(n, place, head, src, dst, sems, lambda cp: cp.wait_send())
 
 
-def send_from_owners(n, place, head, mine, src, dst, sems):
-    start_from_owners(n, place, head, mine, src, dst, sems)
-    wait_from_owners(n, place, head, src, dst, sems)
-    finish_from_owners(n, place, head, mine, src, dst, sems)
-
-
 def swap_halves(tile):
     return pltpu.roll(tile, HD, tile.ndim - 1)
 
@@ -268,26 +238,6 @@
 VMEM = pl.BlockSpec(memory_space=pltpu.VMEM)
 SMEM = pl.BlockSpec(memory_space=pltpu.SMEM)
 MSG = TOK_SEQ + TOK_SEQ // 2
-
-
-def from_owners_kernel(n, src, dst, *sems):
-    place = lax.axis_index("seq")
-    head, mine = owned(place, n)
-    greet_senders(n, place, mine, False)
-    send_from_owners(n, place, head, mine, src, dst, sems)
-
-
-def exchange(kernel, slots, messages, ident, name):
-    n = lax.axis_size("seq")
-    return pl.pallas_call(
-        functools.partial(kernel, n),
-        out_shape=jax.ShapeDtypeStruct((slots,) + messages.shape[1:], messages.dtype),
-        in_specs=[ANY],
-        out_specs=ANY,
-        scratch_shapes=exchange_sems(n),
-        compiler_params=pltpu.CompilerParams(collective_id=ident, has_side_effects=True),
-        name=name,
-    )(messages)
 
 
 def key_list(i, n, picks_ref):
@@ -345,86 +295,30 @@
     lax.fori_loop(0, n, body, 0)
 
 
-def attend_back_kernel(
-    n, kv_ref, q_ref, picks_ref, lse_ref, grad_ref, out_ref, vk_ref, keys, values, sum_k, sum_v
-):
-    place = lax.axis_index("seq")
-    head, mine = owned(place, n)
-
-    @pl.when(mine)
-    def _():
-        turn_pairs(n, kv_ref, vk_ref)
-
-        def clear(s, _):
-            for t in range(BPD):
-                sum_k[s * BPD + t] = jnp.zeros((BLOCK, 128), jnp.float32)
-                sum_v[s * BPD + t] = jnp.zeros((BLOCK, 128), jnp.float32)
-            return 0
-
-        lax.fori_loop(0, n, clear, 0)
-        left = low_lanes((BLOCK, 128))
-
-        def body(s, _):
-            lists = [key_list(s * (BPD // 2) + t, n, picks_ref) for t in range(BPD // 2)]
-            for t in range(BPD // 2):
-                fill_pair(lists[t], kv_ref, vk_ref, keys.at[t], values.at[t])
-            parts = []
-            for t in range(BPD // 2):
-                i = s * (BPD // 2) + t
-                part = slice(t * BLOCK, (t + 1) * BLOCK)
-                query = two_blocks(q_ref[s, part, :])
-                grad = two_blocks(grad_ref[s, part, :])
-                probs = jnp.exp(pair_scores(i, n, keys[t], query) - lse_ref[i])
-                d_probs = outer_cols(values[t], grad)
-                rows = jnp.sum(probs * d_probs, axis=0, keepdims=True)
-                d_scores = (probs * (d_probs - rows)).astype(jnp.bfloat16)
-                d_values = matmul(probs.astype(jnp.bfloat16), grad)
-                d_keys = matmul(d_scores, query)
-                full = inner_rows(d_scores, keys[t]) * HD ** (-0.5)
-                to = slice(TOK_SEQ + t * BLOCK, TOK_SEQ + (t + 1) * BLOCK)
-                out_ref[s, to, :] = jnp.where(left, full[:BLOCK], full[BLOCK:]).astype(jnp.bfloat16)
-                parts.append((d_keys, d_values))
-            for t in range(BPD // 2):
-                for j in range(8):
-                    part = slice(j * BLOCK, (j + 1) * BLOCK)
-                    for u in range(2):
-                        b = lists[t][u][j]
-                        lanes = slice(u * HD, (u + 1) * HD)
-                        sum_k[b, :, lanes] += parts[t][0][part, lanes]
-                        sum_v[b, :, lanes] += parts[t][1][part, lanes]
-            return 0
-
-        lax.fori_loop(0, n, body, 0)
-
-        def close(s, _):
-            for t in range(BPD):
-                k, v = sum_k[s * BPD + t], sum_v[s * BPD + t]
-                both = jnp.where(left, k + swap_halves(k), v + swap_halves(v))
-                out_ref[s, t * BLOCK : (t + 1) * BLOCK, :] = both.astype(jnp.bfloat16)
-            return 0
-
-        lax.fori_loop(0, n, close, 0)
-
-
-def attend_heads_back(kv, queries, picks, lse, grad):
-    n = lax.axis_size("seq")
-    return pl.pallas_call(
-        functools.partial(attend_back_kernel, n),
-        out_shape=jax.ShapeDtypeStruct((n, MSG, 128), jnp.bfloat16),
-        in_specs=[VMEM, VMEM, SMEM, VMEM, VMEM],
-        out_specs=VMEM,
-        scratch_shapes=[
-            pltpu.VMEM((n * BPD, BLOCK, 128), jnp.bfloat16),
-            pltpu.VMEM((BPD // 2, 8 * BLOCK, 128), jnp.bfloat16),
-            pltpu.VMEM((BPD // 2, 8 * BLOCK, 128), jnp.bfloat16),
-            pltpu.VMEM((n * BPD, BLOCK, 128), jnp.float32),
-            pltpu.VMEM((n * BPD, BLOCK, 128), jnp.float32),
-        ],
-        compiler_params=pltpu.CompilerParams(vmem_limit_bytes=56 << 20),
-        name="attend_heads_back",
-    )(kv, queries, picks, lse, grad)
-
-
+def chain_table(n, place, picks_vmem, picks_smem, links_ref):
+    none = PICKS * n
+    lane = lax.broadcasted_iota(jnp.int32, (n, 128), 1)
+    turn = (lax.broadcasted_iota(jnp.int32, (n, 128), 0) + 2 * n - place - 1) % n
+    order = jnp.where(lane < PICKS, turn * PICKS + lane, -1)
+    picks = picks_vmem[:, 0, :]
+    blocks = lax.broadcasted_iota(jnp.int32, (8, 128), 1)
+
+    def body(k, tables):
+        before, final = tables
+        s = (place + 1 + k) % n
+        for j in range(PICKS):
+            pick, e = picks_smem[s, 0, j], k * PICKS + j
+            before = jnp.where(jnp.logical_and(picks == pick, order > e), e, before)
+            final = jnp.where(blocks == pick, e, final)
+        return before, final
+
+    start = (jnp.full((n, 128), none, jnp.int32), jnp.full((8, 128), none, jnp.int32))
+    before, final = lax.fori_loop(0, n, body, start)
+    links_ref[0:n] = before
+    links_ref[n : n + 8] = final
+
+
+PICKS = 3 * BPD
 UNITS = 32
 WIDE = 768
 
@@ -452,41 +346,40 @@
     return (jnp.where(left, a, swap_halves(b)), jnp.where(left, swap_halves(a), b))
 
 
-def add_flat(out_ref, base, srcs):
+def add_flat(out_ref, base, srcs, width=None):
     rows, cols = srcs[0].shape
+    width = width or cols
     for k in range(cols // 128):
         lanes = slice(k * 128, (k + 1) * 128)
         total = srcs[0][:, lanes].astype(jnp.float32)
         for s in srcs[1:]:
             total = total + s[:, lanes].astype(jnp.float32)
-        out_ref[pl.ds(base + k, rows, stride=cols // 128), :] = total
+        out_ref[pl.ds(base + k, rows, stride=width // 128), :] = total
 
 
 class Reduction:
-    def __init__(self, nz, me, links, z_first, own, give, emit, bufs, sems, pending):
-        self.nz, self.me, self.links, self.z_first = nz, me, links, z_first
+    def __init__(self, nz, me, links, direct, own, give, emit, bufs, sems, pending):
+        self.nz, self.me, self.links, self.direct = nz, me, links, direct
         self.own, self.give, self.emit = own, give, emit
         self.rc, self.ra, self.rb, self.below, self.above = bufs
         self.csend, self.crecv, self.send, self.recv = sems
         self.pending = pending
 
     @staticmethod
-    def buffers(nz, slab, z_first):
-        chips = 4 * nz
-        counts = (chips, 2, 2, chips, chips) if z_first else (chips, nz, 2 * nz, nz, nz)
+    def buffers(nz, slab):
+        counts = (4 * nz, nz, 2 * nz, nz, nz)
         return [pltpu.VMEM((c,) + slab, jnp.bfloat16) for c in counts]
 
     @staticmethod
-    def semaphores(nz, z_first):
-        count = 8 * nz + 3 if z_first else 5 * nz
-        return [pltpu.SemaphoreType.DMA((c,)) for c in (4 * nz, 4 * nz, count, count)]
-
-    def start(self, src, dst, slot, to, cond=None):
+    def semaphores(nz):
+        return [pltpu.SemaphoreType.DMA((c * nz,)) for c in (4, 4, 5, 5)]
+
+    def start(self, src, dst, slot, to, cond=None, there=None):
         cp = pltpu.make_async_remote_copy(
             src_ref=src,
             dst_ref=dst,
             send_sem=self.send.at[slot],
-            recv_sem=self.recv.at[slot],
+            recv_sem=self.recv.at[slot if there is None else there],
             device_id=device(to),
             device_id_type=MESH,
         )
@@ -521,10 +414,7 @@
     def hand_over(self):
         nz = self.nz
         zs = sorted(range(nz), key=lambda z: -abs(2 * z - nz + 1))
-        if self.z_first:
-            order = [(z, fa, fb) for z in zs for fa, fb in ((1, 1), (0, 1), (1, 0), (0, 0))]
-        else:
-            order = [(z, fa, fb) for fb in (1, 0) for fa in (1, 0) for z in zs]
+        order = [(z, fa, fb) for fb in (1, 0) for fa in (1, 0) for z in zs]
 
         def one(z, fa, fb):
             def run():
@@ -586,9 +476,6 @@
         return out
 
     def steps(self):
-        return self.steps_z_first() if self.z_first else self.steps_z_last()
-
-    def steps_z_last(self):
         nz, me = self.nz, self.me
         zs = sorted(range(nz), key=lambda z: -abs(2 * z - nz + 1))
 
@@ -622,6 +509,18 @@
                 self.arrived(self.rb.at[s], self.recv.at[s])
                 self.arrived(self.ra.at[z], self.recv.at[2 * nz + z])
                 srcs += [self.rb.at[s], self.ra.at[z]]
+                if self.direct:
+                    mz = me["z"]
+
+                    @pl.when(mz != z)
+                    def _():
+                        combine(self.rc.at[p], srcs)
+
+                    to = dict(me, z=z)
+                    self.start(
+                        self.rc.at[p], self.below.at[mz], 3 * nz + z, to, mz != z, 3 * nz + mz
+                    )
+                    return
                 bref, aref = self.below.at[z], self.above.at[z]
                 self.relay(z, p, srcs, bref, aref, 3 * nz + z, 4 * nz + z)
 
@@ -635,6 +534,14 @@
                     p = self.piece(z, self.flip(0, 0), self.flip(1, 0))
                     s = z * 2 + self.flip(0, 0)
                     srcs = [self.own(p), self.rc.at[p], self.rb.at[s], self.ra.at[z]]
+                    if self.direct:
+                        for other in range(nz):
+                            if other != z:
+                                ref = self.below.at[other]
+                                self.arrived(ref, self.recv.at[3 * nz + other])
+                                srcs.append(ref)
+                        self.emit(srcs)
+                        return
                     bref, aref = self.below.at[z], self.above.at[z]
                     self.emit(srcs + self.ends(z, bref, aref, 3 * nz + z, 4 * nz + z))
 
@@ -643,57 +550,6 @@
         out += [(5.5 + i, along_a(z)) for i, z in enumerate(zs)]
         out += [(9.5 + i, chain(z)) for i, z in enumerate(zs)]
         return out + [(20, last)]
-
-    def steps_z_first(self):
-        nz, me = self.nz, self.me
-        zs = sorted(range(nz), key=lambda z: -abs(2 * z - nz + 1))
-        s0 = 8 * nz
-
-        def slots(z, fa, fb):
-            q = self.flip(0, fa) * 2 + self.flip(1, fb)
-            return self.below.at[z * 4 + q], self.above.at[z * 4 + q], z * 4 + q, 4 * nz + z * 4 + q
-
-        def chain(z, fa, fb):
-            def run():
-                p = self.piece(z, self.flip(0, fa), self.flip(1, fb))
-                self.relay(z, p, self.mine(p), *slots(z, fa, fb))
-
-            return run
-
-        def settle(fa, fb):
-            for z in range(nz):
-
-                @pl.when(me["z"] == z)
-                def _():
-                    p = self.piece(z, self.flip(0, fa), self.flip(1, fb))
-                    srcs = [self.own(p), self.rc.at[p]] + self.ends(z, *slots(z, fa, fb))
-                    combine(self.rc.at[p], srcs)
-
-            return self.rc.at[self.piece(me["z"], self.flip(0, fa), self.flip(1, fb))]
-
-        def along_b(fa):
-            def run():
-                self.start(settle(fa, 1), self.rb.at[fa], s0 + fa, self.across(1))
-
-            return run
-
-        def along_a():
-            ref = settle(1, 0)
-            self.arrived(self.rb.at[1], self.recv.at[s0 + 1])
-            combine(self.ra.at[0], [ref, self.rb.at[1]])
-            self.start(self.ra.at[0], self.ra.at[1], s0 + 2, self.across(0))
-
-        def last():
-            ref = settle(0, 0)
-            self.arrived(self.rb.at[0], self.recv.at[s0])
-            self.arrived(self.ra.at[1], self.recv.at[s0 + 2])
-            self.emit([ref, self.rb.at[0], self.ra.at[1]])
-
-        out = []
-        for i, z in enumerate(zs):
-            for m, (fa, fb) in enumerate(((1, 1), (0, 1), (1, 0), (0, 0))):
-                out.append((1 + i * 2.5 + m * 0.5, chain(z, fa, fb)))
-        return out + [(11.1, along_b(1)), (11.2, along_b(0)), (12.5, along_a), (21, last)]
 
 
 class Spread:
@@ -862,7 +718,8 @@
         small_ref,
         d_ffn_ref,
         w_hbm,
-    ) = refs[8:21]
+        links_hbm,
+    ) = refs[8:22]
     (
         w_ref,
         first_ref,
@@ -892,9 +749,11 @@
         keep_sem,
         vsend,
         vrecv,
-    ) = refs[21:49]
-    sems_qkv, sems_in, sems_out = refs[49:52], refs[52:55], refs[55:58]
-    rest = list(refs[58:])
+        links_ref,
+        picks_vmem,
+    ) = refs[22:52]
+    sems_qkv, sems_in, sems_out = refs[52:55], refs[55:58], refs[58:61]
+    rest = list(refs[61:])
     place_row = lax.axis_index("seq")
     head, mine = owned(place_row, n)
     pending = []
@@ -1036,16 +895,24 @@
     )
     keep_w = pltpu.make_async_copy(w_ref, w_hbm, keep_sem.at[2])
     keep_w.start()
+    keep_links = pltpu.make_async_copy(links_ref, links_hbm, keep_sem.at[4])
     groups = 4
 
     @pl.when(mine)
     def _():
         for copy in keep:
             copy.start()
-        cp = pltpu.make_async_copy(picks_hbm, picks_smem, keep_sem.at[1])
-        cp.start()
-        cp.wait()
+        copies = (
+            pltpu.make_async_copy(picks_hbm, picks_smem, keep_sem.at[1]),
+            pltpu.make_async_copy(picks_hbm, picks_vmem, keep_sem.at[5]),
+        )
+        for cp in copies:
+            cp.start()
+        for cp in copies:
+            cp.wait()
         turn_pairs(n, kv_ref, vk_ref)
+        chain_table(n, place_row, picks_vmem, picks_smem, links_ref)
+        keep_links.start()
 
     def attend_some(k, _):
         s = (place_row + 1 + k) % n
@@ -1204,6 +1071,7 @@
     def _():
         for copy in keep:
             copy.wait()
+        keep_links.wait()
 
     keep_w.wait()
     finish_from_owners(n, place_row, head, mine, attended, inbox, sems_in)
@@ -1229,7 +1097,7 @@
     shapes += [((n * BPD, BLOCK, 128), low), ((n,) + part, low)]
     shapes += [((n, 8, 128), jnp.int32), ((pairs, 1, 128), full), ((n,) + part, low)]
     shapes += [(u, low) for u in units] + [((8, D), full), ((1, FF), full)]
-    shapes += [((3 * UNITS, UNIT, D), low)]
+    shapes += [((3 * UNITS, UNIT, D), low), ((n + 8, 128), jnp.int32)]
     stages = 3 + (max(nz, 1) - 1).bit_length()
     where = VMEM if nz else ANY
     extra = []
@@ -1239,7 +1107,7 @@
         functools.partial(front_kernel, n, nz),
         out_shape=[jax.ShapeDtypeStruct(s, d) for s, d in shapes],
         in_specs=[VMEM, VMEM, ANY, VMEM, where, where, where, where],
-        out_specs=[VMEM, VMEM, ANY, ANY, ANY, VMEM, ANY, ANY, ANY, ANY, VMEM, VMEM, ANY],
+        out_specs=[VMEM, VMEM, ANY, ANY, ANY, VMEM, ANY, ANY, ANY, ANY, VMEM, VMEM, ANY, ANY],
         scratch_shapes=[
             pltpu.VMEM((3 * UNITS, UNIT, D), low),
             pltpu.VMEM((UNITS, UNIT, FF + D), low),
@@ -1264,9 +1132,11 @@
             pltpu.VMEM((TOK_SEQ, D), low),
             pltpu.SemaphoreType.DMA((3,)),
             pltpu.SemaphoreType.DMA((2, FF // WIDE)),
-            pltpu.SemaphoreType.DMA((4,)),
+            pltpu.SemaphoreType.DMA((6,)),
             pltpu.SemaphoreType.DMA((stages,)),
             pltpu.SemaphoreType.DMA((stages,)),
+            pltpu.VMEM((n + 8, 128), jnp.int32),
+            pltpu.VMEM((n, 8, 128), jnp.int32),
             *exchange_sems(n, 3),
             *exchange_sems(n),
             *exchange_sems(n),
@@ -1280,97 +1150,117 @@
 
 
 FFN_KINDS = (
-    ("expand", 0, D // UNITS, ("x", "y"), False),
-    ("contract", FF // UNITS // 3, FF // UNITS, ("y", "x"), False),
-    ("contract", 0, FF // UNITS // 3, ("x", "y"), False),
-    ("out", 0, D // UNITS, ("x", "y"), False),
+    ("expand", 0, UNIT, ("x", "y")),
+    ("contract", THIRD, FF // UNITS, ("y", "x")),
+    ("contract", 0, THIRD, ("x", "y")),
+    ("out", 0, UNIT, ("x", "y")),
 )
 QKV_KINDS = (
-    (0, ("x", "y"), False),
-    (1, ("y", "x"), False),
-    (2, ("x", "y"), True),
+    (0, 0, D, ("x", "y")),
+    (1, 0, D, ("y", "x")),
+    (2, 0, D // 2, ("x", "y")),
+    (2, D // 2, D, ("y", "x")),
 )
 QKV_UNITS = 3 * UNITS
 
 
-def finish_kernel(n, nz, *refs):
-    heads, rows_ref, w_hbm, d_sum1_ref, dw1, dw2, dwo, small_ref, ffn_ref = refs[:9]
-    d_tokens_ref, qkv_out, out_out, expand_out, contract_out, vec_out = refs[9:15]
-    inbox, proj, w_ref, own1, own2, owno, ownq, value, land = refs[15:24]
-    load_sem, vsend, vrecv = refs[24:27]
-    sems_in = refs[27:30]
-    rest = list(refs[30:])
+def send_one(sems, src, dst, head, to):
+    return pltpu.make_async_remote_copy(
+        src_ref=src.at[to],
+        dst_ref=dst.at[head],
+        send_sem=sems[0].at[0, to],
+        recv_sem=sems[1].at[0, head],
+        device_id=(lax.axis_index("dp"), to),
+        device_id_type=MESH,
+    )
+
+
+def back_kernel(n, nz, *refs):
+    kv_ref, q_ref, picks_ref, links_ref, lse_ref, grad_ref = refs[:6]
+    rows_ref, w_hbm, d_sum1_ref, small_ref, ffn_ref, dw1, dw2, dwo = refs[6:14]
+    d_tokens_ref, vec_out = refs[14:16]
+    outs = refs[16 : 20 if nz else 17]
+    rest = list(refs[20 if nz else 17 :])
+    vk_ref, keys, values, acc, out_q, out_kv, inbox_q, inbox_kv, proj, w_ref, ownq = rest[:11]
+    value, land, load_sem, vsend, vrecv = rest[11:16]
+    sems_q, sems_kv = rest[16:19], rest[19:22]
+    own1, own2, owno = rest[22:25] if nz else (None, None, None)
+    rest = rest[25:]
     place_row = lax.axis_index("seq")
     head, mine = owned(place_row, n)
-    me = place(nz)
-
-    loads = [
-        pltpu.make_async_copy(src, dst, load_sem.at[i])
-        for i, (src, dst) in enumerate(((dw1, own1), (dw2, own2), (dwo, owno), (w_hbm, w_ref)))
-    ]
-    for cp in loads:
-        cp.start()
-    bar = pltpu.get_barrier_semaphore()
-
-    def greet(k, _):
-        to = (place_row + 1 + k) % n
-        pl.semaphore_signal(bar, inc=1, device_id=(me["y"], to), device_id_type=MESH)
-        return 0
-
-    lax.fori_loop(0, n - 1, greet, 0)
-    pl.semaphore_signal(bar, inc=1, device_id=(1 - me["y"], place_row), device_id_type=MESH)
-    pl.semaphore_wait(bar, n)
-
-    start_from_owners(n, place_row, head, mine, heads, inbox, sems_in)
+    blocks, none = n * BPD, n * BPD + n * PICKS
     pending = []
-    core = me["c"]
+
+    load_w = pltpu.make_async_copy(w_hbm, w_ref, load_sem.at[0])
+    load_w.start()
+    if nz:
+        me = place(nz)
+        core = me["c"]
+        loads = [
+            pltpu.make_async_copy(src, dst, load_sem.at[1 + i])
+            for i, (src, dst) in enumerate(((dw1, own1), (dw2, own2), (dwo, owno)))
+        ]
+        for cp in loads:
+            cp.start()
+        hold = greet_row_and_y(n, me, place_row)
+    else:
+        greet_row(n, place_row, mine)
+
+    @pl.when(mine)
+    def _():
+        turn_pairs(n, kv_ref, vk_ref)
+
+        def clear(b, _):
+            acc[b] = jnp.zeros((BLOCK, 128), jnp.float32)
+            return 0
+
+        lax.fori_loop(0, blocks, clear, 0)
+        clear(none, 0)
 
     def take(count):
         out = rest[:count]
         del rest[:count]
         return out
 
-    sources = {"expand": (dw1, own1), "contract": (dw2, own2), "out": (dwo, owno)}
-    targets = {"expand": expand_out, "contract": contract_out, "out": out_out}
-
-    def ffn_item(kind, lo, hi, links, z_first):
-        far, near = sources[kind]
-        whole = lo == 0 and hi == far.shape[1]
+    def ffn_item(kind, lo, hi, links):
+        far, near = {"expand": (dw1, own1), "contract": (dw2, own2), "out": (dwo, owno)}[kind]
+        target = outs[("out", "expand", "contract").index(kind) + 1]
+        whole = hi - lo == far.shape[1]
 
         def at(ref, t):
             return ref.at[t] if whole else ref.at[t, lo:hi]
 
-        cols = far.shape[2] // 128
         return Reduction(
             nz,
             me,
             links,
-            z_first,
+            False,
             lambda p: at(near, p * 2 + core),
             lambda p: at(far, p * 2 + 1 - core),
-            lambda srcs: add_flat(targets[kind], lo * cols, srcs),
+            lambda srcs: add_flat(target, lo * (far.shape[2] // 128), srcs),
             take(5),
             take(4),
             pending,
         )
 
-    def qkv_item(j, links, z_first):
+    def qkv_item(j, lo, hi, links):
+        def at(t):
+            ref = ownq.at[t * 3 + j]
+            return ref if hi - lo == D else ref.at[:, lo:hi]
+
         return Reduction(
             nz,
             me,
             links,
-            z_first,
-            lambda p: ownq.at[(p * 2 + core) * 3 + j],
-            lambda p: ownq.at[(p * 2 + 1 - core) * 3 + j],
-            lambda srcs: add_flat(qkv_out, j * UNIT * (D // 128), srcs),
+            True,
+            lambda p: at(p * 2 + core),
+            lambda p: at(p * 2 + 1 - core),
+            lambda srcs: add_flat(outs[0], (j * UNIT * D + lo) // 128, srcs, D),
             take(5),
             take(4),
             pending,
         )
 
-    ffn = [ffn_item(*k) for k in FFN_KINDS]
-    qkv = [qkv_item(*k) for k in QKV_KINDS]
-
     def hand_all(items):
         for group in zip(*[i.hand_over() for i in items]):
             for f in group:
@@ -1380,25 +1270,119 @@
         steps = [(w + 0.01 * i, f) for i, item in enumerate(items) for w, f in item.steps()]
         return sorted(steps, key=lambda s: s[0])
 
-    hand_all(ffn)
-    for cp in loads[:3]:
-        cp.wait()
-    ffn_steps = ordered(ffn)
+    ffn_steps = []
+    if nz:
+        ffn = [ffn_item(*k) for k in FFN_KINDS]
+        qkv = [qkv_item(*k) for k in QKV_KINDS]
+        ffn_steps = ordered(ffn)
+        hold()
+        hand_all(ffn)
+        for cp in loads:
+            cp.wait()
+
+    def ffn_run(low, high, whole_only=False):
+        for w, f in ffn_steps:
+            if low <= w < high and not (whole_only and w % 1 >= 0.5):
+                f()
+
+    left = low_lanes((BLOCK, 128))
+    both = range(BPD // 2)
+
+    def attend_some(k, _):
+        s = (place_row + 1 + k) % n
+        lists = [key_list(s * (BPD // 2) + t, n, picks_ref) for t in both]
+        for t in both:
+            fill_pair(lists[t], kv_ref, vk_ref, keys.at[t], values.at[t])
+        parts = []
+        for t in both:
+            i = s * (BPD // 2) + t
+            part = slice(t * BLOCK, (t + 1) * BLOCK)
+            query = two_blocks(q_ref[s, part, :])
+            grad = two_blocks(grad_ref[s, part, :])
+            probs = jnp.exp(pair_scores(i, n, keys[t], query) - lse_ref[i])
+            d_probs = outer_cols(values[t], grad)
+            rows = jnp.sum(probs * d_probs, axis=0, keepdims=True)
+            d_scores = (probs * (d_probs - rows)).astype(jnp.bfloat16)
+            d_values = matmul(probs.astype(jnp.bfloat16), grad)
+            d_keys = matmul(d_scores, query)
+            full = inner_rows(d_scores, keys[t]) * HD ** (-0.5)
+            out_q[s, part, :] = jnp.where(left, full[:BLOCK], full[BLOCK:]).astype(jnp.bfloat16)
+            parts.append((d_keys, d_values))
+
+        @pl.when(s != place_row)
+        def _():
+            send_one(sems_q, out_q, inbox_q, head, s).start()
+
+        for t in both:
+            tiles = []
+            for j in range(8):
+                part = slice(j * BLOCK, (j + 1) * BLOCK)
+                dk, dv = parts[t][0][part], parts[t][1][part]
+                a = jnp.where(left, dk, swap_halves(dv))
+                b = jnp.where(left, swap_halves(dk), dv)
+                tiles.append((a, b))
+            a = (s * (BPD // 2) + t) * 2
+            acc[jnp.maximum(a - 1, 0)] += tiles[0][0]
+            acc[a] += tiles[1][0] + tiles[0][1]
+            acc[a + 1] += tiles[2][0] + tiles[1][1]
+            acc[jnp.minimum(a + 2, blocks - 1)] += tiles[2][1]
+            acc[0] += tiles[3][0] + tiles[3][1]
+            acc[blocks - 1] += tiles[4][0] + tiles[4][1]
+            for u in range(2):
+                for j in range(3):
+                    e = (2 * t + u) * 3 + j
+                    acc[blocks + k * PICKS + e] = tiles[5 + j][u] + acc[blocks + links_ref[s, e]]
+        return 0
+
+    groups = 4
+    for g in range(groups):
+
+        @pl.when(mine)
+        def _():
+            lax.fori_loop(g * (n // groups), (g + 1) * (n // groups), attend_some, 0)
+
+        if g < 2:
+            ffn_run(4 * g + 1, 4 * g + 5, True)
+
+    @pl.when(mine)
+    def _():
+        def close(k, _):
+            s = (place_row + 1 + k) % n
+            for t in range(BPD):
+                b = s * BPD + t
+                total = acc[b] + acc[blocks + links_ref[n, b]]
+                out_kv[s, t * BLOCK : (t + 1) * BLOCK, :] = total.astype(jnp.bfloat16)
+
+            @pl.when(s != place_row)
+            def _():
+                send_one(sems_kv, out_kv, inbox_kv, head, s).start()
+
+            return 0
+
+        lax.fori_loop(0, n, close, 0)
+        copies = (
+            pltpu.make_async_copy(out_q.at[place_row], inbox_q.at[head], sems_q[2].at[0]),
+            pltpu.make_async_copy(out_kv.at[place_row], inbox_kv.at[head], sems_kv[2].at[0]),
+        )
+        for cp in copies:
+            cp.start()
+        for cp in copies:
+            cp.wait()
+
     for w, f in ffn_steps:
-        if w < 20:
+        if 5 < w < 20 and (w % 1 >= 0.5 or w > 9):
             f()
 
-    wait_from_owners(n, place_row, head, heads, inbox, sems_in)
-    loads[3].wait()
-    half = TOK_SEQ // 2
+    wait_from_owners(n, place_row, head, out_q, inbox_q, sems_q)
+    wait_from_owners(n, place_row, head, out_kv, inbox_kv, sems_kv)
     for h in range(0, H, 2):
         lanes = slice(h * HD, (h + 2) * HD)
-        k, v = unpack_pair(inbox[h, 0:TOK_SEQ, :], inbox[h + 1, 0:TOK_SEQ, :], (TOK_SEQ, 128))
+        k, v = unpack_pair(inbox_kv[h], inbox_kv[h + 1], (TOK_SEQ, 128))
         proj[1, :, lanes] = k.astype(jnp.bfloat16)
         proj[2, :, lanes] = v.astype(jnp.bfloat16)
-        for t in range(BPD // 2):
-            part = slice(TOK_SEQ + t * BLOCK, TOK_SEQ + (t + 1) * BLOCK)
-            a, b = unpack_pair(inbox[h, part, :], inbox[h + 1, part, :], (BLOCK, 128))
+        for t in both:
+            part = slice(t * BLOCK, (t + 1) * BLOCK)
+            a, b = unpack_pair(inbox_q[h, part, :], inbox_q[h + 1, part, :], (BLOCK, 128))
             proj[0, 2 * t * BLOCK : (2 * t + 1) * BLOCK, lanes] = a.astype(jnp.bfloat16)
             proj[0, (2 * t + 1) * BLOCK : (2 * t + 2) * BLOCK, lanes] = b.astype(jnp.bfloat16)
 
@@ -1408,7 +1392,8 @@
         return 0
 
     lax.fori_loop(0, 3, weight_grad, 0)
-    hand_all(qkv)
+    if nz:
+        hand_all(qkv)
 
     def add_rows(x):
         return jnp.sum(x.astype(jnp.float32), axis=0, keepdims=True)
@@ -1418,45 +1403,35 @@
     value[0, 2:8] = small_ref[0:6]
     for c in range(FF // D):
         value[0, 8 + c : 9 + c] = ffn_ref[:, c * D : (c + 1) * D]
-    partners = [dict(me, c=1 - core), dict(me, x=1 - me["x"]), dict(me, y=1 - me["y"])]
-    step = 1
-    while step < nz:
-        partners.append(dict(me, z=me["z"] + step - 2 * step * ((me["z"] // step) % 2)))
-        step *= 2
-
-    def vector_copy(i):
-        return pltpu.make_async_remote_copy(
-            src_ref=value.at[i],
-            dst_ref=land.at[i],
-            send_sem=vsend.at[i],
-            recv_sem=vrecv.at[i],
-            device_id=device(partners[i]),
-            device_id_type=MESH,
-        )
-
-    vector_copy(0).start()
-    for w, f in ffn_steps:
-        if w >= 20:
-            f()
+    partners = exchange_partners(me, nz) if nz else []
+    vsems = (vsend, vrecv)
+    if nz:
+        vector_copy(0, value, land, vsems, partners).start()
+        ffn_run(20, 99)
+    load_w.wait()
     d_tokens = d_sum1_ref[...]
     for e in range(3):
         d_tokens = d_tokens + outer_cols(proj[e], as_matrix(w_ref[e * UNITS : (e + 1) * UNITS]))
     d_tokens_ref[...] = d_tokens
     stage = 0
-    for w, f in ordered(qkv):
+    for w, f in ordered(qkv) if nz else ():
         f()
         if w > 3 + 2 * stage and stage < len(partners):
-            vector_copy(stage).wait_recv()
+            vector_copy(stage, value, land, vsems, partners).wait_recv()
             total = value[stage] + land[stage]
             stage += 1
             if stage < len(partners):
                 value[stage] = total
-                vector_copy(stage).start()
+                vector_copy(stage, value, land, vsems, partners).start()
             else:
                 vec_out[...] = total
+    if not nz:
+        vec_out[...] = value[0]
+        outs[0][...] = ownq[...]
     for i in range(len(partners)):
-        vector_copy(i).wait_send()
-    finish_from_owners(n, place_row, head, mine, heads, inbox, sems_in)
+        vector_copy(i, value, land, vsems, partners).wait_send()
+    finish_from_owners(n, place_row, head, mine, out_q, inbox_q, sems_q)
+    finish_from_owners(n, place_row, head, mine, out_kv, inbox_kv, sems_kv)
     for cp, cond in pending:
         if cond is None:
             cp.wait_send()
@@ -1464,32 +1439,41 @@
             pl.when(cond)(cp.wait_send)
 
 
-def finish(heads, rows, qkv, d_sum1, d_expand, d_contract, d_out, small, d_ffn, nz):
+def back(heads, local, weight_grads, nz):
     n = lax.axis_size("seq")
     low, full = jnp.bfloat16, jnp.float32
-    flat = [(3 * UNIT * D // 128, 128), (UNIT * D // 128, 128)]
-    flat += [(UNIT * FF // 128, 128)] * 2
-    stages = 3 + (nz - 1).bit_length()
-    extra = []
-    for kind, lo, hi, links, z_first in FFN_KINDS:
-        width = FF if kind == "expand" else D
-        extra += Reduction.buffers(nz, (hi - lo, width), z_first)
-        extra += Reduction.semaphores(nz, z_first)
-    for j, links, z_first in QKV_KINDS:
-        extra += Reduction.buffers(nz, (UNIT, D), z_first)
-        extra += Reduction.semaphores(nz, z_first)
+    rows, w_all, d_sum1, small, d_ffn = local
+    outs = [((TOK_SEQ, D), full), ((16, D), full)]
+    if nz:
+        outs += [((3 * UNIT * D // 128, 128), full), ((UNIT * D // 128, 128), full)]
+        outs += [((UNIT * FF // 128, 128), full)] * 2
+    else:
+        outs += [((QKV_UNITS, UNIT, D), low)]
+    stages = 3 + (max(nz, 1) - 1).bit_length()
+    part = (TOK_SEQ // 2, 128)
+    extra = [pltpu.VMEM(g.shape, low) for g in weight_grads] if nz else []
+    slabs = [(hi - lo, FF if kind == "expand" else D) for kind, lo, hi, _ in FFN_KINDS]
+    slabs += [(UNIT, hi - lo) for _, lo, hi, _ in QKV_KINDS]
+    for slab in slabs if nz else ():
+        extra += Reduction.buffers(nz, slab)
+        extra += Reduction.semaphores(nz)
     return pl.pallas_call(
-        functools.partial(finish_kernel, n, nz),
-        out_shape=[jax.ShapeDtypeStruct(s, full) for s in [(TOK_SEQ, D)] + flat + [(16, D)]],
-        in_specs=[ANY, VMEM, ANY, VMEM, ANY, ANY, ANY, VMEM, VMEM],
-        out_specs=[VMEM] * 6,
+        functools.partial(back_kernel, n, nz),
+        out_shape=[jax.ShapeDtypeStruct(s, d) for s, d in outs],
+        in_specs=[VMEM, VMEM, SMEM, SMEM, VMEM, VMEM]
+        + [VMEM, ANY, VMEM, VMEM, VMEM, ANY, ANY, ANY],
+        out_specs=[VMEM] * len(outs),
         scratch_shapes=[
-            pltpu.VMEM((H, MSG, 128), low),
+            pltpu.VMEM((n * BPD, BLOCK, 128), low),
+            pltpu.VMEM((BPD // 2, 8 * BLOCK, 128), low),
+            pltpu.VMEM((BPD // 2, 8 * BLOCK, 128), low),
+            pltpu.VMEM((n * (BPD + PICKS) + 1, BLOCK, 128), full),
+            pltpu.VMEM((n,) + part, low),
+            pltpu.VMEM((n, TOK_SEQ, 128), low),
+            pltpu.VMEM((H,) + part, low),
+            pltpu.VMEM((H, TOK_SEQ, 128), low),
             pltpu.VMEM((3, TOK_SEQ, D), low),
             pltpu.VMEM((QKV_UNITS, UNIT, D), low),
-            pltpu.VMEM(d_expand.shape, low),
-            pltpu.VMEM(d_contract.shape, low),
-            pltpu.VMEM(d_out.shape, low),
             pltpu.VMEM((QKV_UNITS, UNIT, D), low),
             pltpu.VMEM((stages, 16, D), full),
             pltpu.VMEM((stages, 16, D), full),
@@ -1497,23 +1481,14 @@
             pltpu.SemaphoreType.DMA((stages,)),
             pltpu.SemaphoreType.DMA((stages,)),
             *exchange_sems(n),
+            *exchange_sems(n),
             *extra,
         ],
         compiler_params=pltpu.CompilerParams(
-            collective_id=5, has_side_effects=True, vmem_limit_bytes=60 << 20
+            collective_id=5, has_side_effects=True, vmem_limit_bytes=61 << 20
         ),
-        name="finish",
-    )(heads, rows, qkv, d_sum1, d_expand, d_contract, d_out, small, d_ffn)
-
-
-def unpack_heads(parts):
-    parts = parts.reshape(H, BPD // 2, BLOCK, 2, HD).transpose(1, 3, 2, 0, 4)
-    return parts.reshape(TOK_SEQ, D)
-
-
-def unpack_keys(parts):
-    parts = parts.reshape(H, TOK_SEQ, 2, HD).transpose(2, 1, 0, 3)
-    return parts.reshape(2, TOK_SEQ, D)
+        name="back",
+    )(*heads, *local, *weight_grads)
 
 
 def on_device(
@@ -1565,31 +1540,24 @@
         small,
         d_ffn,
         w_all,
+        links,
     ) = front(
         rows, cotangent.reshape(TOK_SEQ, D), random_blocks, vec, qkv, first, out, second, planes
     )
-    d_heads = attend_heads_back(kv, queries, picks, lse, d_heads)
+    d_tokens, totals, *grads = back(
+        (kv, queries, picks, links, lse, d_heads),
+        (rows, w_all, d_sum1, small, d_ffn),
+        (d_expand, d_contract, d_out),
+        planes,
+    )
+    totals = (totals[0:6], totals[6:8], totals[8 : 8 + FF // D])
     if planes:
-        d_tokens, d_qkv, d_out, d_expand, d_contract, totals = finish(
-            d_heads, rows, w_all, d_sum1, d_expand, d_contract, d_out, small, d_ffn, planes
-        )
-        vectors = (totals[0:6], totals[6:8], totals[8 : 8 + FF // D])
         vectors = [
             lax.dynamic_slice(v.reshape(-1), (me * (v.size // shards),), (v.size // shards,))
-            for v in vectors
+            for v in totals
         ]
     else:
-        d_heads = exchange(from_owners_kernel, H, d_heads, 4, "return_head_grads")
-        d_query = unpack_heads(d_heads[:, TOK_SEQ:])
-        d_pair = unpack_keys(d_heads[:, :TOK_SEQ])
-        d_proj = jnp.concatenate([d_query[None], d_pair], axis=0)
-        d_qkv = jnp.einsum("rd,erf->edf", rows, d_proj, preferred_element_type=jnp.float32)
-        d_tokens = d_sum1 + jnp.einsum(
-            "erf,edf->rd", d_proj, qkv.reshape(3, D, D), preferred_element_type=jnp.float32
-        )
-        d_bias_q = jnp.sum(d_query.astype(jnp.float32), axis=0)
-        d_bias_v = jnp.sum(d_pair[1].astype(jnp.float32), axis=0)
-        d_biases = jnp.concatenate([jnp.stack([d_bias_q, d_bias_v]), small[0:4]])
+        grads = [grads[0], d_out, d_expand, d_contract]
         *vectors, d_qkv, d_out, d_expand, d_contract = [
             lax.psum_scatter(
                 g.astype(jnp.float32).reshape(-1),
@@ -1597,10 +1565,10 @@
                 scatter_dimension=0,
                 tiled=True,
             )
-            for g in (d_biases, small[4:6], d_ffn, d_qkv, d_out, d_expand, d_contract)
+            for g in (*totals, *grads)
         ]
-    grads = [g.reshape(-1) for g in (d_qkv, d_out, d_expand, d_contract)]
-    return (result[None], d_tokens[None], *grads, *vectors)
+        grads = (d_qkv, d_out, d_expand, d_contract)
+    return (result[None], d_tokens[None], *[g.reshape(-1) for g in grads], *vectors)
 
 
 def solution(mesh):

time: 287 us -> 271 us (0.944)
  Pallas kernels: 269 us -> 251 us
    pallas_call x2 -> x1, Pallas kernels: 129 us -> 109 us  [back(): pl.pallas_call(functools.partial(back_kernel, n, nz), out_shape=[jax.Shap...]
    unnamed x15 -> x11, local copies, waits for them, and re-layouts: 7.4 us -> 9.23 us
where the time goes in v6:
time: 271 us; the launch traced here: 269 us
  Pallas kernels  251 us (93%)
  local copies, waits for them, and re-layouts  14.7 us (5%)
    pallas_call x1, Pallas kernels, front(): pl.pallas_call(functools.partial(front_kernel, n, nz), out_shape=[jax.Sha...  142 us
    pallas_call x1, Pallas kernels, back(): pl.pallas_call(functools.partial(back_kernel, n, nz), out_shape=[jax.Shap...  109 us
    unnamed x11, local copies, waits for them, and re-layouts  9.23 us

profile of v6, /device:TPU:8, one launch (start us, length us, event | category | flops | bytes accessed | tf_op | source)
XLA Modules:
  0.0 268.6 jit_solution(3513117991366772246)
XLA Ops:
  0.6 0.7 copy.20
  1.3 0.1 copy.21
  1.4 0.7 convert_dynamic-update-slice_fusion.2
  2.2 0.8 convert_dynamic-update-slice_fusion.1
  3.0 0.8 convert_dynamic-update-slice_fusion
  3.7 0.6 pad.9.refs_3_
  4.4 0.6 pad.8.refs_2_
  5.0 141.9 %front.1 = (f32[256,768]{1,0:T(8,128)}, f32[256,768]{1,0:T(8,128)}, bf16[64,64,128]{2,1,0:T(8,128)(2,1)}, bf16[16,128,128]{2,1,0:T(8,128)(2,1)}, s32[16,8,128]{2...) custom-call(bf16[256,768]{1,0:T(8,128)(2,1)} %bitcast.13, ...), custom_call_target="tpu_custom_call" | custom-call | tf_op jit(solution)/shard_map/front/pallas_call | solution.py:1106
  146.9 0.0 copy-start
  146.9 109.0 %back.1 = (f32[256,768]{1,0:T(8,128)}, f32[16,768]{1,0:T(8,128)}, f32[432,128]{1,0:T(8,128)}, f32[144,128]{1,0:T(8,128)}, f32[576,128]{1,0:T(8,128)}, /*index=5*/f32[576,128]{1,0:T(8,128)}) custom-call(bf16[64,64,128]{2,1,0:T(8,128)(2,1)} %get-tuple-element.30.refs_0_, bf16[16,128,128]{2,1,0:T(8,128)(2,1)} %get-tuple-element.31.refs_1_, ...), custom_call_target="tpu_custom_call" | custom-call | tf_op jit(solution)/shard_map/back/pallas_call | solution.py:1460
  255.9 0.0 copy-start.1
  255.9 0.8 slice.10
  256.7 0.6 dynamic_slice.10
  257.3 0.7 slice.11
  258.1 0.7 slice.9
  258.8 0.6 dynamic_slice.9
  259.5 0.6 dynamic_slice.11
  260.1 0.0 copy-done
  260.1 0.9 copy.31
  260.9 2.1 copy.32
  263.0 1.6 copy.33
  264.6 1.5 copy.34
  266.2 1.7 copy.35
  267.8 0.0 copy-done.1
  267.9 0.7 copy.36
  (8 shorter events, 0.1 us)
Async XLA Ops:
  146.9 113.2 %copy-start = (f32[256,768]{1,0:T(8,128)S(1)}, f32[256,768]{1,0:T(8,128)}, u32[]{:S(2)}) copy-start(f32[256,768]{1,0:T(8,128)} %get-tuple-element.29) | copy-start | bytes 2359300
  255.9 11.9 %copy-start.1 = (f32[576,128]{1,0:T(8,128)S(1)}, f32[576,128]{1,0:T(8,128)}, u32[]{:S(2)}) copy-start(f32[576,128]{1,0:T(8,128)} %get-tuple-element.47) | copy-start | bytes 884740

commit v7 on v6

--- a/solution.py
+++ b/solution.py
@@ -103,27 +103,27 @@
     return jnp.minimum(head, H - 1), jnp.logical_and(head < H, owner(head, n) == place)
 
 
+def post(place, h, pairs, sems, act, n):
+    to = owner(h, n)
+    for i, (src, dst) in enumerate(pairs):
+
+        @pl.when(to != place)
+        def _():
+            act(
+                pltpu.make_async_remote_copy(
+                    src_ref=src.at[h],
+                    dst_ref=dst(place),
+                    send_sem=sems[0].at[i, h],
+                    recv_sem=sems[1].at[i, place],
+                    device_id=(lax.axis_index("dp"), to),
+                    device_id_type=MESH,
+                )
+            )
+
+
 def walk_to_owners(n, place, head, pairs, sems, act):
-    row = lax.axis_index("dp")
-
     def body(k, _):
-        h = (head + 1 + k) % H
-        to = owner(h, n)
-        for i, (src, dst) in enumerate(pairs):
-
-            @pl.when(to != place)
-            def _():
-                act(
-                    pltpu.make_async_remote_copy(
-                        src_ref=src.at[h],
-                        dst_ref=dst(place),
-                        send_sem=sems[0].at[i, h],
-                        recv_sem=sems[1].at[i, place],
-                        device_id=(row, to),
-                        device_id_type=MESH,
-                    )
-                )
-
+        post(place, (head + 1 + k) % H, pairs, sems, act, n)
         return 0
 
     lax.fori_loop(0, H, body, 0)
@@ -133,10 +133,7 @@
     walk_to_owners(n, place, head, pairs, sems, lambda cp: cp.wait_send())
 
 
-def send_to_owners(n, place, head, mine, pairs, sems, meanwhile, wait_sends=True):
-    walk_to_owners(n, place, head, pairs, sems, lambda cp: cp.start())
-    meanwhile()
-
+def wait_to_owner(n, place, head, mine, pairs, sems):
     @pl.when(mine)
     def _():
         for i, (src, dst) in enumerate(pairs):
@@ -159,8 +156,12 @@
 
         lax.fori_loop(0, n - 1, body, 0)
 
-    if wait_sends:
-        finish_to_owners(n, place, head, pairs, sems)
+
+def send_to_owners(n, place, head, mine, pairs, sems, meanwhile):
+    walk_to_owners(n, place, head, pairs, sems, lambda cp: cp.start())
+    meanwhile()
+    wait_to_owner(n, place, head, mine, pairs, sems)
+    finish_to_owners(n, place, head, pairs, sems)
 
 
 def walk_from_owners(n, place, head, src, dst, sems, act):
@@ -192,21 +193,22 @@
         cp.wait()
 
 
+def wait_head(n, place, h, src, dst, sems):
+    @pl.when(owner(h, n) != place)
+    def _():
+        pltpu.make_async_remote_copy(
+            src_ref=src.at[0],
+            dst_ref=dst.at[h],
+            send_sem=sems[0].at[0, 0],
+            recv_sem=sems[1].at[0, h],
+            device_id=(lax.axis_index("dp"), place),
+            device_id_type=MESH,
+        ).wait_recv()
+
+
 def wait_from_owners(n, place, head, src, dst, sems):
     def body(k, _):
-        h = (head + k) % H
-
-        @pl.when(owner(h, n) != place)
-        def _():
-            pltpu.make_async_remote_copy(
-                src_ref=src.at[0],
-                dst_ref=dst.at[h],
-                send_sem=sems[0].at[0, 0],
-                recv_sem=sems[1].at[0, h],
-                device_id=(lax.axis_index("dp"), place),
-                device_id_type=MESH,
-            ).wait_recv()
-
+        wait_head(n, place, (head + k) % H, src, dst, sems)
         return 0
 
     lax.fori_loop(0, H, body, 0)
@@ -685,6 +687,10 @@
 )
 
 
+EARLY = {1: (0, 1), 4: (1, 2), 5: (2, 3)}
+LATE = ((3, 4), (4, 5), (5, 99), (99, 99), (99, 99))
+
+
 def from_flat(flat, cols, rows):
     step = cols // 128
     return [flat[pl.ds(k, rows, stride=step), :] for k in range(step)]
@@ -700,6 +706,25 @@
     if lax.axis_size("dp") != 2 or 2 * seq != UNITS or seq % 4:
         return 0
     return seq // 4
+
+
+def place_vectors(me, shards, pieces, line, value):
+    packed = pieces[...]
+    at, row = 0, 0
+    value[0] = jnp.zeros_like(value[0])
+    for size in VECTORS:
+        width = size // shards
+        start = me * width
+        inside = lax.broadcasted_iota(jnp.int32, packed.shape, 1)
+        inside = jnp.logical_and(inside >= at, inside < at + width)
+        moved = jnp.where(inside, packed, 0.0)
+        line[...] = jnp.zeros_like(line)
+        base = pl.multiple_of(start // 128 * 128, 128)
+        line[:, pl.ds(base, 384)] = pltpu.roll(moved, (start % 128 - at) % 384, 1)
+        for r in range(size // D):
+            value[0, row + r : row + r + 1] = line[:, r * D : (r + 1) * D]
+        row += size // D
+        at += width
 
 
 def front_kernel(n, nz, *refs):
@@ -751,9 +776,10 @@
         vrecv,
         links_ref,
         picks_vmem,
-    ) = refs[22:52]
-    sems_qkv, sems_in, sems_out = refs[52:55], refs[55:58], refs[58:61]
-    rest = list(refs[61:])
+        line,
+    ) = refs[22:53]
+    sems_qkv, sems_in, sems_out = refs[53:56], refs[56:59], refs[59:62]
+    rest = list(refs[62:])
     place_row = lax.axis_index("seq")
     head, mine = owned(place_row, n)
     pending = []
@@ -779,7 +805,7 @@
             for k in range(step):
                 col = flat[pl.ds(j * UNIT * step + k, UNIT, stride=step), :]
                 w_ref[slot * 3 + j, :, k * 128 : (k + 1) * 128] = col.astype(jnp.bfloat16)
-        value[0] = vec_in[...]
+        place_vectors(slot, 8 * nz, vec_in, line, value)
         hold()
         qkv_items = [
             Spread(nz, me, order, lambda s, j=j: w_ref.at[s * 3 + j], take(), pending)
@@ -819,8 +845,8 @@
         for depth in range(1, nz + 2):
             vector_stage(min(depth - 1, stages)) if depth <= stages else None
             run_in_order(qkv_items, depth, depth + 1)
-            if depth == 2:
-                run_in_order(rest_items, 0, 1)
+            if depth in EARLY:
+                run_in_order(rest_items, *EARLY[depth])
         for i in range(nz + 1, stages):
             vector_stage(i)
         for item in qkv_items:
@@ -848,8 +874,15 @@
     left = low_lanes((TOK_SEQ, 128))
     left_q = low_lanes((BLOCK, 128))
     wide = 256
-    for g in range(D // wide):
-        cols = slice(g * wide, (g + 1) * wide)
+    parcels = (
+        (box_kv, lambda s: kv_ref.at[pl.ds(s * BPD, BPD)]),
+        (box_q, lambda s: q_ref.at[s]),
+        (picks_ref, lambda s: picks_hbm.at[s]),
+    )
+
+    def project_some(step, _):
+        g = (place_row + step) % (D // wide)
+        cols = pl.ds(pl.multiple_of(g * wide, wide), wide)
 
         def project(e):
             return matmul(rows, as_matrix(w_ref[e * UNITS : (e + 1) * UNITS, :, cols]))
@@ -858,7 +891,7 @@
         k = project(1)
         v = project(2) + vec[1:2, cols]
         for p in range(wide // 128):
-            h = (g * wide + p * 128) // HD
+            h = g * (wide // HD) + p * 2
             lanes = slice(p * 128, (p + 1) * 128)
             kp, vp, qp = k[:, lanes], v[:, lanes], q[:, lanes]
             even, odd = jnp.where(left, kp, swap_halves(vp)), jnp.where(left, swap_halves(kp), vp)
@@ -873,21 +906,13 @@
                 to = slice(t * BLOCK, (t + 1) * BLOCK)
                 box_q[h, to, :] = jnp.where(left_q, qp[a], turned[b]).astype(jnp.bfloat16)
                 box_q[h + 1, to, :] = jnp.where(left_q, turned[a], qp[b]).astype(jnp.bfloat16)
-    parcels = (
-        (box_kv, lambda s: kv_ref.at[pl.ds(s * BPD, BPD)]),
-        (box_q, lambda s: q_ref.at[s]),
-        (picks_ref, lambda s: picks_hbm.at[s]),
-    )
-    send_to_owners(
-        n,
-        place_row,
-        head,
-        mine,
-        parcels,
-        sems_qkv,
-        lambda: rest_steps(1, 3),
-        wait_sends=False,
-    )
+            for u in range(2):
+                post(place_row, h + u, parcels, sems_qkv, lambda cp: cp.start(), n)
+        return 0
+
+    lax.fori_loop(0, D // wide, project_some, 0)
+    rest_steps(*LATE[0])
+    wait_to_owner(n, place_row, head, mine, parcels, sems_qkv)
 
     keep = (
         pltpu.make_async_copy(kv_ref, kv_hbm, keep_sem.at[0]),
@@ -953,7 +978,7 @@
         def _():
             lax.fori_loop(g * (n // groups), (g + 1) * (n // groups), attend_some, 0)
 
-        rest_steps(3 + g, 4 + g if g < groups - 1 else 99)
+        rest_steps(*LATE[1 + g])
 
     @pl.when(mine)
     def _():
@@ -1137,6 +1162,7 @@
             pltpu.SemaphoreType.DMA((stages,)),
             pltpu.VMEM((n + 8, 128), jnp.int32),
             pltpu.VMEM((n, 8, 128), jnp.int32),
+            pltpu.VMEM((1, max(VECTORS) + 384), full),
             *exchange_sems(n, 3),
             *exchange_sems(n),
             *exchange_sems(n),
@@ -1182,10 +1208,10 @@
     outs = refs[16 : 20 if nz else 17]
     rest = list(refs[20 if nz else 17 :])
     vk_ref, keys, values, acc, out_q, out_kv, inbox_q, inbox_kv, proj, w_ref, ownq = rest[:11]
-    value, land, load_sem, vsend, vrecv = rest[11:16]
-    sems_q, sems_kv = rest[16:19], rest[19:22]
-    own1, own2, owno = rest[22:25] if nz else (None, None, None)
-    rest = rest[25:]
+    turned_rows, value, land, load_sem, vsend, vrecv = rest[11:17]
+    sems_q, sems_kv = rest[17:20], rest[20:23]
+    own1, own2, owno = rest[23:26] if nz else (None, None, None)
+    rest = rest[26:]
     place_row = lax.axis_index("seq")
     head, mine = owned(place_row, n)
     blocks, none = n * BPD, n * BPD + n * PICKS
@@ -1270,6 +1296,7 @@
         steps = [(w + 0.01 * i, f) for i, item in enumerate(items) for w, f in item.steps()]
         return sorted(steps, key=lambda s: s[0])
 
+    turned_rows[...] = rows_ref[...].T
     ffn_steps = []
     if nz:
         ffn = [ffn_item(*k) for k in FFN_KINDS]
@@ -1370,30 +1397,39 @@
             cp.wait()
 
     for w, f in ffn_steps:
-        if 5 < w < 20 and (w % 1 >= 0.5 or w > 9):
+        if w < 9 and w % 1 >= 0.5:
             f()
 
-    wait_from_owners(n, place_row, head, out_q, inbox_q, sems_q)
-    wait_from_owners(n, place_row, head, out_kv, inbox_kv, sems_kv)
-    for h in range(0, H, 2):
-        lanes = slice(h * HD, (h + 2) * HD)
-        k, v = unpack_pair(inbox_kv[h], inbox_kv[h + 1], (TOK_SEQ, 128))
-        proj[1, :, lanes] = k.astype(jnp.bfloat16)
-        proj[2, :, lanes] = v.astype(jnp.bfloat16)
+    def head_pair(k, _):
+        p = (place_row + k) % (H // 2)
+        for u in range(2):
+            wait_head(n, place_row, 2 * p + u, out_q, inbox_q, sems_q)
+            wait_head(n, place_row, 2 * p + u, out_kv, inbox_kv, sems_kv)
+        lanes = pl.ds(pl.multiple_of(p * 128, 128), 128)
+        keys_values = unpack_pair(inbox_kv[2 * p], inbox_kv[2 * p + 1], (TOK_SEQ, 128))
+        queries = []
         for t in both:
             part = slice(t * BLOCK, (t + 1) * BLOCK)
-            a, b = unpack_pair(inbox_q[h, part, :], inbox_q[h + 1, part, :], (BLOCK, 128))
-            proj[0, 2 * t * BLOCK : (2 * t + 1) * BLOCK, lanes] = a.astype(jnp.bfloat16)
-            proj[0, (2 * t + 1) * BLOCK : (2 * t + 2) * BLOCK, lanes] = b.astype(jnp.bfloat16)
-
-    def weight_grad(e, _):
-        grad = inner_rows(rows_ref[...], proj[e])
-        ownq[pl.ds(e * UNITS, UNITS)] = grad.reshape(UNITS, UNIT, D).astype(jnp.bfloat16)
+            queries += unpack_pair(inbox_q[2 * p, part, :], inbox_q[2 * p + 1, part, :], (BLOCK, 128))
+        grads = (jnp.concatenate(queries, axis=0), *keys_values)
+        for e in range(3):
+            proj[e, :, lanes] = grads[e].astype(jnp.bfloat16)
+        joined = jnp.concatenate(grads, axis=1).astype(jnp.bfloat16)
+        grad = matmul(turned_rows[...], joined).reshape(UNITS, UNIT, 3 * 128).astype(jnp.bfloat16)
+        for e in range(3):
+            ownq[pl.ds(e * UNITS, UNITS), :, lanes] = grad[:, :, e * 128 : (e + 1) * 128]
         return 0
 
-    lax.fori_loop(0, 3, weight_grad, 0)
+    lax.fori_loop(0, H // 2, head_pair, 0)
+    qkv_steps = []
     if nz:
         hand_all(qkv)
+        qkv_steps = ordered(qkv)
+
+    def qkv_run(low, high):
+        for w, f in qkv_steps:
+            if low <= w < high:
+                f()
 
     def add_rows(x):
         return jnp.sum(x.astype(jnp.float32), axis=0, keepdims=True)
@@ -1407,24 +1443,33 @@
     vsems = (vsend, vrecv)
     if nz:
         vector_copy(0, value, land, vsems, partners).start()
-        ffn_run(20, 99)
+
+    def vector_stage(i):
+        if i < len(partners):
+            vector_copy(i, value, land, vsems, partners).wait_recv()
+            total = value[i] + land[i]
+            if i + 1 < len(partners):
+                value[i + 1] = total
+                vector_copy(i + 1, value, land, vsems, partners).start()
+            else:
+                vec_out[...] = total
+
+    qkv_run(1, 5)
+    ffn_run(9, 20)
+    vector_stage(0)
+    qkv_run(5, 9)
     load_w.wait()
     d_tokens = d_sum1_ref[...]
     for e in range(3):
         d_tokens = d_tokens + outer_cols(proj[e], as_matrix(w_ref[e * UNITS : (e + 1) * UNITS]))
     d_tokens_ref[...] = d_tokens
-    stage = 0
-    for w, f in ordered(qkv) if nz else ():
-        f()
-        if w > 3 + 2 * stage and stage < len(partners):
-            vector_copy(stage, value, land, vsems, partners).wait_recv()
-            total = value[stage] + land[stage]
-            stage += 1
-            if stage < len(partners):
-                value[stage] = total
-                vector_copy(stage, value, land, vsems, partners).start()
-            else:
-                vec_out[...] = total
+    vector_stage(1)
+    ffn_run(20, 99)
+    vector_stage(2)
+    qkv_run(9, 20)
+    vector_stage(3)
+    vector_stage(4)
+    qkv_run(20, 99)
     if not nz:
         vec_out[...] = value[0]
         outs[0][...] = ownq[...]
@@ -1475,6 +1520,7 @@
             pltpu.VMEM((3, TOK_SEQ, D), low),
             pltpu.VMEM((QKV_UNITS, UNIT, D), low),
             pltpu.VMEM((QKV_UNITS, UNIT, D), low),
+            pltpu.VMEM((D, TOK_SEQ), low),
             pltpu.VMEM((stages, 16, D), full),
             pltpu.VMEM((stages, 16, D), full),
             pltpu.SemaphoreType.DMA((4,)),
@@ -1489,6 +1535,52 @@
         ),
         name="back",
     )(*heads, *local, *weight_grads)
+
+
+VECTORS = (6 * D, 2 * D, FF)
+
+
+def hand_out_kernel(shards, *refs):
+    count = (len(refs) - 6) // 3
+    arrays, totals, outs = refs[:count], refs[count], refs[count + 1 : 2 * count + 1]
+    pieces = refs[2 * count + 1 : 2 * count + 4]
+    held, (line, sem) = refs[2 * count + 4 : -2], refs[-2:]
+    into = [pltpu.make_async_copy(*pair, sem.at[i]) for i, pair in enumerate(zip(arrays, held))]
+    onto = [pltpu.make_async_copy(*pair, sem.at[i]) for i, pair in enumerate(zip(held, outs))]
+    for cp in into:
+        cp.start()
+    for first, second in zip(into, onto):
+        first.wait()
+        second.start()
+    me = lax.axis_index("dp") * lax.axis_size("seq") + lax.axis_index("seq")
+    row = 0
+    for size, out in zip(VECTORS, pieces):
+        for r in range(size // D):
+            line[:, r * D : (r + 1) * D] = totals[row + r : row + r + 1]
+        row += size // D
+        start = me * (size // shards)
+        base = pl.multiple_of(start // 128 * 128, 128)
+        some = line[:, pl.ds(base, 384)]
+        out[...] = pltpu.roll(some, 384 - start % 128, 1)[:, 0 : size // shards]
+    for cp in onto:
+        cp.wait()
+
+
+def hand_out(arrays, totals):
+    shards = lax.axis_size("dp") * lax.axis_size("seq")
+    shapes = [a.shape for a in arrays] + [(1, v // shards) for v in VECTORS]
+    return pl.pallas_call(
+        functools.partial(hand_out_kernel, shards),
+        out_shape=[jax.ShapeDtypeStruct(s, jnp.float32) for s in shapes],
+        in_specs=[ANY] * len(arrays) + [VMEM],
+        out_specs=[ANY] * len(arrays) + [VMEM] * 3,
+        scratch_shapes=[
+            *[pltpu.VMEM(a.shape, jnp.float32) for a in arrays],
+            pltpu.VMEM((1, max(VECTORS) + 384), jnp.float32),
+            pltpu.SemaphoreType.DMA((len(arrays),)),
+        ],
+        name="hand_out",
+    )(*arrays, totals)
 
 
 def on_device(
@@ -1510,12 +1602,8 @@
     weights = (qkv_weight, expand_weight, out_weight, contract_weight)
     vectors = (bias_vectors, gain_vectors, ffn_bias)
     if planes:
-        placed = [
-            lax.dynamic_update_slice(
-                jnp.zeros((v.size * shards,), jnp.float32), v.astype(jnp.float32), (me * v.size,)
-            )
-            for v in vectors
-        ]
+        vec = jnp.concatenate(vectors).astype(jnp.float32)
+        vec = jnp.pad(vec, (0, -vec.size % 128)).reshape(1, -1)
         qkv, first, out, second = [w.reshape(-1, 128) for w in weights]
     else:
         gather = functools.partial(lax.all_gather, axis_name=("dp", "seq"), axis=0, tiled=True)
@@ -1525,7 +1613,7 @@
         first, out = first.reshape(UNITS, UNIT, FF), out.reshape(UNITS, UNIT, D)
         first = jnp.concatenate([first, out], axis=2)
         second = second.reshape(UNITS, FF // UNITS, D)
-    vec = jnp.pad(jnp.concatenate(placed).reshape(-1, D), ((0, 4), (0, 0)))
+        vec = jnp.pad(jnp.concatenate(placed).reshape(-1, D), ((0, 4), (0, 0)))
     (
         result,
         d_sum1,
@@ -1550,12 +1638,9 @@
         (d_expand, d_contract, d_out),
         planes,
     )
-    totals = (totals[0:6], totals[6:8], totals[8 : 8 + FF // D])
     if planes:
-        vectors = [
-            lax.dynamic_slice(v.reshape(-1), (me * (v.size // shards),), (v.size // shards,))
-            for v in totals
-        ]
+        result, d_tokens, *grads = hand_out((result, d_tokens, *grads), totals)
+        grads, vectors = grads[:4], [v.reshape(-1) for v in grads[4:]]
     else:
         grads = [grads[0], d_out, d_expand, d_contract]
         *vectors, d_qkv, d_out, d_expand, d_contract = [
@@ -1565,7 +1650,7 @@
                 scatter_dimension=0,
                 tiled=True,
             )
-            for g in (*totals, *grads)
+            for g in (totals[0:6], totals[6:8], totals[8 : 8 + FF // D], *grads)
         ]
         grads = (d_qkv, d_out, d_expand, d_contract)
     return (result[None], d_tokens[None], *[g.reshape(-1) for g in grads], *vectors)

time: 271 us -> 244 us (0.900)
  Pallas kernels: 251 us -> 236 us
  local copies, waits for them, and re-layouts: 14.7 us -> 1.99 us
    pallas_call x1, Pallas kernels: 142 us -> 129 us  [front(): pl.pallas_call(functools.partial(front_kernel, n, nz), out_shape=[jax.Sha...]
    unnamed x11 -> x1, local copies, waits for them, and re-layouts: 9.23 us -> 0.7 us
    pallas_call x1, Pallas kernels: 109 us -> 103 us  [back(): pl.pallas_call(functools.partial(back_kernel, n, nz), out_shape=[jax.Shap...]
    pallas_call x0 -> x1, Pallas kernels: none -> 3.98 us  [hand_out(): pl.pallas_call(functools.partial(hand_out_kernel, shards), out_shape=[jax...]
where the time goes in v7:
time: 244 us; the launch traced here: 240 us
  Pallas kernels  236 us (97%)
    pallas_call x1, Pallas kernels, front(): pl.pallas_call(functools.partial(front_kernel, n, nz), out_shape=[jax.Sha...  129 us
    pallas_call x1, Pallas kernels, back(): pl.pallas_call(functools.partial(back_kernel, n, nz), out_shape=[jax.Shap...  103 us

profile of v7, /device:TPU:8, one launch (start us, length us, event | category | flops | bytes accessed | tf_op | source)
XLA Modules:
  0.0 239.7 jit_solution(7326001624352007006)
XLA Ops:
  0.6 0.8 fusion.5
  1.4 0.6 reshape.82.refs_3_
  2.0 0.7 copy.20
  2.7 0.1 copy.21
  2.8 0.6 pad.9.refs_2_
  3.4 129.5 %front.1 = (f32[256,768]{1,0:T(8,128)}, f32[256,768]{1,0:T(8,128)}, bf16[64,64,128]{2,1,0:T(8,128)(2,1)}, bf16[16,128,128]{2,1,0:T(8,128)(2,1)}, s32[16,8,128]{2...) custom-call(bf16[256,768]{1,0:T(8,128)(2,1)} %bitcast.16, ...), custom_call_target="tpu_custom_call" | custom-call | tf_op jit(solution)/shard_map/front/pallas_call | solution.py:1131
  132.9 102.7 %back.1 = (f32[256,768]{1,0:T(8,128)}, f32[16,768]{1,0:T(8,128)}, f32[432,128]{1,0:T(8,128)}, f32[144,128]{1,0:T(8,128)}, f32[576,128]{1,0:T(8,128)}, /*index=5*/f32[576,128]{1,0:T(8,128)}) custom-call(bf16[64,64,128]{2,1,0:T(8,128)(2,1)} %get-tuple-element.39.refs_0_, bf16[16,128,128]{2,1,0:T(8,128)(2,1)} %get-tuple-element.40.refs_1_, ...), custom_call_target="tpu_custom_call" | custom-call | tf_op jit(solution)/shard_map/back/pallas_call | solution.py:1505
  235.6 4.0 %hand_out.1 = (f32[256,768]{1,0:T(8,128)}, f32[256,768]{1,0:T(8,128)}, f32[432,128]{1,0:T(8,128)}, f32[144,128]{1,0:T(8,128)}, f32[576,128]{1,0:T(8,128)}, /*ind...) custom-call(f32[256,768]{1,0:T(8,128)} %get-tuple-element.38.refs_0_, ...), custom_call_target="tpu_custom_call" | custom-call | tf_op jit(solution)/shard_map/hand_out/pallas_call | solution.py:1572

commit v8 on v7

--- a/solution.py
+++ b/solution.py
@@ -777,9 +777,10 @@
         links_ref,
         picks_vmem,
         line,
-    ) = refs[22:53]
-    sems_qkv, sems_in, sems_out = refs[53:56], refs[56:59], refs[59:62]
-    rest = list(refs[62:])
+        d_up_ref,
+    ) = refs[22:54]
+    sems_qkv, sems_in, sems_out = refs[54:57], refs[57:60], refs[60:63]
+    rest = list(refs[63:])
     place_row = lax.axis_index("seq")
     head, mine = owned(place_row, n)
     pending = []
@@ -1047,12 +1048,7 @@
         d_active = outer_cols(d_down, second_rows(c))
         d_up = (d_active * slope_ref[:, cols]).astype(jnp.bfloat16)
         d_ffn_ref[:, cols] = add_rows(d_up.astype(jnp.float32))
-        dw2 = inner_rows(active_ref[:, cols], d_down)
-        dw2_ref[pl.ds(c * per, per)] = dw2.reshape(per, FF // UNITS, D).astype(jnp.bfloat16)
-        dw1 = inner_rows(lowered, d_up)
-        dw1_ref[:, :, cols] = dw1.reshape(UNITS, UNIT, WIDE).astype(jnp.bfloat16)
-        for cp in stores(c):
-            cp.start()
+        d_up_ref[:, cols] = d_up
         return d_norm1 + outer_cols(d_up, as_matrix(first_ref[:, :, cols]))
 
     d_norm1 = lax.fori_loop(0, FF // WIDE, back_step, d_sum2)
@@ -1077,7 +1073,18 @@
 
     store_out = pltpu.make_async_copy(dwo_ref, dwo_hbm, load_sem.at[0])
 
+    def weight_grads(c, _):
+        cols = pl.ds(pl.multiple_of(c * WIDE, WIDE), WIDE)
+        dw2 = inner_rows(active_ref[:, cols], d_down)
+        dw2_ref[pl.ds(c * per, per)] = dw2.reshape(per, FF // UNITS, D).astype(jnp.bfloat16)
+        dw1 = inner_rows(lowered, d_up_ref[:, cols])
+        dw1_ref[:, :, cols] = dw1.reshape(UNITS, UNIT, WIDE).astype(jnp.bfloat16)
+        for cp in stores(c):
+            cp.start()
+        return 0
+
     def late():
+        lax.fori_loop(0, FF // WIDE, weight_grads, 0)
         dwo = inner_rows(mixed_ref[...], d_attn).reshape(UNITS, UNIT, D)
         dwo_ref[...] = dwo.astype(jnp.bfloat16)
         store_out.start()
@@ -1163,6 +1170,7 @@
             pltpu.VMEM((n + 8, 128), jnp.int32),
             pltpu.VMEM((n, 8, 128), jnp.int32),
             pltpu.VMEM((1, max(VECTORS) + 384), full),
+            pltpu.VMEM((TOK_SEQ, FF), low),
             *exchange_sems(n, 3),
             *exchange_sems(n),
             *exchange_sems(n),
@@ -1188,6 +1196,10 @@
     (2, D // 2, D, ("y", "x")),
 )
 QKV_UNITS = 3 * UNITS
+
+
+FFN_WITH = ((1,), (2,), (3,), (4,))
+FFN_AFTER = ((5, 5.5, 6, 6.5, 7, 7.5, 8, 8.5), (9.5, 10.5, 11.5, 12.5))
 
 
 def send_one(sems, src, dst, head, to):
@@ -1307,10 +1319,11 @@
         for cp in loads:
             cp.wait()
 
-    def ffn_run(low, high, whole_only=False):
-        for w, f in ffn_steps:
-            if low <= w < high and not (whole_only and w % 1 >= 0.5):
-                f()
+    def ffn_run(*wanted):
+        for at in wanted:
+            for w, f in ffn_steps:
+                if abs(w - at) < 0.1:
+                    f()
 
     left = low_lanes((BLOCK, 128))
     both = range(BPD // 2)
@@ -1368,8 +1381,7 @@
         def _():
             lax.fori_loop(g * (n // groups), (g + 1) * (n // groups), attend_some, 0)
 
-        if g < 2:
-            ffn_run(4 * g + 1, 4 * g + 5, True)
+        ffn_run(*FFN_WITH[g])
 
     @pl.when(mine)
     def _():
@@ -1396,9 +1408,7 @@
         for cp in copies:
             cp.wait()
 
-    for w, f in ffn_steps:
-        if w < 9 and w % 1 >= 0.5:
-            f()
+    ffn_run(*FFN_AFTER[0])
 
     def head_pair(k, _):
         p = (place_row + k) % (H // 2)
@@ -1455,7 +1465,7 @@
                 vec_out[...] = total
 
     qkv_run(1, 5)
-    ffn_run(9, 20)
+    ffn_run(*FFN_AFTER[1])
     vector_stage(0)
     qkv_run(5, 9)
     load_w.wait()
@@ -1464,7 +1474,7 @@
         d_tokens = d_tokens + outer_cols(proj[e], as_matrix(w_ref[e * UNITS : (e + 1) * UNITS]))
     d_tokens_ref[...] = d_tokens
     vector_stage(1)
-    ffn_run(20, 99)
+    ffn_run(20)
     vector_stage(2)
     qkv_run(9, 20)
     vector_stage(3)

time: 244 us -> 240 us (0.984)
  the two profiles are of different devices: /device:TPU:8 before, /device:TPU:2 now
where the time goes in v8:
time: 240 us
  Pallas kernels  236 us (98%)
    pallas_call x1, Pallas kernels, front(): pl.pallas_call(functools.partial(front_kernel, n, nz), out_shape=[jax.Sha...  127 us
    pallas_call x1, Pallas kernels, back(): pl.pallas_call(functools.partial(back_kernel, n, nz), out_shape=[jax.Shap...  106 us

profile of v8, /device:TPU:2, one launch (start us, length us, event | category | flops | bytes accessed | tf_op | source)
XLA Modules:
  0.0 239.8 jit_solution(13494311712785878876)
XLA Ops:
  0.6 0.8 fusion.5
  1.4 0.6 reshape.82.refs_3_
  2.0 0.7 copy.20
  2.7 0.1 copy.21
  2.8 0.6 pad.9.refs_2_
  3.4 126.6 %front.1 = (f32[256,768]{1,0:T(8,128)}, f32[256,768]{1,0:T(8,128)}, bf16[64,64,128]{2,1,0:T(8,128)(2,1)}, bf16[16,128,128]{2,1,0:T(8,128)(2,1)}, s32[16,8,128]{2...) custom-call(bf16[256,768]{1,0:T(8,128)(2,1)} %bitcast.16, ...), custom_call_target="tpu_custom_call" | custom-call | tf_op jit(solution)/shard_map/front/pallas_call | solution.py:1138
  130.0 105.6 %back.1 = (f32[256,768]{1,0:T(8,128)}, f32[16,768]{1,0:T(8,128)}, f32[432,128]{1,0:T(8,128)}, f32[144,128]{1,0:T(8,128)}, f32[576,128]{1,0:T(8,128)}, /*index=5*/f32[576,128]{1,0:T(8,128)}) custom-call(bf16[64,64,128]{2,1,0:T(8,128)(2,1)} %get-tuple-element.39.refs_0_, bf16[16,128,128]{2,1,0:T(8,128)(2,1)} %get-tuple-element.40.refs_1_, ...), custom_call_target="tpu_custom_call" | custom-call | tf_op jit(solution)/shard_map/back/pallas_call | solution.py:1515
  235.7 4.0 %hand_out.1 = (f32[256,768]{1,0:T(8,128)}, f32[256,768]{1,0:T(8,128)}, f32[432,128]{1,0:T(8,128)}, f32[144,128]{1,0:T(8,128)}, f32[576,128]{1,0:T(8,128)}, /*ind...) custom-call(f32[256,768]{1,0:T(8,128)} %get-tuple-element.38.refs_0_, ...), custom_call_target="tpu_custom_call" | custom-call | tf_op jit(solution)/shard_map/hand_out/pallas_call | solution.py:1582

commit v9 on v8

--- a/solution.py
+++ b/solution.py
@@ -681,14 +681,14 @@
 THIRD = FF // UNITS // 3
 QKV_ORDERS = (("z", "x", "y"), ("z", "y", "x"), ("x", "y", "z"))
 REST = (
+    ("first", 0, UNIT, ("z", "x", "y")),
     ("second", THIRD, FF // UNITS, ("z", "y", "x")),
-    ("first", 0, UNIT, ("z", "x", "y")),
     ("second", 0, THIRD, ("z", "x", "y")),
 )
 
 
 EARLY = {1: (0, 1), 4: (1, 2), 5: (2, 3)}
-LATE = ((3, 4), (4, 5), (5, 99), (99, 99), (99, 99))
+LATE = ((3, 4), (4, 5), (99, 99), (99, 99), (99, 99))
 
 
 def from_flat(flat, cols, rows):
@@ -867,9 +867,9 @@
             cp.wait()
         vec = vec_in
 
-    def rest_steps(low, high):
+    def rest_steps(low, high, part=slice(None)):
         if nz:
-            run_in_order(rest_items, low, high)
+            run_in_order(rest_items[part], low, high)
 
     rows = rows_ref[...]
     left = low_lanes((TOK_SEQ, 128))
@@ -987,9 +987,9 @@
         cp.start()
         cp.wait()
 
+    rest_steps(5, 99, slice(0, 1))
     if nz:
-        for item in rest_items:
-            item.finish()
+        rest_items[0].finish()
     wait_from_owners(n, place_row, head, attended, inbox, sems_in)
 
     for h in range(0, H, 2):
@@ -1008,7 +1008,7 @@
     def second_rows(c):
         return second_ref[pl.ds(c * per, per)].reshape(WIDE, D)
 
-    def up_step(c, hidden):
+    def up_step(c, _):
         cols = pl.ds(pl.multiple_of(c * WIDE, WIDE), WIDE)
         up = matmul(lowered, as_matrix(first_ref[:, :, cols])) + vec[pl.ds(8 + c, 1)]
         square = up * up
@@ -1019,9 +1019,18 @@
             (2 / jnp.pi) ** 0.5 * (1 + 3 * 0.044715 * square)
         )
         active_ref[:, cols] = active
-        return hidden + matmul(active, second_rows(c))
-
-    hidden2 = lax.fori_loop(0, FF // WIDE, up_step, normed_out1 + vec[4:5])
+        return 0
+
+    def down_step(c, hidden):
+        cols = pl.ds(pl.multiple_of(c * WIDE, WIDE), WIDE)
+        return hidden + matmul(active_ref[:, cols], second_rows(c))
+
+    rest_steps(5, 99, slice(1, 3))
+    lax.fori_loop(0, FF // WIDE, up_step, 0)
+    if nz:
+        for item in rest_items[1:]:
+            item.finish()
+    hidden2 = lax.fori_loop(0, FF // WIDE, down_step, normed_out1 + vec[4:5])
     result, normed2, inverse2 = normalize(hidden2, vec[7:8], vec[5:6])
     result_ref[...] = result
     grad = cot_ref[...].astype(jnp.float32)
@@ -1185,8 +1194,7 @@
 
 FFN_KINDS = (
     ("expand", 0, UNIT, ("x", "y")),
-    ("contract", THIRD, FF // UNITS, ("y", "x")),
-    ("contract", 0, THIRD, ("x", "y")),
+    ("contract", 0, FF // UNITS, ("y", "x")),
     ("out", 0, UNIT, ("x", "y")),
 )
 QKV_KINDS = (
@@ -1464,15 +1472,15 @@
             else:
                 vec_out[...] = total
 
-    qkv_run(1, 5)
-    ffn_run(*FFN_AFTER[1])
-    vector_stage(0)
-    qkv_run(5, 9)
     load_w.wait()
     d_tokens = d_sum1_ref[...]
     for e in range(3):
         d_tokens = d_tokens + outer_cols(proj[e], as_matrix(w_ref[e * UNITS : (e + 1) * UNITS]))
     d_tokens_ref[...] = d_tokens
+    qkv_run(1, 5)
+    ffn_run(*FFN_AFTER[1])
+    vector_stage(0)
+    qkv_run(5, 9)
     vector_stage(1)
     ffn_run(20)
     vector_stage(2)

time: 240 us -> 237 us (0.988)
  the two profiles are of different devices: /device:TPU:2 before, /device:TPU:8 now
where the time goes in v9:
time: 237 us; the launch traced here: 233 us
  Pallas kernels  230 us (97%)
    pallas_call x1, Pallas kernels, front(): pl.pallas_call(functools.partial(front_kernel, n, nz), out_shape=[jax.Sha...  124 us
    pallas_call x1, Pallas kernels, back(): pl.pallas_call(functools.partial(back_kernel, n, nz), out_shape=[jax.Shap...  102 us

profile of v9, /device:TPU:8, one launch (start us, length us, event | category | flops | bytes accessed | tf_op | source)
XLA Modules:
  0.0 233.4 jit_solution(14874829884323283188)
XLA Ops:
  0.6 0.8 fusion.5
  1.4 0.6 reshape.82.refs_3_
  2.0 0.7 copy.20
  2.7 0.1 copy.21
  2.8 0.6 pad.9.refs_2_
  3.4 124.0 %front.1 = (f32[256,768]{1,0:T(8,128)}, f32[256,768]{1,0:T(8,128)}, bf16[64,64,128]{2,1,0:T(8,128)(2,1)}, bf16[16,128,128]{2,1,0:T(8,128)(2,1)}, s32[16,8,128]{2...) custom-call(bf16[256,768]{1,0:T(8,128)(2,1)} %bitcast.16, ...), custom_call_target="tpu_custom_call" | custom-call | tf_op jit(solution)/shard_map/front/pallas_call | solution.py:1147
  127.4 101.8 %back.1 = (f32[256,768]{1,0:T(8,128)}, f32[16,768]{1,0:T(8,128)}, f32[432,128]{1,0:T(8,128)}, f32[144,128]{1,0:T(8,128)}, f32[576,128]{1,0:T(8,128)}, /*index=5*/f32[576,128]{1,0:T(8,128)}) custom-call(bf16[64,64,128]{2,1,0:T(8,128)(2,1)} %get-tuple-element.39.refs_0_, bf16[16,128,128]{2,1,0:T(8,128)(2,1)} %get-tuple-element.40.refs_1_, ...), custom_call_target="tpu_custom_call" | custom-call | tf_op jit(solution)/shard_map/back/pallas_call | solution.py:1523
  229.2 4.0 %hand_out.1 = (f32[256,768]{1,0:T(8,128)}, f32[256,768]{1,0:T(8,128)}, f32[432,128]{1,0:T(8,128)}, f32[144,128]{1,0:T(8,128)}, f32[576,128]{1,0:T(8,128)}, /*ind...) custom-call(f32[256,768]{1,0:T(8,128)} %get-tuple-element.38.refs_0_, ...), custom_call_target="tpu_custom_call" | custom-call | tf_op jit(solution)/shard_map/hand_out/pallas_call | solution.py:1590

commit v10 on v9

--- a/solution.py
+++ b/solution.py
@@ -1206,7 +1206,7 @@
 QKV_UNITS = 3 * UNITS
 
 
-FFN_WITH = ((1,), (2,), (3,), (4,))
+FFN_WITH = ((1,), (2,), (3,), (4,), (), (), (), ())
 FFN_AFTER = ((5, 5.5, 6, 6.5, 7, 7.5, 8, 8.5), (9.5, 10.5, 11.5, 12.5))
 
 
@@ -1382,7 +1382,7 @@
                     acc[blocks + k * PICKS + e] = tiles[5 + j][u] + acc[blocks + links_ref[s, e]]
         return 0
 
-    groups = 4
+    groups = 8
     for g in range(groups):
 
         @pl.when(mine)

time: 237 us -> 237 us (level)
  no operation moved by 1% of the time
where the time goes in v10:
time: 237 us; the launch traced here: 234 us
  Pallas kernels  230 us (97%)
    pallas_call x1, Pallas kernels, front(): pl.pallas_call(functools.partial(front_kernel, n, nz), out_shape=[jax.Sha...  124 us
    pallas_call x1, Pallas kernels, back(): pl.pallas_call(functools.partial(back_kernel, n, nz), out_shape=[jax.Shap...  102 us

profile of v10, /device:TPU:8, one launch (start us, length us, event | category | flops | bytes accessed | tf_op | source)
XLA Modules:
  0.0 233.8 jit_solution(172999740963235422)
XLA Ops:
  0.6 0.8 fusion.5
  1.4 0.6 reshape.82.refs_3_
  2.0 0.7 copy.20
  2.7 0.1 copy.21
  2.8 0.6 pad.9.refs_2_
  3.4 124.0 %front.1 = (f32[256,768]{1,0:T(8,128)}, f32[256,768]{1,0:T(8,128)}, bf16[64,64,128]{2,1,0:T(8,128)(2,1)}, bf16[16,128,128]{2,1,0:T(8,128)(2,1)}, s32[16,8,128]{2...) custom-call(bf16[256,768]{1,0:T(8,128)(2,1)} %bitcast.16, ...), custom_call_target="tpu_custom_call" | custom-call | tf_op jit(solution)/shard_map/front/pallas_call | solution.py:1147
  127.4 102.2 %back.1 = (f32[256,768]{1,0:T(8,128)}, f32[16,768]{1,0:T(8,128)}, f32[432,128]{1,0:T(8,128)}, f32[144,128]{1,0:T(8,128)}, f32[576,128]{1,0:T(8,128)}, /*index=5*/f32[576,128]{1,0:T(8,128)}) custom-call(bf16[64,64,128]{2,1,0:T(8,128)(2,1)} %get-tuple-element.39.refs_0_, bf16[16,128,128]{2,1,0:T(8,128)(2,1)} %get-tuple-element.40.refs_1_, ...), custom_call_target="tpu_custom_call" | custom-call | tf_op jit(solution)/shard_map/back/pallas_call | solution.py:1523
  229.6 4.0 %hand_out.1 = (f32[256,768]{1,0:T(8,128)}, f32[256,768]{1,0:T(8,128)}, f32[432,128]{1,0:T(8,128)}, f32[144,128]{1,0:T(8,128)}, f32[576,128]{1,0:T(8,128)}, /*ind...) custom-call(f32[256,768]{1,0:T(8,128)} %get-tuple-element.38.refs_0_, ...), custom_call_target="tpu_custom_call" | custom-call | tf_op jit(solution)/shard_map/hand_out/pallas_call | solution.py:1590
